TPU v7x, 32 devices: a whole 2x2x4 slice. The times are simulated.
32 devices in a mesh: dp: 8 (over y, x, core), head: 4 (over z).
Axes of the slice: x: 2, y: 2, z: 4, core: 2. Of those that a mesh axis runs over, the one named last changes fastest.
Arguments:
- series: bfloat16 [32768, 512], P(('dp', 'head')), may hold values from -6 to 6
- target: float32 [32768, 512], P(('dp', 'head')), may hold values from -6 to 6
- valid: int32 [32768], P(('dp', 'head')), may hold values from 0 to 1
- window_id: int32 [256, 128], P(('dp', 'head')), may hold values from 0 to 3, never falling along the last dimension, each value on 1 to 48 neighbouring positions
- mode_index: int32 [8, 64], P('head'), may hold values from 0 to 64, as said below
- query_weight: float32 [512, 512], P(None, 'head'), may hold values from -0.25 to 0.25
- query_first: float32 [512, 512], P(None, 'head'), may hold values from -4.7683716e-06 to 4.7683716e-06
- query_second: float32 [512, 512], P(None, 'head'), may hold values from 5.867866e-14 to 2.3471465e-13
- out_weight: float32 [512, 512], P('head'), may hold values from -0.25 to 0.25
- out_first: float32 [512, 512], P('head'), may hold values from -4.7683716e-06 to 4.7683716e-06
- out_second: float32 [512, 512], P('head'), may hold values from 5.867866e-14 to 2.3471465e-13
- mode_weight: float32 [2, 8, 64, 4096], P(None, 'head'), may hold values from -0.36 to 0.36
- mode_first: float32 [2, 8, 64, 4096], P(None, 'head'), may hold values from -4.7683716e-06 to 4.7683716e-06
- mode_second: float32 [2, 8, 64, 4096], P(None, 'head'), may hold values from 5.867866e-14 to 2.3471465e-13
- up_weight: float32 [512, 2048], P(None, 'head'), may hold values from -0.25 to 0.25
- up_first: float32 [512, 2048], P(None, 'head'), may hold values from -4.7683716e-06 to 4.7683716e-06
- up_second: float32 [512, 2048], P(None, 'head'), may hold values from 5.867866e-14 to 2.3471465e-13
- down_weight: float32 [2048, 512], P('head'), may hold values from -0.125 to 0.125
- down_first: float32 [2048, 512], P('head'), may hold values from -4.7683716e-06 to 4.7683716e-06
- down_second: float32 [2048, 512], P('head'), may hold values from 5.867866e-14 to 2.3471465e-13
- bias_pair: float32 [2, 512], replicated, may hold values from -3 to 3
- bias_first: float32 [2, 512], replicated, may hold values from -4.7683716e-06 to 4.7683716e-06
- bias_second: float32 [2, 512], replicated, may hold values from 5.867866e-14 to 2.3471465e-13
- decomp_params: float32 [2, 2, 5], replicated, may hold values from -3 to 3
- decomp_first: float32 [2, 2, 5], replicated, may hold values from -4.7683716e-06 to 4.7683716e-06
- decomp_second: float32 [2, 2, 5], replicated, may hold values from 5.867866e-14 to 2.3471465e-13
Outputs:
- loss_sum: float32 [], replicated
- valid_count: float32 [], replicated
- grad_norm: float32 [], replicated
- query_weight_new: float32 [512, 512], P(None, 'head')
- query_first_new: float32 [512, 512], P(None, 'head')
- query_second_new: float32 [512, 512], P(None, 'head')
- out_weight_new: float32 [512, 512], P('head')
- out_first_new: float32 [512, 512], P('head')
- out_second_new: float32 [512, 512], P('head')
- mode_weight_new: float32 [2, 8, 64, 4096], P(None, 'head')
- mode_first_new: float32 [2, 8, 64, 4096], P(None, 'head')
- mode_second_new: float32 [2, 8, 64, 4096], P(None, 'head')
- up_weight_new: float32 [512, 2048], P(None, 'head')
- up_first_new: float32 [512, 2048], P(None, 'head')
- up_second_new: float32 [512, 2048], P(None, 'head')
- down_weight_new: float32 [2048, 512], P('head')
- down_first_new: float32 [2048, 512], P('head')
- down_second_new: float32 [2048, 512], P('head')
- bias_pair_new: float32 [2, 512], replicated
- bias_first_new: float32 [2, 512], replicated
- bias_second_new: float32 [2, 512], replicated
- decomp_params_new: float32 [2, 2, 5], replicated
- decomp_first_new: float32 [2, 2, 5], replicated
- decomp_second_new: float32 [2, 2, 5], replicated
Inputs may be any that keep to these rules, and one draw needn't show every extreme that they name: `mode_index`: each head's list names 64 different frequencies. `window_id`: along a context the window numbers never fall; every window holds 1 to 48 steps.
All inputs are finite; a program needn't handle non-finite values.
Results may differ from a plain program's by a relative error of at most 0.0022.
Values may be sent and summed in bfloat16 or wider, within the bound.
No kernel may reach another device: no remote copies, remote signals or barrier semaphores. Data moves between devices by JAX's collectives and lax.ppermute only.
A program may use at most 256 MiB of HBM per device.

v0:
```python
from functools import partial
import math

import jax
import jax.numpy as jnp
from jax import lax
from jax.sharding import PartitionSpec as P

MODES = 64
SEQ_LEN = 128
MICRO = 2
STEP = 10


HIGHEST_PRECISION = lax.Precision.HIGHEST
KERNEL_WIDTHS = (7, 12, 14, 24, 48)
BETA_ONE = 0.9
BETA_TWO = 0.999
LEARN_RATE = 0.05
EPSILON = 1e-08
DECAY = 0.01
CLIP_NORM = 0.02


def window_averages(window_rows):
    length = window_rows.shape[1]
    earlier = (window_rows[:, None, :] < window_rows[:, :, None]).astype(jnp.int32)
    first = jnp.sum(earlier, axis=2)[:, :, None]
    upto = (window_rows[:, None, :] <= window_rows[:, :, None]).astype(jnp.int32)
    last = (jnp.sum(upto, axis=2) - 1)[:, :, None]
    row_steps = jnp.arange(length, dtype=jnp.int32)[None, :, None]
    columns = jnp.arange(length, dtype=jnp.int32)[None, None, :]
    matrices = []
    for kernel_width in KERNEL_WIDTHS:
        lead_pad = kernel_width - 1 - (kernel_width - 1) // 2
        matrix = jnp.zeros((window_rows.shape[0], length, length), jnp.float32)
        for offset in range(kernel_width):
            position = jnp.minimum(jnp.maximum(row_steps - lead_pad + offset, first), last)
            matrix = matrix + (position == columns).astype(jnp.float32)
        matrices.append(matrix / kernel_width)
    return jnp.stack(matrices, axis=1)


def forward_tables(mode_index, length):
    steps_t = jnp.arange(length, dtype=jnp.int32)
    phase_index = mode_index[:, :, None] * steps_t[None, None, :] % length
    angles = phase_index.astype(jnp.float32) * (2.0 * math.pi / length)
    return (jnp.cos(angles), jnp.sin(angles))


def inverse_tables(count_modes, length):
    steps_t = jnp.arange(length, dtype=jnp.int32)[:, None]
    orders = jnp.arange(count_modes, dtype=jnp.int32)[None, :]
    angles = (steps_t * orders % length).astype(jnp.float32) * (2.0 * math.pi / length)
    weights = jnp.where(orders == 0, 1.0, 2.0).astype(jnp.float32) / length
    return (jnp.cos(angles) * weights, jnp.sin(angles) * weights)


def spectral(queries, mode_weights, cos_fwd, sin_fwd, cos_inv, sin_inv):
    heads = cos_fwd.shape[0]
    count_modes = cos_fwd.shape[1]
    length = cos_fwd.shape[2]
    contexts = queries.shape[0] // length
    shaped = queries.reshape(contexts, length, heads, -1)
    width = shaped.shape[3]
    merged = mode_weights.reshape(2, heads, width, -1, count_modes)
    real_in = jnp.einsum("hmt,bthe->bhme", cos_fwd, shaped, precision=HIGHEST_PRECISION)
    imag_in = -jnp.einsum("hmt,bthe->bhme", sin_fwd, shaped, precision=HIGHEST_PRECISION)
    w_real = merged[0]
    w_imag = merged[1]
    real_out = jnp.einsum(
        "bhme,heom->bhmo", real_in, w_real, precision=HIGHEST_PRECISION
    ) - jnp.einsum("bhme,heom->bhmo", imag_in, w_imag, precision=HIGHEST_PRECISION)
    imag_out = jnp.einsum(
        "bhme,heom->bhmo", real_in, w_imag, precision=HIGHEST_PRECISION
    ) + jnp.einsum("bhme,heom->bhmo", imag_in, w_real, precision=HIGHEST_PRECISION)
    result = jnp.einsum(
        "tm,bhmo->btho", cos_inv, real_out, precision=HIGHEST_PRECISION
    ) - jnp.einsum("tm,bhmo->btho", sin_inv, imag_out, precision=HIGHEST_PRECISION)
    return result.reshape(queries.shape[0], -1)


def decompose(values, decomp_row, averages):
    length = averages.shape[2]
    contexts = values.shape[0] // length
    shaped = values.reshape(contexts, length, values.shape[1])
    averaged = jnp.einsum("bkts,bsf->kbtf", averages, shaped, precision=HIGHEST_PRECISION)
    logits = shaped[None] * decomp_row[0][:, None, None, None] + decomp_row[1][:, None, None, None]
    shares = jax.nn.softmax(logits, axis=0)
    trend_part = jnp.sum(shares * averaged, axis=0).reshape(values.shape)
    return (values - trend_part, trend_part)


def plain_dot(left, right):
    return jnp.dot(left, right, preferred_element_type=jnp.float32)


def inner_dot(left, right):
    return lax.dot_general(
        left, right, (((0,), (0,)), ((), ())), preferred_element_type=jnp.float32
    )


def back_dot(left, right):
    return lax.dot_general(
        left, right, (((1,), (1,)), ((), ())), preferred_element_type=jnp.float32
    )


def one_micro(
    series_rows,
    target_rows,
    valid_rows,
    window_rows,
    low_weights,
    mode_weight,
    bias_pair,
    decomp_params,
    tables,
):
    query_low, out_low, up_low, down_low = low_weights
    averages = window_averages(window_rows)
    columns = query_low.shape[1]
    column_start = lax.axis_index("head") * columns
    query_bias = lax.dynamic_slice_in_dim(bias_pair[0], column_start, columns, 0)
    inputs = series_rows.astype(jnp.float32)
    whole = lax.all_gather(series_rows, "head", axis=0, tiled=True)
    queries = plain_dot(whole, query_low) + query_bias
    spectrum = spectral(queries, mode_weight, *tables).astype(jnp.bfloat16)
    attention = (
        lax.psum_scatter(plain_dot(spectrum, out_low), "head", scatter_dimension=0, tiled=True)
        + bias_pair[1]
    )
    pre_one = inputs + attention
    season_one, trend_one = decompose(pre_one, decomp_params[0], averages)
    season_low = season_one.astype(jnp.bfloat16)
    feed_in = lax.all_gather(season_low, "head", axis=0, tiled=True)
    hidden = plain_dot(feed_in, up_low)
    active = jax.nn.gelu(hidden, approximate=False).astype(jnp.bfloat16)
    feed_out = lax.psum_scatter(
        plain_dot(active, down_low), "head", scatter_dimension=0, tiled=True
    )
    pre_two = season_one + feed_out
    trend_two, pull_two = jax.vjp(
        lambda values, params: decompose(values, params, averages)[1], pre_two, decomp_params[1]
    )
    misfit = trend_one + trend_two - target_rows
    row_weight = valid_rows[:, None]
    loss_part = jnp.sum(row_weight * misfit * misfit)
    d_trend = 2.0 * row_weight * misfit
    d_pre_two, d_decomp_two = pull_two(d_trend)
    d_feed = d_pre_two.astype(jnp.bfloat16)
    d_feed_rows = lax.all_gather(d_feed, "head", axis=0, tiled=True)
    up_use, down_use = (up_low, down_low)
    d_active = back_dot(d_feed_rows, down_use)
    gelu_pull = jax.vjp(partial(jax.nn.gelu, approximate=False), hidden)[1]
    d_hidden = gelu_pull(d_active)[0].astype(jnp.bfloat16)
    d_down = inner_dot(active, d_feed_rows)
    d_up = inner_dot(feed_in, d_hidden)
    d_back = back_dot(d_hidden, up_use)
    d_season = d_pre_two + lax.psum_scatter(
        d_back.astype(jnp.bfloat16), "head", scatter_dimension=0, tiled=True
    ).astype(jnp.float32)
    pull_one = jax.vjp(
        lambda values, params: decompose(values, params, averages), pre_one, decomp_params[0]
    )[1]
    d_pre_one, d_decomp_one = pull_one((d_season, d_trend))
    d_attn = d_pre_one.astype(jnp.bfloat16)
    d_attn_whole = lax.all_gather(d_attn, "head", axis=0, tiled=True)
    d_out = inner_dot(spectrum, d_attn_whole)
    d_spectrum = back_dot(d_attn_whole, out_low)
    spec_pull = jax.vjp(
        lambda values, params: spectral(values, params, *tables), queries, mode_weight
    )[1]
    d_queries, d_modes = spec_pull(d_spectrum)
    d_queries = d_queries.astype(jnp.bfloat16)
    d_query = inner_dot(whole, d_queries)
    query_bias_grad = jnp.sum(d_queries.astype(jnp.float32), axis=0)
    bias_row_one = lax.dynamic_update_slice_in_dim(
        jnp.zeros(bias_pair.shape[1:], jnp.float32), query_bias_grad, column_start, 0
    )
    d_bias = jnp.stack([bias_row_one, jnp.sum(d_pre_one, axis=0)])
    d_decomp = jnp.stack([d_decomp_one, d_decomp_two])
    return ((d_query, d_out, d_modes, d_up, d_down), d_bias, d_decomp, loss_part)


def adam_step(weight, gradient, moment_one, second):
    moment_one = BETA_ONE * moment_one + (1.0 - BETA_ONE) * gradient
    second = BETA_TWO * second + (1.0 - BETA_TWO) * gradient * gradient
    first_hat = moment_one / (1.0 - BETA_ONE**STEP)
    second_hat = second / (1.0 - BETA_TWO**STEP)
    weight = weight - LEARN_RATE * (first_hat / (jnp.sqrt(second_hat) + EPSILON) + DECAY * weight)
    return (weight, moment_one, second)


def on_device(
    series,
    target,
    valid,
    window_id,
    mode_index,
    query_weight,
    query_first,
    query_second,
    out_weight,
    out_first,
    out_second,
    mode_weight,
    mode_first,
    mode_second,
    up_weight,
    up_first,
    up_second,
    down_weight,
    down_first,
    down_second,
    bias_pair,
    bias_first,
    bias_second,
    decomp_params,
    decomp_first,
    decomp_second,
):
    tables = forward_tables(mode_index, SEQ_LEN) + inverse_tables(MODES, SEQ_LEN)
    low_weights = (
        query_weight.astype(jnp.bfloat16),
        out_weight.astype(jnp.bfloat16),
        up_weight.astype(jnp.bfloat16),
        down_weight.astype(jnp.bfloat16),
    )
    valid_float = valid.astype(jnp.float32)
    rows_micro = series.shape[0] // MICRO
    ctx_micro = window_id.shape[0] // MICRO
    summed = None
    bias_total = jnp.zeros(bias_pair.shape, jnp.float32)
    decomp_total = jnp.zeros(decomp_params.shape, jnp.float32)
    loss_total = jnp.zeros((), jnp.float32)
    for micro_index in range(MICRO):
        start = micro_index * rows_micro
        ctx_start = micro_index * ctx_micro
        gradients, d_bias, d_decomp, loss_part = one_micro(
            series[start : start + rows_micro],
            target[start : start + rows_micro],
            valid_float[start : start + rows_micro],
            window_id[ctx_start : ctx_start + ctx_micro],
            low_weights,
            mode_weight,
            bias_pair,
            decomp_params,
            tables,
        )
        gradients = lax.psum(
            (gradients[0], gradients[1], gradients[2], gradients[3], gradients[4]), "dp"
        )
        summed = gradients if summed is None else jax.tree.map(jnp.add, summed, gradients)
        bias_total = bias_total + d_bias
        decomp_total = decomp_total + d_decomp
        loss_total = loss_total + loss_part
    bias_total, decomp_total, loss_sum, valid_count = lax.psum(
        (bias_total, decomp_total, loss_total, jnp.sum(valid_float)), ("dp", "head")
    )
    gradients = tuple((gradient / valid_count for gradient in summed))
    bias_grad = bias_total / valid_count
    decomp_grad = decomp_total / valid_count
    local_squares = sum((jnp.sum(gradient * gradient) for gradient in gradients))
    grad_norm = jnp.sqrt(
        lax.psum(local_squares, "head")
        + jnp.sum(bias_grad * bias_grad)
        + jnp.sum(decomp_grad * decomp_grad)
    )
    factor = jnp.minimum(1.0, CLIP_NORM / (grad_norm + 1e-06))
    weights = (
        query_weight,
        out_weight,
        mode_weight,
        up_weight,
        down_weight,
        bias_pair,
        decomp_params,
    )
    firsts = (query_first, out_first, mode_first, up_first, down_first, bias_first, decomp_first)
    seconds = (
        query_second,
        out_second,
        mode_second,
        up_second,
        down_second,
        bias_second,
        decomp_second,
    )
    all_grads = gradients + (bias_grad, decomp_grad)
    news = [
        adam_step(weights[index], all_grads[index] * factor, firsts[index], seconds[index])
        for index in range(7)
    ]
    return (
        loss_sum,
        valid_count,
        grad_norm,
        news[0][0],
        news[0][1],
        news[0][2],
        news[1][0],
        news[1][1],
        news[1][2],
        news[2][0],
        news[2][1],
        news[2][2],
        news[3][0],
        news[3][1],
        news[3][2],
        news[4][0],
        news[4][1],
        news[4][2],
        news[5][0],
        news[5][1],
        news[5][2],
        news[6][0],
        news[6][1],
        news[6][2],
    )


def solution(mesh):
    in_specs = (
        P(("dp", "head"), None),
        P(("dp", "head"), None),
        P(("dp", "head")),
        P(("dp", "head"), None),
        P("head", None),
        P(None, "head"),
        P(None, "head"),
        P(None, "head"),
        P("head", None),
        P("head", None),
        P("head", None),
        P(None, "head", None, None),
        P(None, "head", None, None),
        P(None, "head", None, None),
        P(None, "head"),
        P(None, "head"),
        P(None, "head"),
        P("head", None),
        P("head", None),
        P("head", None),
        P(),
        P(),
        P(),
        P(),
        P(),
        P(),
    )
    out_specs = (
        P(),
        P(),
        P(),
        P(None, "head"),
        P(None, "head"),
        P(None, "head"),
        P("head", None),
        P("head", None),
        P("head", None),
        P(None, "head", None, None),
        P(None, "head", None, None),
        P(None, "head", None, None),
        P(None, "head"),
        P(None, "head"),
        P(None, "head"),
        P("head", None),
        P("head", None),
        P("head", None),
        P(),
        P(),
        P(),
        P(),
        P(),
        P(),
    )
    return jax.shard_map(
        on_device, mesh=mesh, in_specs=in_specs, out_specs=out_specs, check_vma=False
    )
```

profile of v0, /device:TPU:0, one launch (start us, length us, event | category | flops | bytes accessed | tf_op | source)
XLA Modules:
  0.0 1386.5 jit_solution(455496082336150011)
XLA Ops:
  33.6 25.3 %all-gather.13.cloned.1.call-done = bf16[2048,512]{1,0:T(8,128)(2,1)} async-done(((bf16[512,512]{1,0:T(8,128)(2,1)}), bf16[2048,512]{1,0:T(8,128)(2,1)}) %all-gather.13.cloned.1.call-update) | async-done | bytes 2097168 | tf_op jit(solution)/shard_map/all_gather | solution.py:127
  93.0 12.6 all-gather.9.cloned.1.call-done
  153.5 30.0 %reduce-scatter.11.cloned.1.call-done = f32[512,512]{1,0:T(8,128)} async-done(((f32[2048,512]{1,0:T(8,128)}), f32[512,512]{1,0:T(8,128)}) %reduce-scatter.11.cloned.1.call-update) | async-done | bytes 1048592 | tf_op jit(solution)/shard_map/reduce_scatter | solution.py:131
  183.5 80.2 %reduce-scatter.7.cloned.1.call-done = f32[512,512]{1,0:T(8,128)} async-done(((f32[2048,512]{1,0:T(8,128)}), f32[512,512]{1,0:T(8,128)}) %reduce-scatter.7.cloned.1.call-update) | async-done | bytes 1048592 | tf_op jit(solution)/shard_map/reduce_scatter | solution.py:131
  270.8 12.6 fusion.1
  292.4 42.4 %all-gather.15.cloned.1.call-done = bf16[2048,512]{1,0:T(8,128)(2,1)} async-done(((bf16[512,512]{1,0:T(8,128)(2,1)}), bf16[2048,512]{1,0:T(8,128)(2,1)}) %all-gather.15.cloned.1.call-update) | async-done | bytes 2097168 | tf_op jit(solution)/shard_map/all_gather | solution.py:137
  334.7 13.0 multiply_convert_fusion
  353.1 75.0 %reduce-scatter.13.cloned.1.call-done = f32[512,512]{1,0:T(8,128)} async-done(((f32[2048,512]{1,0:T(8,128)}), f32[512,512]{1,0:T(8,128)}) %reduce-scatter.13.cloned.1.call-update) | async-done | bytes 1048592 | tf_op jit(solution)/shard_map/reduce_scatter | solution.py:140
  439.6 11.5 fusion
  478.7 9.6 fusion.104
  490.2 46.6 %all-gather.21.cloned.1.call-done = bf16[2048,512]{1,0:T(8,128)(2,1)} async-done(((bf16[512,512]{1,0:T(8,128)(2,1)}), bf16[2048,512]{1,0:T(8,128)(2,1)}) %all-gather.21.cloned.1.call-update) | async-done | bytes 2097168 | tf_op jit(solution)/shard_map/all_gather | solution.py:153
  558.7 31.5 %reduce-scatter.17.cloned.1.call-done = bf16[512,512]{1,0:T(8,128)(2,1)} async-done(((bf16[2048,512]{1,0:T(8,128)(2,1)}), bf16[512,512]{1,0:T(8,128)(2,1)}) %reduce-scatter.17.cloned.1.call-update) | async-done | bytes 524304 | tf_op jit(solution)/shard_map/reduce_scatter | solution.py:161
  602.9 14.2 %add_multiply_fusion = (f32[5,4,128,512]{2,3,0,1:T(8,128)}, f32[4,128,512]{1,2,0:T(8,128)}, f32[4,512,5,128]{3,1,2,0:T(8,128)}) fusion(f32[4,512,5,128]{3,1,2,0:T(8,128)} %get-tuple-element.339, f32[4,128,512]{1,2,0:T(8,128)S(1)} %neg.105, f32[4,128,512]{1,2,0:T(8,128)S(1)} %copy-done.87, f32[4,128,512]{1,2,0:T(8,128)S(1)} %copy-done.78, ...), kind=kOutput, calls=%fused_computation.28 | convolution fusion | flops 2030043136 | bytes 27525160 | tf_op jit(solution)/shard_map/bkts,bsf->kbtf/dot_general | solution.py:87
  621.9 45.4 %all-gather.11.cloned.1.call-done = bf16[2048,512]{1,0:T(8,128)(2,1)} async-done(((bf16[512,512]{1,0:T(8,128)(2,1)}), bf16[2048,512]{1,0:T(8,128)(2,1)}) %all-gather.11.cloned.1.call-update) | async-done | bytes 2097168 | tf_op jit(solution)/shard_map/all_gather | solution.py:137
  667.3 12.9 multiply_convert_fusion.1
  685.1 75.4 %reduce-scatter.9.cloned.1.call-done = f32[512,512]{1,0:T(8,128)} async-done(((f32[2048,512]{1,0:T(8,128)}), f32[512,512]{1,0:T(8,128)}) %reduce-scatter.9.cloned.1.call-update) | async-done | bytes 1048592 | tf_op jit(solution)/shard_map/reduce_scatter | solution.py:140
  772.2 9.7 fusion.2
  811.1 9.6 fusion.110
  822.6 46.5 %all-gather.17.cloned.1.call-done = bf16[2048,512]{1,0:T(8,128)(2,1)} async-done(((bf16[512,512]{1,0:T(8,128)(2,1)}), bf16[2048,512]{1,0:T(8,128)(2,1)}) %all-gather.17.cloned.1.call-update) | async-done | bytes 2097168 | tf_op jit(solution)/shard_map/all_gather | solution.py:153
  886.5 36.2 %reduce-scatter.15.cloned.1.call-done = bf16[512,512]{1,0:T(8,128)(2,1)} async-done(((bf16[2048,512]{1,0:T(8,128)(2,1)}), bf16[512,512]{1,0:T(8,128)(2,1)}) %reduce-scatter.15.cloned.1.call-update) | async-done | bytes 524304 | tf_op jit(solution)/shard_map/reduce_scatter | solution.py:161
  936.7 9.4 fusion.101
  961.4 9.1 fusion.107
  982.3 10.5 all-gather.23.cloned.1.call-done
  998.1 10.3 fusion.360
  1016.0 23.4 %all-gather.19.cloned.1.call-done = bf16[2048,512]{1,0:T(8,128)(2,1)} async-done(((bf16[512,512]{1,0:T(8,128)(2,1)}), bf16[2048,512]{1,0:T(8,128)(2,1)}) %all-gather.19.cloned.1.call-update) | async-done | bytes 2097168 | tf_op jit(solution)/shard_map/all_gather | solution.py:169
  1044.8 9.4 fusion.358
  1103.3 9.5 fusion.91
  1123.9 9.7 fusion.94
  1183.2 9.0 copy.481
  1212.6 39.5 %all-reduce.12 = (f32[]{:T(128)}, f32[]{:T(128)}, f32[2,512]{1,0:T(2,128)S(1)}, f32[2,2,5]{2,1,0:T(2,128)S(1)}) all-reduce(f32[]{:T(128)S(6)} %add.4592, f32[]{:T(128)} %convert_reduce_fusion.6, f32[2,512]{1,0:T(2,128)S(1)} %maximum_add_fusion, f32[2,2,5]{2,1,0:T(2,128)S(1)} %maximum_add_fusion.1), channel_id=1, replica_groups=mesh['dp'=8,'head'=4] {'dp','head'}, use_global_device_ids=true, to_apply=%region_22.23 | all-reduce | flops 1046 | bytes 8368 | tf_op jit(solution)/shard_map/psum | solution.py:259
  1253.4 66.2 %all-reduce.16.cloned.1.call-done = (f32[512,128]{0,1:T(8,128)}, f32[128,512]{1,0:T(8,128)}, f32[2,2,64,4096]{3,2,1,0:T(8,128)}, f32[512,512]{1,0:T(8,128)}, f32[512,512]{1,0:T(8,128)}) async-done(((f32[512,128]{0,1:T(8,128)}, f32[128,512]{1,0:T(8,128)}, f32[2,2,64,4096]{3,2,1,0:T(8,128)}, f32[512,512]{1,0:T(8,128)}, f32[512,512]{1,0:T(8,128)}), (f32[512,128]{0,1:T(8,128)}, f32[128,512]{1,0:T(8,128)}, ...) | async-done | bytes 6815760 | tf_op jit(solution)/shard_map/psum | solution.py:252
  1336.8 12.4 psum.117
  (530 shorter events, 504.4 us)
Async XLA Ops:
  7.2 51.6 %all-gather.13.cloned.1.call-start = ((), (), s32[]{:S(2)}) async-start(), calls=%async_computation.10 | async-start | bytes 2621440 | tf_op jit(solution)/shard_map/all_gather | solution.py:127
  9.5 96.2 %all-gather.9.cloned.1.call-start = ((), (), s32[]{:S(2)}) async-start(), calls=%async_computation.6 | async-start | bytes 2621440 | tf_op jit(solution)/shard_map/all_gather | solution.py:127
  10.2 173.2 %reduce-scatter.11.cloned.1.call-start = ((), (), s32[]{:S(2)}) async-start(), calls=%async_computation.11 | async-start | bytes 5242880 | tf_op jit(solution)/shard_map/reduce_scatter | solution.py:131
  10.3 123.6 %copy-start.114 = (f32[64]{0:T(128)}, f32[64]{0:T(128)S(1)}, u32[]{:S(2)}) copy-start(f32[64]{0:T(128)S(1)} %fusion.283) | copy-start | bytes 772
  28.1 30.8 %copy-start.91 = (f32[512,128]{1,0:T(8,128)S(1)}, f32[512,128]{1,0:T(8,128)}, u32[]{:S(2)}) copy-start(f32[512,128]{1,0:T(8,128)} %param.31) | copy-start | bytes 786436
  33.5 102.8 %copy-start.89 = (bf16[128,512]{1,0:T(8,128)(2,1)}, bf16[128,512]{1,0:T(8,128)(2,1)S(1)}, u32[]{:S(2)}) copy-start(bf16[128,512]{1,0:T(8,128)(2,1)S(1)} %convert_element_type.1797) | copy-start | bytes 393220
  33.6 29.7 %copy-start.109 = (s32[2,64]{1,0:T(2,128)S(1)}, s32[2,64]{1,0:T(2,128)}, u32[]{:S(2)}) copy-start(s32[2,64]{1,0:T(2,128)} %param.30) | copy-start | bytes 1540
  65.1 13.9 %copy-start.11 = (f32[16,2,64,64]{3,0,2,1:T(8,128)}, f32[16,2,64,64]{3,0,2,1:T(8,128)S(1)}, u32[]{:S(2)}) copy-start(f32[16,2,64,64]{3,0,2,1:T(8,128)S(1)} %copy.399) | copy-start | bytes 1572868
  66.9 16.0 %copy-start.7 = (f32[16,2,64,64]{3,0,2,1:T(8,128)}, f32[16,2,64,64]{3,0,2,1:T(8,128)S(1)}, u32[]{:S(2)}) copy-start(f32[16,2,64,64]{3,0,2,1:T(8,128)S(1)} %copy.402) | copy-start | bytes 1572868
  93.0 170.7 %reduce-scatter.7.cloned.1.call-start = ((), (), s32[]{:S(2)}) async-start(), calls=%async_computation.7 | async-start | bytes 5242880 | tf_op jit(solution)/shard_map/reduce_scatter | solution.py:131
  111.9 14.1 %copy-start.13 = (f32[16,2,64,64]{3,0,2,1:T(8,128)}, f32[16,2,64,64]{3,0,2,1:T(8,128)S(1)}, u32[]{:S(2)}) copy-start(f32[16,2,64,64]{3,0,2,1:T(8,128)S(1)} %copy.379) | copy-start | bytes 1572868
  113.7 16.1 %copy-start.9 = (f32[16,2,64,64]{3,0,2,1:T(8,128)}, f32[16,2,64,64]{3,0,2,1:T(8,128)S(1)}, u32[]{:S(2)}) copy-start(f32[16,2,64,64]{3,0,2,1:T(8,128)S(1)} %copy.382) | copy-start | bytes 1572868
  139.9 123.7 %copy-start.76 = (bf16[1024,512]{1,0:T(8,128)(2,1)S(1)}, bf16[1024,512]{1,0:T(8,128)(2,1)}, u32[]{:S(2)}) copy-start(bf16[1024,512]{1,0:T(8,128)(2,1)} %param.26) | copy-start | bytes 3145732
  140.0 194.8 %all-gather.15.cloned.1.call-start = ((), (), s32[]{:S(2)}) async-start(), calls=%async_computation.12 | async-start | bytes 2621440 | tf_op jit(solution)/shard_map/all_gather | solution.py:137
  288.1 139.9 %reduce-scatter.13.cloned.1.call-start = ((), (), s32[]{:S(2)}) async-start(), calls=%async_computation.13 | async-start | bytes 5242880 | tf_op jit(solution)/shard_map/reduce_scatter | solution.py:140
  334.7 14.4 %copy-start.70 = (bf16[512,512]{1,0:T(8,128)(2,1)S(1)}, bf16[512,512]{1,0:T(8,128)(2,1)}, u32[]{:S(2)}) copy-start(bf16[512,512]{1,0:T(8,128)(2,1)} %convert_element_type.1851) | copy-start | bytes 1572868
  352.4 184.3 %all-gather.21.cloned.1.call-start = ((), (), s32[]{:S(2)}) async-start(), calls=%async_computation.17 | async-start | bytes 2621440 | tf_op jit(solution)/shard_map/all_gather | solution.py:153
  435.6 15.6 %copy-start.33 = (f32[4,128,512]{1,2,0:T(8,128)}, f32[4,128,512]{1,2,0:T(8,128)S(1)}, u32[]{:S(2)}) copy-start(f32[4,128,512]{1,2,0:T(8,128)S(1)} %fusion.32) | copy-start | bytes 3145732
  490.1 100.0 %reduce-scatter.17.cloned.1.call-start = ((), (), s32[]{:S(2)}) async-start(), calls=%async_computation.18 | async-start | bytes 2621440 | tf_op jit(solution)/shard_map/reduce_scatter | solution.py:161
  547.4 119.8 %all-gather.11.cloned.1.call-start = ((), (), s32[]{:S(2)}) async-start(), calls=%async_computation.8 | async-start | bytes 2621440 | tf_op jit(solution)/shard_map/all_gather | solution.py:137
  602.8 14.3 %copy-start.60 = (f32[4,128,512]{1,2,0:T(8,128)}, f32[4,128,512]{1,2,0:T(8,128)S(1)}, u32[]{:S(2)}) copy-start(f32[4,128,512]{1,2,0:T(8,128)S(1)} %get-tuple-element.163) | copy-start | bytes 3145732
  621.9 138.7 %reduce-scatter.9.cloned.1.call-start = ((), (), s32[]{:S(2)}) async-start(), calls=%async_computation.9 | async-start | bytes 5242880 | tf_op jit(solution)/shard_map/reduce_scatter | solution.py:140
  667.3 14.3 %copy-start.71 = (bf16[512,512]{1,0:T(8,128)(2,1)S(1)}, bf16[512,512]{1,0:T(8,128)(2,1)}, u32[]{:S(2)}) copy-start(bf16[512,512]{1,0:T(8,128)(2,1)} %convert_element_type.1851) | copy-start | bytes 1572868
  684.9 184.3 %all-gather.17.cloned.1.call-start = ((), (), s32[]{:S(2)}) async-start(), calls=%async_computation.14 | async-start | bytes 2621440 | tf_op jit(solution)/shard_map/all_gather | solution.py:153
  822.6 100.1 %reduce-scatter.15.cloned.1.call-start = ((), (), s32[]{:S(2)}) async-start(), calls=%async_computation.15 | async-start | bytes 2621440 | tf_op jit(solution)/shard_map/reduce_scatter | solution.py:161
  879.9 112.8 %all-gather.23.cloned.1.call-start = ((), (), s32[]{:S(2)}) async-start(), calls=%async_computation.19 | async-start | bytes 2621440 | tf_op jit(solution)/shard_map/all_gather | solution.py:169
  881.3 41.4 %copy-start.26 = (f32[512,512]{1,0:T(8,128)S(1)}, f32[512,512]{1,0:T(8,128)}, u32[]{:S(2)}) copy-start(f32[512,512]{1,0:T(8,128)} %get-tuple-element.205) | copy-start | bytes 3145732
  947.3 92.1 %all-gather.19.cloned.1.call-start = ((), (), s32[]{:S(2)}) async-start(), calls=%async_computation.16 | async-start | bytes 2621440 | tf_op jit(solution)/shard_map/all_gather | solution.py:169
  971.7 347.9 %all-reduce.16.cloned.1.call-start = ((), (), s32[]{:S(2)}) async-start(), calls=%async_computation.20 | async-start | bytes 13631488 | tf_op jit(solution)/shard_map/psum | solution.py:252
  982.2 14.1 %copy-start.115 = (f32[64]{0:T(128)S(1)}, f32[64]{0:T(128)}, u32[]{:S(2)}) copy-start(f32[64]{0:T(128)} %copy-done.114) | copy-start | bytes 772
  998.1 17.9 %copy-start.18 = (f32[2,64,64,16]{2,3,1,0:T(8,128)}, f32[2,64,64,16]{2,3,1,0:T(8,128)S(1)}, u32[]{:S(2)}) copy-start(f32[2,64,64,16]{2,3,1,0:T(8,128)S(1)} %copy.453) | copy-start | bytes 1572868
  1325.1 32.4 %copy-start.83 = (f32[512,512]{1,0:T(8,128)S(1)}, f32[512,512]{1,0:T(8,128)}, u32[]{:S(2)}) copy-start(f32[512,512]{1,0:T(8,128)} %param.43) | copy-start | bytes 3145732
  (118 other events, 742.9 us)
Sparse Core Ops, SparseCore 0:
  10.2 48.6 all-gather.12
  61.0 44.6 all-gather.8
  108.0 75.4 reduce-scatter.10
  186.3 77.2 reduce-scatter.6
  288.3 46.4 all-gather.14
  352.5 75.4 reduce-scatter.12
  490.3 46.4 all-gather.20
  547.6 42.5 reduce-scatter.16
  622.0 45.2 all-gather.10
  685.0 75.4 reduce-scatter.8
  822.7 46.4 all-gather.16
  880.0 42.5 reduce-scatter.14
  947.5 45.2 all-gather.22
  994.7 44.6 all-gather.18
  1209.2 110.2 all-reduce.15
where the time goes:
time: 1400 us; the launch traced here: 1390 us
  waiting for transfers between devices  648 us (46%)
  matrix products  362 us (26%)
  other arithmetic  164 us (12%)
  local copies, waits for them, and re-layouts  136 us (10%)
  blocking collectives  51.9 us (4%)
  between operations  23.9 us (2%)
    reduce_scatter x2, waiting for transfers between devices, one_micro(): lax.psum_scatter(plain_dot(active, down_low), 'head', scatter_dimension=0...  150 us
    reduce_scatter x2, waiting for transfers between devices, one_micro(): lax.psum_scatter(plain_dot(spectrum, out_low), 'head', scatter_dimension=...  110 us
    all_gather x2, waiting for transfers between devices, one_micro(): d_feed_rows = lax.all_gather(d_feed, 'head', axis=0, tiled=True)  93.1 us
    all_gather x2, waiting for transfers between devices, one_micro(): feed_in = lax.all_gather(season_low, 'head', axis=0, tiled=True)  87.7 us
    dot_general x8, matrix products, decompose(): jnp.einsum('bkts,bsf->kbtf', averages, shaped, precision=HIGHEST_PRECISION)  85.7 us
    reduce_scatter x2, waiting for transfers between devices, one_micro(): lax.psum_scatter(d_back.astype(jnp.bfloat16), 'head', scatter_dimension=0...  67.6 us
    psum x1, waiting for transfers between devices, on_device(): lax.psum((gradients[0], gradients[1], gradients[2], gradients[3], gradien...  66.2 us
    dot_general x6, matrix products, spectral(): jnp.einsum('bhme,heom->bhmo', real_in, w_imag, precision=HIGHEST_PRECISION)  44.1 us
  transfers between devices with their start and end apart: 15, of which 15 were waited for; matrix products, arithmetic and copies ran while one was open for 13% of the time, Pallas kernels for 0%

commit v1 on v0

v1 whole, which is shorter than its diff:
```python
from functools import partial
import math

import jax
import jax.numpy as jnp
from jax import lax
from jax.experimental import pallas as pl
from jax.experimental.pallas import tpu as pltpu
from jax.sharding import PartitionSpec as P

MODES = 64
SEQ_LEN = 128
HEAD_DIM = 64
STEP = 10
KERNEL_WIDTHS = (7, 12, 14, 24, 48)
KERNELS = len(KERNEL_WIDTHS)
BETA_ONE = 0.9
BETA_TWO = 0.999
LEARN_RATE = 0.05
EPSILON = 1e-08
DECAY = 0.01
CLIP_NORM = 0.02
LOG2E = math.log2(math.e)
LANES = 128
BF = jnp.bfloat16
F32 = jnp.float32
MIB = 1 << 20

ERF_P = 0.3275911
ERF_A = (0.254829592, -0.284496736, 1.421413741, -1.453152027, 1.061405429)


def dot(a, b, ca=1, cb=0):
    return lax.dot_general(a, b, (((ca,), (cb,)), ((), ())), preferred_element_type=F32)


def query_kernel(x_ref, w_ref, b_ref, q_ref):
    heads, _, width = w_ref.shape
    x = x_ref[...]
    for h in range(heads):
        q_ref[h] = (dot(x, w_ref[h]) + b_ref[h]).astype(BF)


def query_call(x, w_all, bias_row):
    rows, d = x.shape
    heads, _, width = w_all.shape
    step = min(256, rows)
    return pl.pallas_call(
        query_kernel,
        grid=(rows // step,),
        in_specs=[
            pl.BlockSpec((step, d), lambda i: (i, 0)),
            pl.BlockSpec((heads, d, width), lambda i: (0, 0, 0)),
            pl.BlockSpec((heads, 1, width), lambda i: (0, 0, 0)),
        ],
        out_specs=pl.BlockSpec((heads, step, width), lambda i: (0, i, 0)),
        out_shape=jax.ShapeDtypeStruct((heads, rows, width), BF),
        compiler_params=pltpu.CompilerParams(vmem_limit_bytes=24 * MIB),
        name="queries",
    )(x, w_all, bias_row.reshape(heads, 1, width))


def lane_low(rows):
    return lax.broadcasted_iota(jnp.int32, (rows, LANES), 1) < HEAD_DIM


def mix_block(wc_ref, m):
    low = lane_low(HEAD_DIM)
    zero = jnp.zeros((HEAD_DIM, LANES), F32)

    def spread(part):
        part = part.astype(F32)
        return jnp.concatenate([jnp.where(low, part, zero), jnp.where(low, zero, part)], axis=0)

    real = spread(wc_ref[m, 0])
    imag = spread(wc_ref[m, 1])
    top = jnp.concatenate([real, imag], axis=1)
    bottom = jnp.concatenate([-imag, real], axis=1)
    return jnp.concatenate([top, bottom], axis=0).astype(BF)


def pair_width(contexts):
    return 2 if contexts % 2 == 0 else 1


def spectrum_kernel(q_ref, wc_ref, tf_ref, ti_ref, spec_ref, xs_ref, x_scr, y_scr):
    contexts = q_ref.shape[0]
    pair = pair_width(contexts)
    low = lane_low(SEQ_LEN)

    def forward(p, _):
        cols = jnp.concatenate([q_ref[p * pair + k] for k in range(pair)], axis=1)
        res = dot(tf_ref[...], jnp.concatenate([cols, cols], axis=0))
        for k in range(pair):
            part = res[:, k * LANES : (k + 1) * LANES]
            x_scr[pl.ds(pl.multiple_of((p * pair + k) * SEQ_LEN, SEQ_LEN), SEQ_LEN), :] = jnp.where(
                low, part[:SEQ_LEN], part[SEQ_LEN:]
            )
        return 0

    lax.fori_loop(0, contexts // pair, forward, 0)

    def mix(m, _):
        xr = x_scr[pl.ds(m, contexts, stride=SEQ_LEN), :].astype(BF)
        xi = x_scr[pl.ds(MODES + m, contexts, stride=SEQ_LEN), :].astype(BF)
        xs_ref[m] = jnp.concatenate([xr, xi], axis=0)
        y = dot(jnp.concatenate([xr, xi], axis=1), mix_block(wc_ref, m))
        y_scr[pl.ds(m, contexts, stride=SEQ_LEN), :] = y[:, :LANES]
        y_scr[pl.ds(MODES + m, contexts, stride=SEQ_LEN), :] = y[:, LANES:]
        return 0

    lax.fori_loop(0, MODES, mix, 0, unroll=4)

    def inverse(p, _):
        parts = [
            y_scr[pl.ds(pl.multiple_of((p * pair + k) * SEQ_LEN, SEQ_LEN), SEQ_LEN), :].astype(BF)
            for k in range(pair)
        ]
        cols = jnp.concatenate(parts, axis=1)
        res = dot(ti_ref[...], jnp.concatenate([cols, cols], axis=0)).astype(BF)
        for k in range(pair):
            spec_ref[p * pair + k] = res[:, k * LANES : (k + 1) * LANES]
        return 0

    lax.fori_loop(0, contexts // pair, inverse, 0)


def spectrum_call(q, wc, tf, ti):
    contexts = q.shape[0]
    return pl.pallas_call(
        spectrum_kernel,
        out_shape=(
            jax.ShapeDtypeStruct((contexts, SEQ_LEN, LANES), BF),
            jax.ShapeDtypeStruct((MODES, 2 * contexts, LANES), BF),
        ),
        scratch_shapes=[
            pltpu.VMEM((contexts * SEQ_LEN, LANES), F32),
            pltpu.VMEM((contexts * SEQ_LEN, LANES), F32),
        ],
        compiler_params=pltpu.CompilerParams(vmem_limit_bytes=32 * MIB),
        name="spectrum",
    )(q, wc, tf, ti)


def mode_grad_kernel(me_ref, ds_ref, xs_ref, tit_ref, dy_ref, send_ref, keep_ref, y_scr, dw_scr, sems):
    contexts = ds_ref.shape[0]
    pair = pair_width(contexts)
    pieces = dw_scr.shape[0]
    depth = HEAD_DIM // pieces
    low = lane_low(HEAD_DIM)
    me = me_ref[0]

    def forward(p, _):
        cols = jnp.concatenate([ds_ref[p * pair + k] for k in range(pair)], axis=1)
        res = dot(tit_ref[...], jnp.concatenate([cols, cols], axis=0))
        for k in range(pair):
            y_scr[pl.ds(pl.multiple_of((p * pair + k) * SEQ_LEN, SEQ_LEN), SEQ_LEN), :] = res[
                :, k * LANES : (k + 1) * LANES
            ]
        return 0

    lax.fori_loop(0, contexts // pair, forward, 0)

    def mix(m, _):
        yr = y_scr[pl.ds(m, contexts, stride=SEQ_LEN), :]
        yi = y_scr[pl.ds(MODES + m, contexts, stride=SEQ_LEN), :]
        dy_ref[m] = jnp.concatenate([yr, yi], axis=1).astype(BF)
        right = jnp.concatenate(
            [jnp.concatenate([yr, yi], axis=0), jnp.concatenate([yi, -yr], axis=0)], axis=1
        ).astype(BF)
        dw = dot(xs_ref[m], right, 0, 0)
        for c in range(2):
            half = dw[:, c * LANES : (c + 1) * LANES]
            part = jnp.where(low, half[:HEAD_DIM], half[HEAD_DIM:])
            for d in range(pieces):
                dw_scr[me ^ d, m, c] = part[d * depth : (d + 1) * depth]
        return 0

    lax.fori_loop(0, MODES, mix, 0, unroll=4)
    copies = []
    for j in range(pieces):
        target = (send_ref if j % 2 else keep_ref).at[j // 2]
        copies.append(pltpu.make_async_copy(dw_scr.at[j], target, sems.at[j]))
        copies[-1].start()
    for copy in copies:
        copy.wait()


def mode_grad_call(me, ds, xs, tit, pieces):
    contexts = ds.shape[0]
    half = jax.ShapeDtypeStruct((pieces // 2, MODES, 2, HEAD_DIM // pieces, LANES), F32)
    whole = pl.BlockSpec(memory_space=pltpu.VMEM)
    anywhere = pl.BlockSpec(memory_space=pl.ANY)
    return pl.pallas_call(
        mode_grad_kernel,
        in_specs=[pl.BlockSpec(memory_space=pltpu.SMEM), whole, whole, whole],
        out_specs=(whole, anywhere, anywhere),
        out_shape=(jax.ShapeDtypeStruct((MODES, contexts, 2 * LANES), BF), half, half),
        scratch_shapes=[
            pltpu.VMEM((contexts * SEQ_LEN, LANES), F32),
            pltpu.VMEM((pieces,) + half.shape[1:], F32),
            pltpu.SemaphoreType.DMA((pieces,)),
        ],
        compiler_params=pltpu.CompilerParams(vmem_limit_bytes=40 * MIB),
        name="mode_grads",
    )(me, ds, xs, tit)


def query_grad_kernel(dy_ref, wc_ref, tft_ref, dq_ref, bias_ref, x_scr):
    contexts = dq_ref.shape[0]
    pair = pair_width(contexts)
    low = lane_low(SEQ_LEN)
    zero = jnp.zeros((SEQ_LEN, LANES), F32)

    def mix(m, _):
        dx = dot(dy_ref[m], mix_block(wc_ref, m), 1, 1)
        x_scr[pl.ds(m, contexts, stride=SEQ_LEN), :] = dx[:, :LANES]
        x_scr[pl.ds(MODES + m, contexts, stride=SEQ_LEN), :] = dx[:, LANES:]
        return 0

    lax.fori_loop(0, MODES, mix, 0, unroll=4)
    bias_ref[...] = jnp.zeros_like(bias_ref)

    def inverse(p, _):
        parts = []
        for k in range(pair):
            one = x_scr[pl.ds(pl.multiple_of((p * pair + k) * SEQ_LEN, SEQ_LEN), SEQ_LEN), :]
            parts.append(
                jnp.concatenate([jnp.where(low, one, zero), jnp.where(low, zero, one)], axis=0)
            )
        cols = jnp.concatenate(parts, axis=1).astype(BF)
        res = dot(tft_ref[...], jnp.concatenate([cols, cols], axis=0)).astype(BF)
        total = jnp.zeros((8, LANES), F32)
        for k in range(pair):
            one = res[:, k * LANES : (k + 1) * LANES]
            dq_ref[p * pair + k] = one
            total = total + jnp.sum(one.astype(F32).reshape(SEQ_LEN // 8, 8, LANES), axis=0)
        bias_ref[...] += total
        return 0

    lax.fori_loop(0, contexts // pair, inverse, 0)


def query_grad_call(dy, wc, tft):
    contexts = dy.shape[1]
    return pl.pallas_call(
        query_grad_kernel,
        out_shape=(
            jax.ShapeDtypeStruct((contexts, SEQ_LEN, LANES), BF),
            jax.ShapeDtypeStruct((8, LANES), F32),
        ),
        scratch_shapes=[pltpu.VMEM((contexts * SEQ_LEN, LANES), F32)],
        compiler_params=pltpu.CompilerParams(vmem_limit_bytes=32 * MIB),
        name="query_grads",
    )(dy, wc, tft)


SUM_SLOPE = (0, 10)
SUM_OFFSET = (5, 15)
SUM_LOSS = 20
SUM_BIAS = 21
SUM_ROWS = 24


def window_counts(first, last, rows, cols, width):
    lead = width - 1 - (width - 1) // 2
    reach = cols - rows + (lead + 1)
    here = jnp.where(cols < first, 0, jnp.where(cols >= last, width, jnp.clip(reach, 0, width)))
    before = jnp.where(
        cols <= first, 0, jnp.where(cols > last, width, jnp.clip(reach - 1, 0, width))
    )
    return (here - before).astype(F32)


def window_edges(starts, rows):
    s1, s2, s3 = starts
    first = jnp.where(rows >= s3, s3, jnp.where(rows >= s2, s2, jnp.where(rows >= s1, s1, 0)))
    last = jnp.where(
        rows < s1, s1 - 1, jnp.where(rows < s2, s2 - 1, jnp.where(rows < s3, s3 - 1, SEQ_LEN - 1))
    )
    return first, last


def fold(v):
    return jnp.sum(v.reshape(v.shape[0] // 8, 8, v.shape[1]), axis=0)


def local_kernel(
    starts_ref,
    prm_ref,
    me_ref,
    x_ref,
    spec_ref,
    tgt_ref,
    val_ref,
    up_ref,
    down_ref,
    out_ref,
    bias_ref,
    dspec_ref,
    sums_ref,
    up_send,
    up_keep,
    down_send,
    down_keep,
    out_send,
    out_keep,
    u_scr,
    trend_scr,
    season_scr,
    low_scr,
    av1_scr,
    share_scr,
    av2_scr,
    da_scr,
    part_scr,
    g_scr,
    act_scr,
    slope_scr,
    a_scr,
    at_scr,
    gup,
    gdown,
    gout,
    sems,
    *,
    chunk,
):
    step = pl.program_id(0)
    rows, d = x_ref.shape
    nctx = rows // SEQ_LEN
    heads, _, hidden_width = up_ref.shape
    out_width = out_ref.shape[1]
    groups = d // LANES
    loops = SEQ_LEN // chunk

    @pl.when(step == 0)
    def _():
        sums_ref[...] = jnp.zeros_like(sums_ref)
        gup[...] = jnp.zeros_like(gup)
        gdown[...] = jnp.zeros_like(gdown)
        gout[...] = jnp.zeros_like(gout)

    row_ids = lax.broadcasted_iota(jnp.int32, (SEQ_LEN, SEQ_LEN), 0)
    col_ids = lax.broadcasted_iota(jnp.int32, (SEQ_LEN, SEQ_LEN), 1)
    for c in range(nctx):
        ctx = step * nctx + c
        starts = [starts_ref[ctx, k] for k in range(1, 4)]
        first, last = window_edges(starts, row_ids)
        first_t, last_t = window_edges(starts, col_ids)
        for w, width in enumerate(KERNEL_WIDTHS):
            counts = window_counts(first, last, row_ids, col_ids, width).astype(BF)
            a_scr[c, w * SEQ_LEN : (w + 1) * SEQ_LEN, :SEQ_LEN] = counts
            a_scr[c, w * SEQ_LEN : (w + 1) * SEQ_LEN, SEQ_LEN:] = counts
            at_scr[c, :, w * SEQ_LEN : (w + 1) * SEQ_LEN] = window_counts(
                first_t, last_t, col_ids, row_ids, width
            ).astype(BF)

    def averages(c, u, av):
        high = u.astype(BF)
        rest = (u - high.astype(F32)).astype(BF)
        av[c] = dot(a_scr[c], jnp.concatenate([high, rest], axis=0))

    spec = jnp.concatenate([spec_ref[h] for h in range(heads)], axis=1)
    out_all = jnp.concatenate([out_ref[h] for h in range(heads)], axis=0)
    pre = x_ref[...].astype(F32) + (dot(spec, out_all) + bias_ref[...])
    u_scr[...] = pre
    for c in range(nctx):
        averages(c, pre[c * SEQ_LEN : (c + 1) * SEQ_LEN], av1_scr)

    def shares_of(u, avs, layer):
        logits = [
            u * (prm_ref[layer, 0, w] * LOG2E) + prm_ref[layer, 1, w] * LOG2E
            for w in range(KERNELS)
        ]
        top = logits[0]
        for v in logits[1:]:
            top = jnp.maximum(top, v)
        powers = [jnp.exp2(v - top) for v in logits]
        total = powers[0]
        for v in powers[1:]:
            total = total + v
        scale = 1.0 / total
        shares = [v * scale for v in powers]
        trend = shares[0] * avs[0]
        for s, a in zip(shares[1:], avs[1:]):
            trend = trend + s * a
        return shares, trend

    def read_averages(av, c, row, lanes):
        return [
            av[c, pl.ds(w * SEQ_LEN + row, chunk), lanes] * (1.0 / width)
            for w, width in enumerate(KERNEL_WIDTHS)
        ]

    def pull(shares, avs, trend, grad, u, layer, base, c, row, lanes, sums):
        rest = base
        slopes, offsets = [], []
        for w, width in enumerate(KERNEL_WIDTHS):
            d_avg = shares[w] * grad
            da_scr[c, pl.ds(w * SEQ_LEN + row, chunk), lanes] = (d_avg * (1.0 / width)).astype(BF)
            d_logit = d_avg * (avs[w] - trend)
            rest = rest + d_logit * prm_ref[layer, 0, w]
            slopes.append(sums[w] + fold(d_logit * u))
            offsets.append(sums[KERNELS + w] + fold(d_logit))
        return rest, slopes + offsets

    for c in range(nctx):
        for g in range(groups):
            lanes = slice(g * LANES, (g + 1) * LANES)

            def first_pass(r, _, c=c, lanes=lanes):
                row = pl.multiple_of(r * chunk, chunk)
                at = pl.ds(c * SEQ_LEN + row, chunk)
                u = u_scr[at, lanes]
                avs = read_averages(av1_scr, c, row, lanes)
                shares, trend = shares_of(u, avs, 0)
                for w in range(KERNELS):
                    share_scr[c, pl.ds(w * SEQ_LEN + row, chunk), lanes] = shares[w]
                season = u - trend
                trend_scr[at, lanes] = trend
                season_scr[at, lanes] = season
                low_scr[at, lanes] = season.astype(BF)
                return 0

            lax.fori_loop(0, loops, first_pass, 0)

    season_low = low_scr[...]
    feed = jnp.zeros((rows, d), F32)
    for h in range(heads):
        hid = dot(season_low, up_ref[h])
        z = jnp.abs(hid) * (2.0**-0.5)
        t = 1.0 / (1.0 + ERF_P * z)
        e = jnp.exp2(hid * hid * (-0.5 * LOG2E))
        poly = ERF_A[4]
        for coef in ERF_A[3::-1]:
            poly = poly * t + coef
        tail = (0.5 * t) * poly * e
        phi = jnp.where(hid < 0, tail, 1.0 - tail)
        active = (hid * phi).astype(BF)
        slope_scr[h] = phi + hid * e * ((2.0 * math.pi) ** -0.5)
        act_scr[h] = active
        feed = feed + dot(active, down_ref[h])

    pre = season_scr[...] + feed
    g_scr[...] = pre
    for c in range(nctx):
        averages(c, pre[c * SEQ_LEN : (c + 1) * SEQ_LEN], av2_scr)

    for c in range(nctx):
        for g in range(groups):
            lanes = slice(g * LANES, (g + 1) * LANES)

            def second_pass(r, sums, c=c, lanes=lanes):
                row = pl.multiple_of(r * chunk, chunk)
                at = pl.ds(c * SEQ_LEN + row, chunk)
                u = g_scr[at, lanes]
                avs = read_averages(av2_scr, c, row, lanes)
                shares, trend = shares_of(u, avs, 1)
                misfit = trend_scr[at, lanes] + trend - tgt_ref[at, lanes]
                weighted = val_ref[at, :] * misfit
                grad = 2.0 * weighted
                rest, new = pull(
                    shares, avs, trend, grad, u, 1, jnp.zeros_like(u), c, row, lanes, sums
                )
                part_scr[at, lanes] = rest
                g_scr[at, lanes] = grad
                return tuple(new) + (sums[2 * KERNELS] + fold(weighted * misfit),)

            zeros = tuple(jnp.zeros((8, LANES), F32) for _ in range(2 * KERNELS + 1))
            sums = lax.fori_loop(0, loops, second_pass, zeros)
            for k in range(KERNELS):
                sums_ref[SUM_SLOPE[1] + k, :, lanes] += sums[k]
                sums_ref[SUM_OFFSET[1] + k, :, lanes] += sums[KERNELS + k]
            sums_ref[SUM_LOSS, :, lanes] += sums[2 * KERNELS]

    for c in range(nctx):
        at = slice(c * SEQ_LEN, (c + 1) * SEQ_LEN)
        part_scr[at, :] += dot(at_scr[c], da_scr[c])

    d_pre = part_scr[...]
    d_feed = d_pre.astype(BF)
    back = d_pre
    for h in range(heads):
        d_hid = (dot(d_feed, down_ref[h], 1, 1) * slope_scr[h]).astype(BF)
        back = back + dot(d_hid, up_ref[h], 1, 1)
        gup[h] += dot(season_low, d_hid, 0, 0)
        gdown[h] += dot(act_scr[h], d_feed, 0, 0)
    season_scr[...] = back

    for c in range(nctx):
        for g in range(groups):
            lanes = slice(g * LANES, (g + 1) * LANES)

            def third_pass(r, sums, c=c, lanes=lanes):
                row = pl.multiple_of(r * chunk, chunk)
                at = pl.ds(c * SEQ_LEN + row, chunk)
                u = u_scr[at, lanes]
                avs = read_averages(av1_scr, c, row, lanes)
                shares = [
                    share_scr[c, pl.ds(w * SEQ_LEN + row, chunk), lanes] for w in range(KERNELS)
                ]
                d_season = season_scr[at, lanes]
                rest, new = pull(
                    shares,
                    avs,
                    trend_scr[at, lanes],
                    g_scr[at, lanes] - d_season,
                    u,
                    0,
                    d_season,
                    c,
                    row,
                    lanes,
                    sums,
                )
                part_scr[at, lanes] = rest
                return tuple(new)

            zeros = tuple(jnp.zeros((8, LANES), F32) for _ in range(2 * KERNELS))
            sums = lax.fori_loop(0, loops, third_pass, zeros)
            for k in range(KERNELS):
                sums_ref[SUM_SLOPE[0] + k, :, lanes] += sums[k]
                sums_ref[SUM_OFFSET[0] + k, :, lanes] += sums[KERNELS + k]

    for c in range(nctx):
        at = slice(c * SEQ_LEN, (c + 1) * SEQ_LEN)
        part_scr[at, :] += dot(at_scr[c], da_scr[c])

    d_pre = part_scr[...]
    sums_ref[SUM_BIAS] += fold(d_pre)
    d_attn = d_pre.astype(BF)
    d_spec = dot(d_attn, out_all, 1, 1).astype(BF)
    pieces = gout.shape[1]
    depth = out_width // pieces
    g_out = dot(spec, d_attn, 0, 0)
    for h in range(heads):
        dspec_ref[h] = d_spec[:, h * out_width : (h + 1) * out_width]
        for p in range(pieces):
            start = h * out_width + p * depth
            gout[h, p] += g_out[start : start + depth]

    @pl.when(step == pl.num_programs(0) - 1)
    def _():
        me = me_ref[0]
        copies = []
        for j in range(pieces):
            piece = me ^ j
            for k, (grad, send, keep) in enumerate(
                ((gup, up_send, up_keep), (gdown, down_send, down_keep))
            ):
                size = grad.shape[1] // pieces
                source = grad.at[:, pl.ds(pl.multiple_of(piece * size, size), size), :]
                target = (send if j % 2 else keep).at[j // 2]
                copies.append(pltpu.make_async_copy(source, target, sems.at[k, j]))
            target = (out_send if j % 2 else out_keep).at[j // 2]
            copies.append(pltpu.make_async_copy(gout.at[:, piece], target, sems.at[2, j]))
        for copy in copies:
            copy.start()
        for copy in copies:
            copy.wait()


def local_call(starts, prm, me, x, spec, target, valid, up, down, out, bias, pieces):
    rows_all, d = x.shape
    heads, _, hidden = up.shape
    width = out.shape[1]
    nctx = 2 if rows_all % (2 * SEQ_LEN) == 0 else 1
    rows = nctx * SEQ_LEN
    smem = pl.BlockSpec(memory_space=pltpu.SMEM)
    whole = pl.BlockSpec(memory_space=pltpu.VMEM)
    anywhere = pl.BlockSpec(memory_space=pl.ANY)
    halves = [
        jax.ShapeDtypeStruct((pieces // 2, heads, d // pieces, hidden), F32),
        jax.ShapeDtypeStruct((pieces // 2, heads, hidden // pieces, d), F32),
        jax.ShapeDtypeStruct((pieces // 2, heads, width // pieces, d), F32),
    ]
    return pl.pallas_call(
        partial(local_kernel, chunk=16),
        grid=(rows_all // rows,),
        in_specs=[
            smem,
            smem,
            smem,
            pl.BlockSpec((rows, d), lambda i: (i, 0)),
            pl.BlockSpec((heads, rows, width), lambda i: (0, i, 0)),
            pl.BlockSpec((rows, d), lambda i: (i, 0)),
            pl.BlockSpec((rows, 1), lambda i: (i, 0)),
            whole,
            whole,
            whole,
            whole,
        ],
        out_specs=[
            pl.BlockSpec((heads, rows, width), lambda i: (0, i, 0)),
            pl.BlockSpec((SUM_ROWS, 8, d), lambda i: (0, 0, 0)),
        ]
        + [anywhere] * 6,
        out_shape=[
            jax.ShapeDtypeStruct((heads, rows_all, width), BF),
            jax.ShapeDtypeStruct((SUM_ROWS, 8, d), F32),
        ]
        + [h for h in halves for _ in range(2)],
        scratch_shapes=[
            pltpu.VMEM((rows, d), F32),
            pltpu.VMEM((rows, d), F32),
            pltpu.VMEM((rows, d), F32),
            pltpu.VMEM((rows, d), BF),
            pltpu.VMEM((nctx, KERNELS * SEQ_LEN, d), F32),
            pltpu.VMEM((nctx, KERNELS * SEQ_LEN, d), F32),
            pltpu.VMEM((nctx, KERNELS * SEQ_LEN, d), F32),
            pltpu.VMEM((nctx, KERNELS * SEQ_LEN, d), BF),
            pltpu.VMEM((rows, d), F32),
            pltpu.VMEM((rows, d), F32),
            pltpu.VMEM((heads, rows, hidden), BF),
            pltpu.VMEM((heads, rows, hidden), F32),
            pltpu.VMEM((nctx, KERNELS * SEQ_LEN, 2 * SEQ_LEN), BF),
            pltpu.VMEM((nctx, SEQ_LEN, KERNELS * SEQ_LEN), BF),
            pltpu.VMEM((heads, d, hidden), F32),
            pltpu.VMEM((heads, hidden, d), F32),
            pltpu.VMEM((heads, pieces, width // pieces, d), F32),
            pltpu.SemaphoreType.DMA((3, pieces)),
        ],
        compiler_params=pltpu.CompilerParams(vmem_limit_bytes=56 * MIB),
        name="local_layer",
    )(starts, prm, me, x, spec, target, valid, up, down, out, bias)


def adam_kernel(me_ref, scale_ref, *refs):
    scale = scale_ref[0]
    count = len(refs) // 7
    for k in range(count):
        grad, weight, first, second = refs[4 * k : 4 * k + 4]
        outs = refs[4 * count + 3 * k : 4 * count + 3 * k + 3]
        g = grad[...] * scale
        m = BETA_ONE * first[...] + (1.0 - BETA_ONE) * g
        v = BETA_TWO * second[...] + (1.0 - BETA_TWO) * g * g
        first_hat = m * (1.0 / (1.0 - BETA_ONE**STEP))
        second_hat = v * (1.0 / (1.0 - BETA_TWO**STEP))
        w = weight[...]
        outs[0][...] = w - LEARN_RATE * (first_hat / (jnp.sqrt(second_hat) + EPSILON) + DECAY * w)
        outs[1][...] = m
        outs[2][...] = v


def adam_call(me, scale, items):
    pieces = items[0][0].shape[0]
    operands, specs, out_specs, out_shapes = [], [], [], []
    for grad, *states in items:
        block = (1,) + grad.shape[1:]
        zeros = (0,) * (grad.ndim - 1)
        specs.append(pl.BlockSpec(block, lambda i, me_ref, z=zeros: (i ^ me_ref[0],) + z))
        operands.append(grad)
        for state, axis in states:
            shape = state.shape
            state_block = shape[:axis] + (1,) + shape[axis + 1 :]
            spec = pl.BlockSpec(
                state_block,
                lambda i, me_ref, a=axis, n=len(shape): (0,) * a + (i,) + (0,) * (n - a - 1),
            )
            specs.append(spec)
            operands.append(state)
            out_specs.append(spec)
            out_shapes.append(jax.ShapeDtypeStruct(shape, F32))
    return pl.pallas_call(
        adam_body_for(items),
        grid_spec=pltpu.PrefetchScalarGridSpec(
            num_scalar_prefetch=1,
            grid=(pieces,),
            in_specs=[pl.BlockSpec(memory_space=pltpu.SMEM)] + specs,
            out_specs=out_specs,
        ),
        out_shape=out_shapes,
        compiler_params=pltpu.CompilerParams(vmem_limit_bytes=48 * MIB),
        name="adam",
    )(me, scale, *operands)


def adam_body_for(items):
    def body(me_ref, scale_ref, *refs):
        count = len(refs) // 7
        views = []
        for k in range(count):
            grad = refs[4 * k]
            axis = items[k][1][1]
            views.append(grad.at[0])
            for ref in refs[4 * k + 1 : 4 * k + 4]:
                views.append(ref.at[(slice(None),) * axis + (0,)])
        outs = []
        for k in range(count):
            axis = items[k][1][1]
            for ref in refs[4 * count + 3 * k : 4 * count + 3 * k + 3]:
                outs.append(ref.at[(slice(None),) * axis + (0,)])
        adam_kernel(me_ref, scale_ref, *views, *outs)

    return body


def adam_step(weight, gradient, moment_one, second):
    moment_one = BETA_ONE * moment_one + (1.0 - BETA_ONE) * gradient
    second = BETA_TWO * second + (1.0 - BETA_TWO) * gradient * gradient
    first_hat = moment_one / (1.0 - BETA_ONE**STEP)
    second_hat = second / (1.0 - BETA_TWO**STEP)
    weight = weight - LEARN_RATE * (first_hat / (jnp.sqrt(second_hat) + EPSILON) + DECAY * weight)
    return (weight, moment_one, second)


def swap(value, axis, size, bit):
    return lax.ppermute(value, axis, [(i, i ^ (1 << bit)) for i in range(size)])


def reduce_pieces(send, keep, size, order):
    bits = size.bit_length() - 1
    piece = keep.shape[1:]
    now = keep + swap(send, "dp", size, 0)
    now = now.reshape((2,) * (bits - 1) + piece)
    left = list(range(bits - 1, 0, -1))
    for bit in order:
        at = left.index(bit)
        away = lax.index_in_dim(now, 1, at, keepdims=False)
        stay = lax.index_in_dim(now, 0, at, keepdims=False)
        now = stay + swap(away, "dp", size, bit)
        left.remove(bit)
    return now


def gather_pieces(piece, size, order):
    have = []
    now = piece
    for bit in order:
        at = len([b for b in have if b > bit])
        now = jnp.stack([now, swap(now, "dp", size, bit)], axis=at)
        have = sorted(have + [bit], reverse=True)
    return now.reshape((size,) + piece.shape)


def sum_everywhere(value, sizes):
    for axis, size in sizes:
        for bit in range(size.bit_length() - 1):
            value = value + swap(value, axis, size, bit)
    return value


def split_low(table):
    high = lax.reduce_precision(table, 8, 7)
    return high.astype(BF), (table - high).astype(BF)


def spectral_tables(mode_index):
    heads = mode_index.shape[0]
    steps = jnp.arange(SEQ_LEN, dtype=jnp.int32)
    angles = (mode_index[:, :, None] * steps % SEQ_LEN).astype(F32) * (2.0 * math.pi / SEQ_LEN)
    ahead = jnp.concatenate([jnp.cos(angles), -jnp.sin(angles)], axis=1)
    if heads == 1:
        ahead = jnp.concatenate([ahead, jnp.zeros_like(ahead)], axis=0)
    ahead = ahead.reshape(2 * SEQ_LEN, SEQ_LEN)
    orders = jnp.arange(MODES, dtype=jnp.int32)
    angles = (steps[:, None] * orders % SEQ_LEN).astype(F32) * (2.0 * math.pi / SEQ_LEN)
    weights = jnp.where(orders == 0, 1.0, 2.0).astype(F32) / SEQ_LEN
    back = jnp.concatenate([jnp.cos(angles) * weights, -jnp.sin(angles) * weights], axis=1)
    return tuple(
        jnp.concatenate(split_low(t), axis=1) for t in (ahead, back, back.T, ahead.T)
    )


def on_device(
    sizes,
    series,
    target,
    valid,
    window_id,
    mode_index,
    query_weight,
    query_first,
    query_second,
    out_weight,
    out_first,
    out_second,
    mode_weight,
    mode_first,
    mode_second,
    up_weight,
    up_first,
    up_second,
    down_weight,
    down_first,
    down_second,
    bias_pair,
    bias_first,
    bias_second,
    decomp_params,
    decomp_first,
    decomp_second,
):
    ndp, nhead = sizes
    bits = ndp.bit_length() - 1
    order_a = list(range(1, bits))
    order_b = order_a[::-1]
    dp = lax.axis_index("dp")
    head = lax.axis_index("head")
    me = dp.astype(jnp.int32).reshape(1)
    rows, d = series.shape
    own_heads = mode_index.shape[0]
    width = query_weight.shape[1]
    hidden = up_weight.shape[1]

    query_all = lax.all_gather(query_weight.astype(BF), "head")
    packed = jnp.concatenate(
        [w.astype(BF).reshape(-1, d) for w in (up_weight, down_weight, out_weight)], axis=0
    )
    part = packed.shape[0] // ndp
    packed = lax.dynamic_slice_in_dim(packed, dp * part, part, 0)
    packed = lax.all_gather(lax.all_gather(packed, "head"), "dp")
    packed = packed.transpose(1, 0, 2, 3).reshape(nhead, -1, d)
    up_all = packed[:, :hidden].reshape(nhead, d, hidden)
    down_all = packed[:, hidden : 2 * hidden]
    out_all = packed[:, 2 * hidden :]

    tf, ti, tit, tft = spectral_tables(mode_index)
    wc = mode_weight.astype(BF).reshape(2, own_heads, HEAD_DIM, HEAD_DIM, MODES)
    wc = wc.transpose(4, 0, 2, 1, 3).reshape(MODES, 2, HEAD_DIM, own_heads * HEAD_DIM)

    def wide(v):
        pad = LANES - v.shape[-1]
        return jnp.pad(v, [(0, 0)] * (v.ndim - 1) + [(0, pad)]) if pad else v

    wc = wide(wc)

    def exchange(v):
        return lax.all_to_all(v, "head", 0, 0, tiled=True)

    queries = exchange(query_call(series, query_all, bias_pair[0]))
    queries = wide(queries.reshape(-1, SEQ_LEN, width))
    spectrum, modes_in = spectrum_call(queries, wc, tf, ti)
    spectrum = exchange(spectrum[:, :, :width].reshape(nhead, rows, width))

    series_late, spectrum = lax.optimization_barrier((series, spectrum))
    neighbours = [series] + [
        lax.ppermute(series_late, "head", [(i, (i + r) % nhead) for i in range(nhead)])
        for r in range(1, nhead)
    ]

    starts = jnp.sum(window_id[:, None, :] < jnp.arange(5)[None, :, None], axis=2).astype(jnp.int32)
    valid_float = valid.astype(F32)
    local = local_call(
        starts,
        decomp_params,
        me,
        series,
        spectrum,
        target,
        valid_float[:, None],
        up_all,
        down_all,
        out_all,
        bias_pair[1:],
        ndp,
    )
    d_spectrum, sums, up_send, up_keep, down_send, down_keep, out_send, out_keep = local

    d_spectrum = wide(exchange(d_spectrum).reshape(-1, SEQ_LEN, width))
    d_modes, mode_send, mode_keep = mode_grad_call(me, d_spectrum, modes_in, tit, ndp)
    d_queries, bias_part = query_grad_call(d_modes, wc, tft)
    d_queries = d_queries[:, :, :width].reshape(nhead, rows, width)
    d_query = sum(
        dot(x, lax.dynamic_index_in_dim(d_queries, lax.rem(head + nhead - r, nhead), 0, False), 0, 0)
        for r, x in enumerate(neighbours)
    )

    sums = jnp.sum(sums, axis=1)
    bias_zero = lax.dynamic_update_slice_in_dim(
        jnp.zeros((d,), F32), jnp.sum(bias_part, axis=0)[:width], head * width, 0
    )
    small = jnp.concatenate(
        [bias_zero, sums[SUM_BIAS], jnp.sum(sums[:SUM_BIAS], axis=1), jnp.sum(valid_float)[None]]
    )
    small = jnp.pad(small, (0, -small.shape[0] % LANES)).reshape(-1, LANES)
    everyone = (("dp", ndp), ("head", nhead))
    small = sum_everywhere(small, everyone).reshape(-1)
    loss_sum = small[2 * d + SUM_LOSS]
    valid_count = small[2 * d + SUM_BIAS]
    bias_grad = small[: 2 * d].reshape(2, d) / valid_count
    flat = small[2 * d : 2 * d + 4 * KERNELS]
    decomp_grad = flat.reshape(2, 2, KERNELS) / valid_count

    up_piece = jnp.sum(exchange(reduce_pieces(up_send, up_keep, ndp, order_a)), axis=0)
    down_piece = jnp.sum(exchange(reduce_pieces(down_send, down_keep, ndp, order_b)), axis=0)
    out_piece = jnp.sum(exchange(reduce_pieces(out_send, out_keep, ndp, order_a)), axis=0)
    query_piece = jnp.sum(
        lax.all_to_all(d_query.reshape(ndp, d // ndp, width), "dp", 0, 0, tiled=True), axis=0
    )
    half = MODES // 2
    mode_piece = jnp.concatenate(
        [
            reduce_pieces(mode_send[:, :half], mode_keep[:, :half], ndp, order_a),
            reduce_pieces(mode_send[:, half:], mode_keep[:, half:], ndp, order_b),
        ],
        axis=0,
    )
    depth = HEAD_DIM // ndp
    mode_piece = mode_piece.reshape(MODES, 2, depth, 2, HEAD_DIM).transpose(1, 3, 2, 4, 0)
    mode_piece = mode_piece.reshape(2, 2, depth, HEAD_DIM * MODES)[:, :own_heads]

    pieces = (query_piece, out_piece, mode_piece, up_piece, down_piece)
    squares = sum(jnp.sum(p * p) for p in pieces)
    squares = sum_everywhere(jnp.broadcast_to(squares, (8, LANES)), everyone)[0, 0]
    inverse = 1.0 / valid_count
    grad_norm = jnp.sqrt(
        squares * inverse * inverse
        + jnp.sum(bias_grad * bias_grad)
        + jnp.sum(decomp_grad * decomp_grad)
    )
    factor = jnp.minimum(1.0, CLIP_NORM / (grad_norm + 1e-06))

    down_order = list(range(bits - 1, -1, -1))
    up_order = order_a[:] + [0]
    query_g = gather_pieces(query_piece, ndp, down_order)
    out_g = gather_pieces(out_piece, ndp, down_order)
    up_g = gather_pieces(up_piece, ndp, down_order)
    down_g = gather_pieces(down_piece, ndp, up_order)
    mode_g = jnp.concatenate(
        [
            gather_pieces(mode_piece[:1], ndp, down_order),
            gather_pieces(mode_piece[1:], ndp, up_order),
        ],
        axis=1,
    )

    def cut(arrays, axis):
        return [
            (a.reshape(a.shape[:axis] + (ndp, a.shape[axis] // ndp) + a.shape[axis + 1 :]), axis)
            for a in arrays
        ]

    states = (
        (query_weight, query_first, query_second),
        (out_weight, out_first, out_second),
        (mode_weight, mode_first, mode_second),
        (up_weight, up_first, up_second),
        (down_weight, down_first, down_second),
    )
    axes = (0, 0, 2, 0, 0)
    items = [
        (g, *cut(s, a)) for g, s, a in zip((query_g, out_g, mode_g, up_g, down_g), states, axes)
    ]
    news = adam_call(me, (factor * inverse).reshape(1), items)
    news = [n.reshape(states[k // 3][0].shape) for k, n in enumerate(news)]
    news += adam_step(bias_pair, bias_grad * factor, bias_first, bias_second)
    news += adam_step(decomp_params, decomp_grad * factor, decomp_first, decomp_second)
    return (loss_sum, valid_count, grad_norm, *news)


def solution(mesh):
    rows = P(("dp", "head"), None)
    down = P("head", None)
    across = P(None, "head")
    modes = P(None, "head", None, None)
    weights = (across,) * 3 + (down,) * 3 + (modes,) * 3 + (across,) * 3 + (down,) * 3 + (P(),) * 6
    sizes = (mesh.shape["dp"], mesh.shape["head"])
    return jax.shard_map(
        partial(on_device, sizes),
        mesh=mesh,
        in_specs=(rows, rows, P(("dp", "head")), rows, down) + weights,
        out_specs=(P(), P(), P()) + weights,
        check_vma=False,
    )
```

time: 1400 us -> 551 us (0.39)
  waiting for transfers between devices: 648 us -> 121 us
  matrix products: 362 us -> 5.05 us
  Pallas kernels: 0 us -> 127 us
  starting transfers between devices: 1 us -> 111 us
  other arithmetic: 164 us -> 57 us
  local copies, waits for them, and re-layouts: 136 us -> 61.2 us
    dot_general x70 -> x4, matrix products: 362 us -> 5.05 us  [dot(): lax.dot_general(a, b, (((ca,), (cb,)), ((), ())), preferred_element_type=...]
    reduce_scatter x6 -> x0, waiting for transfers between devices: 328 us -> none  [the longest x2 150 us: one_micro(): lax.psum_scatter(plain_dot(active, down_low), 'head', scatter_dimension=0...]
    all_gather x8 -> x1, waiting for transfers between devices: 253 us -> 0.01 us  [on_device(): packed = lax.all_gather(lax.all_gather(packed, 'head'), 'dp')]
    pallas_call x0 -> x6, Pallas kernels: none -> 127 us  [the longest x1 80.4 us: local_call(): pl.pallas_call(partial(local_kernel, chunk=16), grid=(rows_all // rows,),...]
    ppermute x0 -> x46, waiting for transfers between devices: none -> 85.7 us  [the longest x43 75.5 us: swap(): return lax.ppermute(value, axis, [(i, i ^ 1 << bit) for i in range(size)])]
    ppermute x0 -> x46, starting transfers between devices: none -> 85 us  [the longest x43 80.1 us: swap(): return lax.ppermute(value, axis, [(i, i ^ 1 << bit) for i in range(size)])]
    psum x1 -> x0, waiting for transfers between devices: 66.2 us -> none  [on_device(): lax.psum((gradients[0], gradients[1], gradients[2], gradients[3], gradien...]
    reduce_sum x18 -> x14, other arithmetic: 71 us -> 11 us  [the longest x5 4.92 us: on_device(): squares = sum((jnp.sum(p * p) for p in pieces))]
  transfers between devices with their start and end apart: 15 -> 53, of which waited for: 15 -> 21; matrix products, arithmetic and copies ran while one was open for 13% -> 18% of each run, Pallas kernels for 0% -> 5%
where the time goes in v1:
time: 551 us; the launch traced here: 548 us
  Pallas kernels  127 us (23%)
  waiting for transfers between devices  121 us (22%)
  starting transfers between devices  111 us (20%)
  local copies, waits for them, and re-layouts  61.2 us (11%)
  other arithmetic  57 us (10%)
  blocking collectives  43.8 us (8%)
  between operations  22.1 us (4%)
    pallas_call x1, Pallas kernels, local_call(): pl.pallas_call(partial(local_kernel, chunk=16), grid=(rows_all // rows,),...  80.4 us
    ppermute x43, starting transfers between devices, swap(): return lax.ppermute(value, axis, [(i, i ^ 1 << bit) for i in range(size)])  80.1 us
    ppermute x43, waiting for transfers between devices, swap(): return lax.ppermute(value, axis, [(i, i ^ 1 << bit) for i in range(size)])  75.5 us
    all_to_all x5, waiting for transfers between devices, exchange(): return lax.all_to_all(v, 'head', 0, 0, tiled=True)  32.3 us
    all_to_all x5, starting transfers between devices, exchange(): return lax.all_to_all(v, 'head', 0, 0, tiled=True)  21.9 us
    all_gather x1, blocking collectives, on_device(): packed = lax.all_gather(lax.all_gather(packed, 'head'), 'dp')  18.6 us
    pallas_call x1, Pallas kernels, adam_call(): pl.pallas_call(adam_body_for(items), grid_spec=pltpu.PrefetchScalarGridSp...  17.4 us
    reshape x2, local copies, waits for them, and re-layouts, on_device(): wc = mode_weight.astype(BF).reshape(2, own_heads, HEAD_DIM, HEAD_DIM, MODES)  17.2 us
  transfers between devices with their start and end apart: 53, of which 21 were waited for; matrix products, arithmetic and copies ran while one was open for 18% of the time, Pallas kernels for 5%

profile of v1, /device:TPU:0, one launch (start us, length us, event | category | flops | bytes accessed | tf_op | source)
XLA Modules:
  0.0 548.1 jit_solution(11028377126115868072)
XLA Ops:
  10.0 18.6 %all-gather.1 = bf16[576,512]{1,0:T(8,128)(2,1)} all-gather(bf16[144,512]{1,0:T(8,128)(2,1)S(1)} %fusion.20), channel_id=3, replica_groups=mesh['dp'=8,'head'=4] {'head'}, dimensions={0}, use_global_device_ids=true | all-gather | bytes 737280 | tf_op jit(solution)/shard_map/all_gather | solution.py:813
  28.6 16.3 %all-gather = bf16[2048,128]{1,0:T(8,128)(2,1)S(1)} all-gather(bf16[512,128]{1,0:T(8,128)(2,1)S(1)} %convert_element_type.56), channel_id=2, replica_groups=mesh['dp'=8,'head'=4] {'head'}, dimensions={0}, use_global_device_ids=true | all-gather | bytes 655360 | tf_op jit(solution)/shard_map/all_gather | solution.py:807
  48.2 4.8 all-to-all-start
  55.5 5.5 %reshape.244 = bf16[2,2,64,64,64]{4,3,2,1,0:T(8,128)(2,1)} reshape(bf16[2,2,64,4096]{3,2,1,0:T(8,128)(2,1)S(1)} %convert_element_type.57) | data formatting | bytes 4194304 | tf_op jit(solution)/shard_map/reshape | solution.py:820
  61.0 11.7 %copy.158 = bf16[2,2,64,64,64]{3,1,2,0,4:T(2,128)(2,1)} copy(bf16[2,2,64,64,64]{4,3,2,1,0:T(8,128)(2,1)} %reshape.244) | data formatting | bytes 4194304 | tf_op jit(solution)/shard_map/reshape | solution.py:820
  72.7 6.8 %reshape.245.wc_ref = bf16[64,2,64,128]{3,2,1,0:T(8,128)(2,1)S(1)} reshape(bf16[64,2,64,2,64]{4,3,2,1,0:T(2,128)(2,1)} %bitcast.251) | data formatting | bytes 4194304 | tf_op jit(solution)/shard_map/reshape | solution.py:821
  87.8 9.9 %spectrum.1 = (bf16[32,128,128]{2,1,0:T(8,128)(2,1)S(1)}, bf16[64,64,128]{2,1,0:T(8,128)(2,1)S(1)}) custom-call(bf16[32,128,128]{2,1,0:T(8,128)(2,1)S(1)} %bitcast.231, bf16[64,2,64,128]{3,2,1,0:T(8,128)(2,1)S(1)} %reshape.245.wc_ref, bf16[256,256]{1,0:T(8,128)(2,1)S(1)} %copy.160.tf_ref, bf16[128,256]{1,0:T(8,128)(2,1)S(1)} %copy-done.20), custom_call_target="tpu_custom_call" | custom-call | tf_op jit(solution)/shard_map/spectrum/pallas_call | solution.py:130
  99.6 5.0 all-to-all-start.1
  106.5 17.5 %all-to-all-done.1.spec_ref = bf16[4,1024,128]{2,1,0:T(8,128)(2,1)S(1)} async-done(((bf16[4,1024,128]{2,1,0:T(8,128)(2,1)}), bf16[4,1024,128]{2,1,0:T(8,128)(2,1)S(1)}, u32[]{:S(2)}, u32[]{:S(2)}) %all-to-all-start.1) | async-done | bytes 1048608 | tf_op jit(solution)/shard_map/all_to_all | solution.py:830
  130.2 80.4 %local_layer.1 = (bf16[4,1024,128]{2,1,0:T(8,128)(2,1)}, f32[24,8,512]{2,1,0:T(8,128)}, f32[4,4,64,512]{3,2,1,0:T(8,128)}, f32[4,4,64,512]{3,2,1,0:T(8,128)}, f3...) custom-call(s32[8,5]{1,0:T(8,128)} %copy.163.starts_ref, ...), custom_call_target="tpu_custom_call" | custom-call | tf_op jit(solution)/shard_map/local_layer/pallas_call | solution.py:578
  215.4 6.9 %collective-permute-done.9 = f32[2,4,16,512]{3,2,1,0:T(8,128)S(1)} collective-permute-done((f32[2,4,16,512]{3,2,1,0:T(8,128)S(1)}, f32[2,4,16,512]{3,2,1,0:T(8,128)S(1)}, u32[]{:S(2)}, u32[]{:S(2)}) %collective-permute-start.9) | collective-permute-done | bytes 262176 | tf_op jit(solution)/shard_map/ppermute | solution.py:709
  224.0 3.4 collective-permute-done.10
  227.4 9.0 %all_to_all.35 = f32[4,16,512]{2,1,0:T(8,128)} all-to-all(f32[4,16,512]{2,1,0:T(8,128)S(1)} %fusion.23), channel_id=1, replica_groups=mesh['dp'=8,'head'=4] {'head'}, dimensions={0} | all-to-all | bytes 262144 | tf_op jit(solution)/shard_map/all_to_all | solution.py:830
  236.4 4.2 all-to-all-start.2
  245.8 3.8 collective-permute-start.7
  260.6 4.5 all-to-all-done.2
  267.2 8.8 %mode_grads.1 = (bf16[64,32,256]{2,1,0:T(8,128)(2,1)S(1)}, f32[4,64,2,8,128]{4,3,2,1,0:T(8,128)S(1)}, f32[4,64,2,8,128]{4,3,2,1,0:T(8,128)S(1)}) custom-call(s32[1]{0:T(128)} %bitcast.me_ref, bf16[32,128,128]{2,1,0:T(8,128)(2,1)} %bitcast.12.ds_ref, bf16[64,64,128]{2,1,0:T(8,128)(2,1)S(1)} %copy-done.10, bf16[128,256]{1,0:T(8,128)(2,1)S(1)} %copy-done.19), custom_call_target="tpu_custom_call" | custom-call | tf_op jit(solution)/shard_map/mode_grads/pallas_call | solution.py:194
  277.3 8.1 %query_grads.1 = (bf16[32,128,128]{2,1,0:T(8,128)(2,1)S(1)}, f32[8,128]{1,0:T(8,128)S(1)}) custom-call(bf16[64,32,256]{2,1,0:T(8,128)(2,1)S(1)} %get-tuple-element.60.dy_ref, bf16[64,2,64,128]{3,2,1,0:T(8,128)(2,1)S(1)} %reshape.245.wc_ref, bf16[128,512]{1,0:T(8,128)(2,1)S(1)} %pad_maximum_fusion.18.tft_ref), custom_call_target="tpu_custom_call" | custom-call | tf_op jit(solution)/shard_map/query_grads/pallas_call | solution.py:246
  290.1 3.1 fusion.62
  296.9 45.3 %collective-permute-start.3 = (f32[9,128]{1,0:T(8,128)S(1)}, f32[9,128]{1,0:T(8,128)S(1)}, u32[]{:S(2)}, u32[]{:S(2)}) collective-permute-start(f32[9,128]{1,0:T(8,128)S(1)} %add.188), channel_id=1, source_target_pairs={{0,1},{1,0},{2,3},{3,2},{4,5},{5,4},{6,7},{7,6},{8,9},{9,8},{10,11... | collective-permute-start | bytes 13832 | tf_op jit(solution)/shard_map/ppermute | solution.py:709
  343.8 10.2 %collective-permute-done.6 = bf16[1024,512]{1,0:T(8,128)(2,1)} collective-permute-done((bf16[1024,512]{1,0:T(8,128)(2,1)S(1)}, bf16[1024,512]{1,0:T(8,128)(2,1)}, u32[]{:S(2)}, u32[]{:S(2)}) %collective-permute-start.6) | collective-permute-done | bytes 1048608 | tf_op jit(solution)/shard_map/ppermute | solution.py:839
  358.6 3.8 all-to-all-start.3
  366.2 3.1 all-to-all-done.3
  383.3 16.1 %collective-permute-done.29 = f32[2,64,128]{2,1,0:T(8,128)S(1)} collective-permute-done((f32[2,64,128]{2,1,0:T(8,128)S(1)}, f32[2,64,128]{2,1,0:T(8,128)S(1)}, u32[]{:S(2)}, u32[]{:S(2)}) %collective-permute-start.29) | collective-permute-done | bytes 65568 | tf_op jit(solution)/shard_map/ppermute | solution.py:709
  411.1 17.8 %collective-permute-done.21 = f32[2,4,64,512]{3,2,1,0:T(8,128)S(1)} collective-permute-done((f32[2,4,64,512]{3,2,1,0:T(8,128)S(1)}, f32[2,4,64,512]{3,2,1,0:T(8,128)S(1)}, u32[]{:S(2)}, u32[]{:S(2)}) %collective-permute-start.21) | collective-permute-done | bytes 1048608 | tf_op jit(solution)/shard_map/ppermute | solution.py:709
  431.2 8.6 %collective-permute-done.19 = f32[4,64,512]{2,1,0:T(8,128)S(1)} collective-permute-done((f32[4,64,512]{2,1,0:T(8,128)S(1)}, f32[4,64,512]{2,1,0:T(8,128)S(1)}, u32[]{:S(2)}, u32[]{:S(2)}) %collective-permute-start.19) | collective-permute-done | bytes 524320 | tf_op jit(solution)/shard_map/ppermute | solution.py:709
  440.7 4.2 all-to-all-start.5
  451.2 8.7 %all-to-all-done.5 = f32[4,64,512]{2,1,0:T(8,128)} async-done(((f32[4,64,512]{2,1,0:T(8,128)}), f32[4,64,512]{2,1,0:T(8,128)}, u32[]{:S(2)}, u32[]{:S(2)}) %all-to-all-start.5) | async-done | bytes 524320 | tf_op jit(solution)/shard_map/all_to_all | solution.py:830
  459.9 3.7 all-to-all-start.6
  486.8 7.8 %collective-permute-done.25 = f32[8,128]{1,0:T(8,128)S(1)} collective-permute-done((f32[8,128]{1,0:T(8,128)S(1)}, f32[8,128]{1,0:T(8,128)S(1)}, u32[]{:S(2)}, u32[]{:S(2)}) %collective-permute-start.25) | collective-permute-done | bytes 4128 | tf_op jit(solution)/shard_map/ppermute | solution.py:709
  510.3 4.1 collective-permute-done.41
  522.7 17.4 %adam.1 = (f32[8,64,128]{2,1,0:T(8,128)}, f32[8,64,128]{2,1,0:T(8,128)}, f32[8,64,128]{2,1,0:T(8,128)}, f32[8,16,512]{2,1,0:T(8,128)}, f32[8,16,512]{2,1,0:T(8,1...) custom-call(s32[1]{0:T(128)} %bitcast.me_ref, ...), custom_call_target="tpu_custom_call" | custom-call | tf_op jit(solution)/shard_map/adam/pallas_call | solution.py:665
  (295 shorter events, 147.0 us)
Async XLA Ops:
  7.2 116.8 %all-gather.5.cloned.1.call-start = ((), (), s32[]{:S(2)}) async-start(), calls=%async_computation.7 | async-start | bytes 5308416 | tf_op jit(solution)/shard_map/all_gather | solution.py:813
  48.2 38.7 %all-to-all-start = ((bf16[4,1024,128]{2,1,0:T(8,128)(2,1)}), bf16[4,1024,128]{2,1,0:T(8,128)(2,1)S(1)}, u32[]{:S(2)}, u32[]{:S(2)}) async-start(bf16[4,1024,128]{2,1,0:T(8,128)(2,1)} %queries.1), calls=%async_computation | async-start | bytes 2097152 | tf_op jit(solution)/shard_map/all_to_all | solution.py:830
  99.6 24.4 %all-to-all-start.1 = ((bf16[4,1024,128]{2,1,0:T(8,128)(2,1)}), bf16[4,1024,128]{2,1,0:T(8,128)(2,1)S(1)}, u32[]{:S(2)}, u32[]{:S(2)}) async-start(bf16[4,1024,128]{2,1,0:T(8,128)(2,1)} %bitcast.239), calls=%async_computation.1 | async-start | bytes 2097152 | tf_op jit(solution)/shard_map/all_to_all | solution.py:830
  236.4 28.7 %all-to-all-start.2 = ((bf16[4,1024,128]{2,1,0:T(8,128)(2,1)}), bf16[4,1024,128]{2,1,0:T(8,128)(2,1)}, u32[]{:S(2)}, u32[]{:S(2)}) async-start(bf16[4,1024,128]{2,1,0:T(8,128)(2,1)} %get-tuple-element.58), calls=%async_computation.2 | async-start | bytes 2097152 | tf_op jit(solution)/shard_map/all_to_all | solution.py:830
  245.8 51.1 %collective-permute-start.7 = (bf16[1024,512]{1,0:T(8,128)(2,1)S(1)}, bf16[1024,512]{1,0:T(8,128)(2,1)}, u32[]{:S(2)}, u32[]{:S(2)}) collective-permute-start(bf16[1024,512]{1,0:T(8,128)(2,1)S(1)} %copy-done.1), channel_id=1, source_target_pairs={{0,3},{1,0},{2,1},{3,2},{4,7},{5,4},{6,5},{7,6},{8,11},{9,8},{10,9... | collective-permute-start | bytes 3145736 | tf_op jit(solution)/shard_map/ppermute | solution.py:839
  249.6 104.4 %collective-permute-start.6 = (bf16[1024,512]{1,0:T(8,128)(2,1)S(1)}, bf16[1024,512]{1,0:T(8,128)(2,1)}, u32[]{:S(2)}, u32[]{:S(2)}) collective-permute-start(bf16[1024,512]{1,0:T(8,128)(2,1)S(1)} %copy-done.1), channel_id=1, source_target_pairs={{0,2},{1,3},{2,0},{3,1},{4,6},{5,7},{6,4},{7,5},{8,10},{9,11},{10,... | collective-permute-start | bytes 3145736 | tf_op jit(solution)/shard_map/ppermute | solution.py:839
  249.6 106.5 %collective-permute-start.5 = (bf16[1024,512]{1,0:T(8,128)(2,1)S(1)}, bf16[1024,512]{1,0:T(8,128)(2,1)}, u32[]{:S(2)}, u32[]{:S(2)}) collective-permute-start(bf16[1024,512]{1,0:T(8,128)(2,1)S(1)} %copy-done.1), channel_id=1, source_target_pairs={{0,1},{1,2},{2,3},{3,0},{4,5},{5,6},{6,7},{7,4},{8,9},{9,10},{10,1... | collective-permute-start | bytes 3145736 | tf_op jit(solution)/shard_map/ppermute | solution.py:839
  253.2 116.8 %collective-permute-start.17 = (f32[4,4,64,512]{3,2,1,0:T(8,128)}, f32[4,4,64,512]{3,2,1,0:T(8,128)}, u32[]{:S(2)}, u32[]{:S(2)}) collective-permute-start(f32[4,4,64,512]{3,2,1,0:T(8,128)} %get-tuple-element.70), channel_id=1, source_target_pairs={{0,4},{4,0},{8,12},{12,8},{16,20},{20,16},{24,28},{28,24},{1,5},{5... | collective-permute-start | bytes 6291464 | tf_op jit(solution)/shard_map/ppermute | solution.py:709
  259.2 28.1 %collective-permute-start.33 = (f32[2,2,16,512]{3,2,1,0:T(8,128)}, f32[2,2,16,512]{3,2,1,0:T(8,128)}, u32[]{:S(2)}, u32[]{:S(2)}) collective-permute-start(f32[2,2,16,512]{3,2,1,0:T(8,128)} %get-tuple-element.121), channel_id=1, source_target_pairs={{0,4},{4,0},{8,12},{12,8},{16,20},{20,16},{24,28},{28,24},{1,5},{5... | collective-permute-start | bytes 393224 | tf_op jit(solution)/shard_map/ppermute | solution.py:709
  296.9 103.2 %collective-permute-start.20 = (f32[4,4,64,512]{3,2,1,0:T(8,128)}, f32[4,4,64,512]{3,2,1,0:T(8,128)}, u32[]{:S(2)}, u32[]{:S(2)}) collective-permute-start(f32[4,4,64,512]{3,2,1,0:T(8,128)} %get-tuple-element.72), channel_id=1, source_target_pairs={{0,4},{4,0},{8,12},{12,8},{16,20},{20,16},{24,28},{28,24},{1,5},{5... | collective-permute-start | bytes 6291464 | tf_op jit(solution)/shard_map/ppermute | solution.py:709
  296.9 57.1 %collective-permute-start.3 = (f32[9,128]{1,0:T(8,128)S(1)}, f32[9,128]{1,0:T(8,128)S(1)}, u32[]{:S(2)}, u32[]{:S(2)}) collective-permute-start(f32[9,128]{1,0:T(8,128)S(1)} %add.188), channel_id=1, source_target_pairs={{0,1},{1,0},{2,3},{3,2},{4,5},{5,4},{6,7},{7,6},{8,9},{9,8},{10,11... | collective-permute-start | bytes 13832 | tf_op jit(solution)/shard_map/ppermute | solution.py:709
  354.0 20.4 %collective-permute-start.11 = (f32[4,32,2,8,128]{4,3,2,1,0:T(8,128)}, f32[4,32,2,8,128]{4,3,2,1,0:T(8,128)}, u32[]{:S(2)}, u32[]{:S(2)}) collective-permute-start(f32[4,32,2,8,128]{4,3,2,1,0:T(8,128)} %get-tuple-element.100), channel_id=1, source_target_pairs={{0,4},{4,0},{8,12},{12,8},{16,20},{20,16},{24,28},{28,24},{1,5},{5... | collective-permute-start | bytes 3145736 | tf_op jit(solution)/shard_map/ppermute | solution.py:709
  354.0 20.4 %collective-permute-start.14 = (f32[4,32,2,8,128]{4,3,2,1,0:T(8,128)}, f32[4,32,2,8,128]{4,3,2,1,0:T(8,128)}, u32[]{:S(2)}, u32[]{:S(2)}) collective-permute-start(f32[4,32,2,8,128]{4,3,2,1,0:T(8,128)} %get-tuple-element.101), channel_id=1, source_target_pairs={{0,4},{4,0},{8,12},{12,8},{16,20},{20,16},{24,28},{28,24},{1,5},{5... | collective-permute-start | bytes 3145736 | tf_op jit(solution)/shard_map/ppermute | solution.py:709
  369.3 10.8 %collective-permute-start.28 = (f32[64,128]{1,0:T(8,128)S(1)}, f32[64,128]{1,0:T(8,128)S(1)}, u32[]{:S(2)}, u32[]{:S(2)}) collective-permute-start(f32[64,128]{1,0:T(8,128)S(1)} %reduce_sum.149), channel_id=1, source_target_pairs={{0,16},{4,20},{8,24},{12,28},{16,0},{20,4},{24,8},{28,12},{1,17},{... | collective-permute-start | bytes 98312 | tf_op jit(solution)/shard_map/ppermute | solution.py:709
  373.8 34.7 %collective-permute-start.18 = (f32[2,4,64,512]{3,2,1,0:T(8,128)}, f32[2,4,64,512]{3,2,1,0:T(8,128)}, u32[]{:S(2)}, u32[]{:S(2)}) collective-permute-start(f32[2,4,64,512]{3,2,1,0:T(8,128)} %slice_bitcast_fusion), channel_id=1, source_target_pairs={{0,8},{4,12},{8,0},{12,4},{16,24},{20,28},{24,16},{28,20},{1,9},{5... | collective-permute-start | bytes 3145736 | tf_op jit(solution)/shard_map/ppermute | solution.py:709
  378.6 27.9 %collective-permute-start.15 = (f32[2,32,2,8,128]{4,3,2,1,0:T(8,128)S(1)}, f32[2,32,2,8,128]{4,3,2,1,0:T(8,128)}, u32[]{:S(2)}, u32[]{:S(2)}) collective-permute-start(f32[2,32,2,8,128]{4,3,2,1,0:T(8,128)S(1)} %slice.181), channel_id=1, source_target_pairs={{0,16},{4,20},{8,24},{12,28},{16,0},{20,4},{24,8},{28,12},{1,17},{... | collective-permute-start | bytes 1572872 | tf_op jit(solution)/shard_map/ppermute | solution.py:709
  380.2 19.2 %collective-permute-start.29 = (f32[2,64,128]{2,1,0:T(8,128)S(1)}, f32[2,64,128]{2,1,0:T(8,128)S(1)}, u32[]{:S(2)}, u32[]{:S(2)}) collective-permute-start(f32[2,64,128]{2,1,0:T(8,128)S(1)} %get-tuple-element.131), channel_id=1, source_target_pairs={{0,8},{4,12},{8,0},{12,4},{16,24},{20,28},{24,16},{28,20},{1,9},{5... | collective-permute-start | bytes 196616 | tf_op jit(solution)/shard_map/ppermute | solution.py:709
  400.1 85.8 %collective-permute-start.30 = (f32[2,2,64,128]{3,2,1,0:T(8,128)}, f32[2,2,64,128]{3,2,1,0:T(8,128)}, u32[]{:S(2)}, u32[]{:S(2)}) collective-permute-start(f32[2,2,64,128]{3,2,1,0:T(8,128)} %get-tuple-element.123), channel_id=1, source_target_pairs={{0,4},{4,0},{8,12},{12,8},{16,20},{20,16},{24,28},{28,24},{1,5},{5... | collective-permute-start | bytes 393224 | tf_op jit(solution)/shard_map/ppermute | solution.py:709
  402.9 26.0 %collective-permute-start.21 = (f32[2,4,64,512]{3,2,1,0:T(8,128)S(1)}, f32[2,4,64,512]{3,2,1,0:T(8,128)S(1)}, u32[]{:S(2)}, u32[]{:S(2)}) collective-permute-start(f32[2,4,64,512]{3,2,1,0:T(8,128)S(1)} %slice.189), channel_id=1, source_target_pairs={{0,16},{4,20},{8,24},{12,28},{16,0},{20,4},{24,8},{28,12},{1,17},{... | collective-permute-start | bytes 3145736 | tf_op jit(solution)/shard_map/ppermute | solution.py:709
  405.3 39.6 %collective-permute-start.12 = (f32[2,32,2,8,128]{4,3,2,1,0:T(8,128)}, f32[2,32,2,8,128]{4,3,2,1,0:T(8,128)}, u32[]{:S(2)}, u32[]{:S(2)}) collective-permute-start(f32[2,32,2,8,128]{4,3,2,1,0:T(8,128)} %slice_bitcast_fusion.6), channel_id=1, source_target_pairs={{0,8},{4,12},{8,0},{12,4},{16,24},{20,28},{24,16},{28,20},{1,9},{5... | collective-permute-start | bytes 1572872 | tf_op jit(solution)/shard_map/ppermute | solution.py:709
  407.7 40.5 %collective-permute-start.16 = (f32[32,2,8,128]{3,2,1,0:T(8,128)S(1)}, f32[32,2,8,128]{3,2,1,0:T(8,128)}, u32[]{:S(2)}, u32[]{:S(2)}) collective-permute-start(f32[32,2,8,128]{3,2,1,0:T(8,128)S(1)} %slice_bitcast_fusion.8), channel_id=1, source_target_pairs={{0,8},{4,12},{8,0},{12,4},{16,24},{20,28},{24,16},{28,20},{1,9},{5... | collective-permute-start | bytes 786440 | tf_op jit(solution)/shard_map/ppermute | solution.py:709
  410.0 29.8 %collective-permute-start.19 = (f32[4,64,512]{2,1,0:T(8,128)S(1)}, f32[4,64,512]{2,1,0:T(8,128)S(1)}, u32[]{:S(2)}, u32[]{:S(2)}) collective-permute-start(f32[4,64,512]{2,1,0:T(8,128)S(1)} %slice_bitcast_fusion.4), channel_id=1, source_target_pairs={{0,16},{4,20},{8,24},{12,28},{16,0},{20,4},{24,8},{28,12},{1,17},{... | collective-permute-start | bytes 1572872 | tf_op jit(solution)/shard_map/ppermute | solution.py:709
  430.0 19.2 %collective-permute-start.22 = (f32[4,64,512]{2,1,0:T(8,128)}, f32[4,64,512]{2,1,0:T(8,128)}, u32[]{:S(2)}, u32[]{:S(2)}) collective-permute-start(f32[4,64,512]{2,1,0:T(8,128)} %slice_bitcast_fusion.2), channel_id=1, source_target_pairs={{0,8},{4,12},{8,0},{12,4},{16,24},{20,28},{24,16},{28,20},{1,9},{5... | collective-permute-start | bytes 1572872 | tf_op jit(solution)/shard_map/ppermute | solution.py:709
  440.7 19.3 %all-to-all-start.5 = ((f32[4,64,512]{2,1,0:T(8,128)}), f32[4,64,512]{2,1,0:T(8,128)}, u32[]{:S(2)}, u32[]{:S(2)}) async-start(f32[4,64,512]{2,1,0:T(8,128)} %fusion.4), calls=%async_computation.5 | async-start | bytes 1048576 | tf_op jit(solution)/shard_map/all_to_all | solution.py:830
  446.7 16.9 %collective-permute-start.13 = (f32[32,2,8,128]{3,2,1,0:T(8,128)}, f32[32,2,8,128]{3,2,1,0:T(8,128)}, u32[]{:S(2)}, u32[]{:S(2)}) collective-permute-start(f32[32,2,8,128]{3,2,1,0:T(8,128)} %slice_bitcast_fusion.10), channel_id=1, source_target_pairs={{0,16},{4,20},{8,24},{12,28},{16,0},{20,4},{24,8},{28,12},{1,17},{... | collective-permute-start | bytes 786440 | tf_op jit(solution)/shard_map/ppermute | solution.py:709
  459.9 17.8 %all-to-all-start.6 = ((f32[4,64,512]{2,1,0:T(8,128)}), f32[4,64,512]{2,1,0:T(8,128)S(1)}, u32[]{:S(2)}, u32[]{:S(2)}) async-start(f32[4,64,512]{2,1,0:T(8,128)} %fusion.3), calls=%async_computation.6 | async-start | bytes 1048576 | tf_op jit(solution)/shard_map/all_to_all | solution.py:830
  467.7 11.4 %collective-permute-start.37 = (f32[1,2,8,4096]{3,2,1,0:T(8,128)S(1)}, f32[1,2,8,4096]{3,2,1,0:T(8,128)}, u32[]{:S(2)}, u32[]{:S(2)}) collective-permute-start(f32[1,2,8,4096]{3,2,1,0:T(8,128)S(1)} %slice.164), channel_id=1, source_target_pairs={{0,8},{4,12},{8,0},{12,4},{16,24},{20,28},{24,16},{28,20},{1,9},{5... | collective-permute-start | bytes 786440 | tf_op jit(solution)/shard_map/ppermute | solution.py:709
  471.5 11.5 %collective-permute-start.34 = (f32[1,2,8,4096]{3,2,1,0:T(8,128)S(1)}, f32[1,2,8,4096]{3,2,1,0:T(8,128)S(1)}, u32[]{:S(2)}, u32[]{:S(2)}) collective-permute-start(f32[1,2,8,4096]{3,2,1,0:T(8,128)S(1)} %slice.162), channel_id=1, source_target_pairs={{0,16},{4,20},{8,24},{12,28},{16,0},{20,4},{24,8},{28,12},{1,17},{... | collective-permute-start | bytes 786440 | tf_op jit(solution)/shard_map/ppermute | solution.py:709
  480.1 14.7 %collective-permute-start.38 = (f32[2,1,2,8,4096]{4,3,2,0,1:T(8,128)S(1)}, f32[2,1,2,8,4096]{4,3,2,0,1:T(8,128)S(1)}, u32[]{:S(2)}, u32[]{:S(2)}) collective-permute-start(f32[2,1,2,8,4096]{4,3,2,0,1:T(8,128)S(1)} %get-tuple-element.115), channel_id=1, source_target_pairs={{0,16},{4,20},{8,24},{12,28},{16,0},{20,4},{24,8},{28,12},{1,17},{... | collective-permute-start | bytes 1572872 | tf_op jit(solution)/shard_map/ppermute | solution.py:709
  483.1 16.2 %collective-permute-start.35 = (f32[2,1,2,8,4096]{4,3,2,0,1:T(8,128)S(1)}, f32[2,1,2,8,4096]{4,3,2,0,1:T(8,128)S(1)}, u32[]{:S(2)}, u32[]{:S(2)}) collective-permute-start(f32[2,1,2,8,4096]{4,3,2,0,1:T(8,128)S(1)} %get-tuple-element.113), channel_id=1, source_target_pairs={{0,8},{4,12},{8,0},{12,4},{16,24},{20,28},{24,16},{28,20},{1,9},{5... | collective-permute-start | bytes 1572872 | tf_op jit(solution)/shard_map/ppermute | solution.py:709
  496.0 19.4 %collective-permute-start.39 = (f32[2,2,1,2,8,4096]{5,4,3,1,0,2:T(8,128)}, f32[2,2,1,2,8,4096]{5,4,3,1,0,2:T(8,128)}, u32[]{:S(2)}, u32[]{:S(2)}) collective-permute-start(f32[2,2,1,2,8,4096]{5,4,3,1,0,2:T(8,128)} %get-tuple-element.107), channel_id=1, source_target_pairs={{0,4},{4,0},{8,12},{12,8},{16,20},{20,16},{24,28},{28,24},{1,5},{5... | collective-permute-start | bytes 3145736 | tf_op jit(solution)/shard_map/ppermute | solution.py:709
  500.5 16.3 %collective-permute-start.36 = (f32[2,2,1,2,8,4096]{5,4,3,1,0,2:T(8,128)}, f32[2,2,1,2,8,4096]{5,4,3,1,0,2:T(8,128)}, u32[]{:S(2)}, u32[]{:S(2)}) collective-permute-start(f32[2,2,1,2,8,4096]{5,4,3,1,0,2:T(8,128)} %get-tuple-element.103), channel_id=1, source_target_pairs={{0,4},{4,0},{8,12},{12,8},{16,20},{20,16},{24,28},{28,24},{1,5},{5... | collective-permute-start | bytes 3145736 | tf_op jit(solution)/shard_map/ppermute | solution.py:709
  (62 other events, 436.0 us)
Sparse Core Ops, SparseCore 0:
  28.7 40.7 all-gather.4

commit v2 on v1

v2 whole, which is shorter than its diff:
```python
from functools import partial
import math

import jax
import jax.numpy as jnp
from jax import lax
from jax.experimental import pallas as pl
from jax.experimental.pallas import tpu as pltpu
from jax.sharding import PartitionSpec as P

MODES = 64
SEQ_LEN = 128
HEAD_DIM = 64
STEP = 10
KERNEL_WIDTHS = (7, 12, 14, 24, 48)
KERNELS = len(KERNEL_WIDTHS)
BETA_ONE = 0.9
BETA_TWO = 0.999
LEARN_RATE = 0.05
EPSILON = 1e-08
DECAY = 0.01
CLIP_NORM = 0.02
LOG2E = math.log2(math.e)
LANES = 128
BF = jnp.bfloat16
F32 = jnp.float32
MIB = 1 << 20

ERF_P = 0.3275911
ERF_A = (0.254829592, -0.284496736, 1.421413741, -1.453152027, 1.061405429)


def dot(a, b, ca=1, cb=0):
    return lax.dot_general(a, b, (((ca,), (cb,)), ((), ())), preferred_element_type=F32)


def cost(microseconds, moved):
    return pl.CostEstimate(
        flops=int(microseconds * 1.1e9), bytes_accessed=int(moved), transcendentals=0
    )


def query_kernel(head_ref, x_ref, b_ref, *refs):
    heads = len(refs) // 2
    x = x_ref[...]
    for r in range(heads):
        bias = b_ref[lax.rem(head_ref[0] + r, heads)]
        refs[heads + r][...] = (dot(x, refs[r][...]) + bias).astype(BF)


def query_call(head, x, bias_row, weights):
    rows, d = x.shape
    heads = len(weights)
    width = weights[0].shape[1]
    step = min(256, rows)
    return pl.pallas_call(
        query_kernel,
        grid=(rows // step,),
        in_specs=[
            pl.BlockSpec(memory_space=pltpu.SMEM),
            pl.BlockSpec((step, d), lambda i: (i, 0)),
            pl.BlockSpec((heads, 1, width), lambda i: (0, 0, 0)),
        ]
        + [pl.BlockSpec((d, width), lambda i: (0, 0)) for _ in weights],
        out_specs=[pl.BlockSpec((step, width), lambda i: (i, 0)) for _ in weights],
        out_shape=[jax.ShapeDtypeStruct((rows, width), BF) for _ in weights],
        compiler_params=pltpu.CompilerParams(vmem_limit_bytes=24 * MIB),
        cost_estimate=cost(2.5, 3e6),
        name="queries",
    )(head, x, bias_row.reshape(heads, 1, width), *weights)


def lane_low(rows):
    return lax.broadcasted_iota(jnp.int32, (rows, LANES), 1) < HEAD_DIM


def mix_blocks(wt_ref, m, count):
    low = lane_low(HEAD_DIM)
    zero = jnp.zeros((HEAD_DIM, LANES), F32)
    left = [
        wt_ref[pl.ds(c * HEAD_DIM * MODES + m, HEAD_DIM, stride=MODES), :] for c in range(2)
    ]
    blocks = []
    for _ in range(count):
        terms = [v.astype(BF).astype(F32) for v in left]
        left = [v - t for v, t in zip(left, terms)]
        real, imag = (
            jnp.concatenate([jnp.where(low, t, zero), jnp.where(low, zero, t)], axis=0)
            for t in terms
        )
        top = jnp.concatenate([real, -imag], axis=1)
        bottom = jnp.concatenate([imag, real], axis=1)
        blocks.append(jnp.concatenate([top, bottom], axis=0).astype(BF))
    return blocks


def pair_width(contexts):
    return 2 if contexts % 2 == 0 else 1


def spectrum_kernel(wt_ref, tf_ref, ti_ref, *refs):
    owners = (len(refs) - 3) // 3
    q_refs, spec_refs = refs[:owners], refs[owners : 3 * owners]
    xs_ref, x_scr, y_scr = refs[3 * owners :]
    run, width = q_refs[0].shape[0], q_refs[0].shape[2]
    half = run // 2
    contexts = owners * run
    pair = pair_width(half)
    low = lane_low(SEQ_LEN)

    for r in range(owners):

        def forward(p, _, r=r):
            cols = jnp.concatenate([q_refs[r][p * pair + k] for k in range(pair)], axis=1)
            res = dot(tf_ref[...], jnp.concatenate([cols, cols], axis=0))
            for k in range(pair):
                part = res[:, k * LANES : (k + 1) * LANES]
                row = (r * run + p * pair + k) * SEQ_LEN
                x_scr[pl.ds(pl.multiple_of(row, SEQ_LEN), SEQ_LEN), :] = jnp.where(
                    low, part[:SEQ_LEN], part[SEQ_LEN:]
                )
            return 0

        lax.fori_loop(0, run // pair, forward, 0)

    def mix(m, _):
        xr = x_scr[pl.ds(m, contexts, stride=SEQ_LEN), :].astype(BF)
        xi = x_scr[pl.ds(MODES + m, contexts, stride=SEQ_LEN), :].astype(BF)
        xs_ref[m] = jnp.concatenate([xr, xi], axis=0)
        x = jnp.concatenate([xr, xi], axis=1)
        main, rest = mix_blocks(wt_ref, m, 2)
        y = dot(x, main, 1, 1) + dot(x, rest, 1, 1)
        y_scr[pl.ds(m, contexts, stride=SEQ_LEN), :] = y[:, :LANES]
        y_scr[pl.ds(MODES + m, contexts, stride=SEQ_LEN), :] = y[:, LANES:]
        return 0

    lax.fori_loop(0, MODES, mix, 0, unroll=4)

    for r in range(owners):
        for number in range(2):
            target = spec_refs[number * owners + r]

            def inverse(p, _, r=r, number=number, target=target):
                parts = []
                for k in range(pair):
                    row = (r * run + number * half + p * pair + k) * SEQ_LEN
                    parts.append(y_scr[pl.ds(pl.multiple_of(row, SEQ_LEN), SEQ_LEN), :])
                cols = jnp.concatenate(parts, axis=1)
                main = cols.astype(BF)
                rest = (cols - main.astype(F32)).astype(BF)
                res = dot(ti_ref[...], jnp.concatenate([main, main, rest], axis=0)).astype(BF)
                for k in range(pair):
                    target[p * pair + k] = res[:, k * LANES : (k + 1) * LANES]
                return 0

            lax.fori_loop(0, half // pair, inverse, 0)


def spectrum_call(queries, wt, tf, ti):
    owners = len(queries)
    run = queries[0].shape[0]
    contexts = owners * run
    out = jax.ShapeDtypeStruct((run // 2, SEQ_LEN, LANES), BF)
    res = pl.pallas_call(
        spectrum_kernel,
        out_shape=[out] * (2 * owners)
        + [jax.ShapeDtypeStruct((MODES, 2 * contexts, LANES), BF)],
        scratch_shapes=[
            pltpu.VMEM((contexts * SEQ_LEN, LANES), F32),
            pltpu.VMEM((contexts * SEQ_LEN, LANES), F32),
        ],
        compiler_params=pltpu.CompilerParams(vmem_limit_bytes=32 * MIB),
        cost_estimate=cost(15, 7e6),
        name="spectrum",
    )(wt, tf, ti, *queries)
    return res[:owners], res[owners : 2 * owners], res[2 * owners]


def query_grad_kernel(wt_ref, tit_ref, tft_ref, *refs):
    owners = (len(refs) - 4) // 3
    d_refs, dq_refs = refs[: 2 * owners], refs[2 * owners : 3 * owners]
    dy_ref, bias_ref, y_scr, x_scr = refs[3 * owners :]
    half = d_refs[0].shape[0]
    run = 2 * half
    contexts = owners * run
    pair = pair_width(half)
    low = lane_low(SEQ_LEN)
    zero = jnp.zeros((SEQ_LEN, LANES), F32)

    for number in range(2):
        for r in range(owners):
            source = d_refs[number * owners + r]

            def forward(p, _, number=number, r=r, source=source):
                cols = jnp.concatenate([source[p * pair + k] for k in range(pair)], axis=1)
                res = dot(tit_ref[...], jnp.concatenate([cols, cols], axis=0))
                for k in range(pair):
                    row = (r * run + number * half + p * pair + k) * SEQ_LEN
                    y_scr[pl.ds(pl.multiple_of(row, SEQ_LEN), SEQ_LEN), :] = res[
                        :, k * LANES : (k + 1) * LANES
                    ]
                return 0

            lax.fori_loop(0, half // pair, forward, 0)

    def mix(m, _):
        yr = y_scr[pl.ds(m, contexts, stride=SEQ_LEN), :].astype(BF)
        yi = y_scr[pl.ds(MODES + m, contexts, stride=SEQ_LEN), :].astype(BF)
        dy = jnp.concatenate([yr, yi], axis=1)
        dy_ref[m] = dy
        dx = dot(dy, mix_blocks(wt_ref, m, 1)[0])
        x_scr[pl.ds(m, contexts, stride=SEQ_LEN), :] = dx[:, :LANES]
        x_scr[pl.ds(MODES + m, contexts, stride=SEQ_LEN), :] = dx[:, LANES:]
        return 0

    lax.fori_loop(0, MODES, mix, 0, unroll=4)
    bias_ref[...] = jnp.zeros_like(bias_ref)

    for r in range(owners):

        def inverse(p, _, r=r):
            parts = []
            for k in range(pair):
                row = (r * run + p * pair + k) * SEQ_LEN
                one = x_scr[pl.ds(pl.multiple_of(row, SEQ_LEN), SEQ_LEN), :]
                parts.append(
                    jnp.concatenate([jnp.where(low, one, zero), jnp.where(low, zero, one)], axis=0)
                )
            cols = jnp.concatenate(parts, axis=1).astype(BF)
            res = dot(tft_ref[...], jnp.concatenate([cols, cols], axis=0)).astype(BF)
            total = jnp.zeros((8, LANES), F32)
            for k in range(pair):
                one = res[:, k * LANES : (k + 1) * LANES]
                dq_refs[r][p * pair + k] = one
                total = total + jnp.sum(one.astype(F32).reshape(SEQ_LEN // 8, 8, LANES), axis=0)
            bias_ref[...] += total
            return 0

        lax.fori_loop(0, run // pair, inverse, 0)


def query_grad_call(first, second, wt, tit, tft, waits):
    owners = len(first)
    run = 2 * first[0].shape[0]
    contexts = owners * run
    whole = pl.BlockSpec(memory_space=pltpu.VMEM)

    def body(*refs):
        at = 3 + 2 * owners
        query_grad_kernel(*refs[:at], *refs[at + len(waits) :])

    res = pl.pallas_call(
        body,
        in_specs=[whole] * (3 + 2 * owners) + [pl.BlockSpec(memory_space=pl.ANY)] * len(waits),
        out_shape=[jax.ShapeDtypeStruct((run, SEQ_LEN, LANES), BF)] * owners
        + [
            jax.ShapeDtypeStruct((MODES, contexts, 2 * LANES), BF),
            jax.ShapeDtypeStruct((8, LANES), F32),
        ],
        scratch_shapes=[
            pltpu.VMEM((contexts * SEQ_LEN, LANES), F32),
            pltpu.VMEM((contexts * SEQ_LEN, LANES), F32),
        ],
        compiler_params=pltpu.CompilerParams(vmem_limit_bytes=32 * MIB),
        cost_estimate=cost(11, 7e6),
        name="query_grads",
    )(wt, tit, tft, *first, *second, *waits)
    return res[:owners], res[owners], res[owners + 1]


def mode_grad_kernel(me_ref, dy_ref, xs_ref, *refs):
    outs = refs[:4]
    dw_scr, sems = refs[4:]
    pieces, depth = 2 * outs[0].shape[0], outs[0].shape[1]
    total = HEAD_DIM * MODES
    low = lane_low(HEAD_DIM)
    me = me_ref[0]

    def mix(m, _):
        dy = dy_ref[m]
        yr, yi = dy[:, :LANES], dy[:, LANES:]
        right = jnp.concatenate(
            [jnp.concatenate([yr, yi], axis=0), jnp.concatenate([yi, -yr], axis=0)], axis=1
        )
        dw = dot(right, xs_ref[m], 0, 0)
        for c in range(2):
            first = 2 * c * HEAD_DIM
            part = jnp.where(
                low, dw[first : first + HEAD_DIM], dw[first + HEAD_DIM : first + 2 * HEAD_DIM]
            )
            dw_scr[pl.ds(c * total + m, HEAD_DIM, stride=MODES), :] = part
        return 0

    lax.fori_loop(0, MODES, mix, 0, unroll=4)
    copies = []
    for j in range(pieces):
        for c in range(2):
            start = pl.multiple_of(c * total + (me ^ j) * depth, depth)
            copies.append(
                pltpu.make_async_copy(
                    dw_scr.at[pl.ds(start, depth), :],
                    outs[2 * c + (j + 1) % 2].at[j // 2],
                    sems.at[c, j],
                )
            )
    for copy in copies:
        copy.start()
    for copy in copies:
        copy.wait()


def mode_grad_call(me, dy, xs, pieces):
    part = jax.ShapeDtypeStruct((pieces // 2, HEAD_DIM * MODES // pieces, LANES), F32)
    whole = pl.BlockSpec(memory_space=pltpu.VMEM)
    return pl.pallas_call(
        mode_grad_kernel,
        in_specs=[pl.BlockSpec(memory_space=pltpu.SMEM)] + [whole] * 2,
        out_specs=[pl.BlockSpec(memory_space=pl.ANY)] * 4,
        out_shape=[part] * 4,
        scratch_shapes=[
            pltpu.VMEM((2 * HEAD_DIM * MODES, LANES), F32),
            pltpu.SemaphoreType.DMA((2, pieces)),
        ],
        compiler_params=pltpu.CompilerParams(vmem_limit_bytes=40 * MIB),
        cost_estimate=cost(9, 8e6),
        name="mode_grads",
    )(me, dy, xs)


SUM_SLOPE = (0, 10)
SUM_OFFSET = (5, 15)
SUM_LOSS = 20
SUM_BIAS = 21
SUM_ROWS = 24


def window_counts(first, last, rows, cols, width):
    lead = width - 1 - (width - 1) // 2
    reach = cols - rows + (lead + 1)
    here = jnp.where(cols < first, 0, jnp.where(cols >= last, width, jnp.clip(reach, 0, width)))
    before = jnp.where(
        cols <= first, 0, jnp.where(cols > last, width, jnp.clip(reach - 1, 0, width))
    )
    return (here - before).astype(F32)


def window_edges(starts, rows):
    s1, s2, s3 = starts
    first = jnp.where(rows >= s3, s3, jnp.where(rows >= s2, s2, jnp.where(rows >= s1, s1, 0)))
    last = jnp.where(
        rows < s1, s1 - 1, jnp.where(rows < s2, s2 - 1, jnp.where(rows < s3, s3 - 1, SEQ_LEN - 1))
    )
    return first, last


def fold(v):
    return jnp.sum(v.reshape(v.shape[0] // 8, 8, v.shape[1]), axis=0)


def local_kernel(*refs, chunk, hidden_width, heads, waits):
    refs = list(refs)

    def take(n):
        taken = refs[:n]
        del refs[:n]
        return taken

    starts_ref, prm_ref, me_ref, x_ref, tgt_ref, val_ref, bias_ref = take(7)
    spec_refs = take(heads)
    packed_refs = take(4)
    take(waits)
    dspec_refs = take(heads)
    act_ref, dhid_ref, low_ref, dfeed_ref, spec_out, dattn_ref, sums_ref = take(7)
    (
        u_scr,
        trend_scr,
        season_scr,
        av1_scr,
        share_scr,
        av2_scr,
        da_scr,
        part_scr,
        g_scr,
        slope_scr,
        a_scr,
        at_scr,
        weights,
        weight_sems,
    ) = refs
    step = pl.program_id(0)
    rows, d = x_ref.shape
    nctx = rows // SEQ_LEN
    out_width = dspec_refs[0].shape[1]
    up_rows = slice(0, hidden_width)
    down_rows = slice(hidden_width, 2 * hidden_width)
    out_rows = slice(2 * hidden_width, 2 * hidden_width + out_width)
    groups = d // LANES
    loops = SEQ_LEN // chunk

    @pl.when(step == 0)
    def _():
        count, shared, part, _ = packed_refs[0].shape
        copies = []
        for number, ref in enumerate(packed_refs):
            group, bit = number // 2, number % 2
            for k in range(count):
                for r in range(shared):
                    row = pl.multiple_of((me_ref[0] ^ (2 * k + bit)) * part, part)
                    copies.append(
                        pltpu.make_async_copy(
                            ref.at[k, r],
                            weights.at[(heads - group * shared - r) % heads, pl.ds(row, part), :],
                            weight_sems.at[number, k * shared + r],
                        )
                    )
        for copy in copies:
            copy.start()
        sums_ref[...] = jnp.zeros_like(sums_ref)
        for copy in copies:
            copy.wait()

    row_ids = lax.broadcasted_iota(jnp.int32, (SEQ_LEN, SEQ_LEN), 0)
    col_ids = lax.broadcasted_iota(jnp.int32, (SEQ_LEN, SEQ_LEN), 1)
    for c in range(nctx):
        starts = [starts_ref[step * nctx + c, k] for k in range(1, 4)]
        first, last = window_edges(starts, row_ids)
        first_t, last_t = window_edges(starts, col_ids)
        for w, width in enumerate(KERNEL_WIDTHS):
            counts = window_counts(first, last, row_ids, col_ids, width).astype(BF)
            a_scr[c, w * SEQ_LEN : (w + 1) * SEQ_LEN, :SEQ_LEN] = counts
            a_scr[c, w * SEQ_LEN : (w + 1) * SEQ_LEN, SEQ_LEN:] = counts
            at_scr[c, :, w * SEQ_LEN : (w + 1) * SEQ_LEN] = window_counts(
                first_t, last_t, col_ids, row_ids, width
            ).astype(BF)

    def averages(c, u, av):
        high = u.astype(BF)
        rest = (u - high.astype(F32)).astype(BF)
        av[c] = dot(a_scr[c], jnp.concatenate([high, rest], axis=0))

    spec = jnp.concatenate([ref[...] for ref in spec_refs], axis=1)
    for h in range(heads):
        spec_out[h] = spec_refs[h][...]
    out_all = jnp.concatenate([weights[h, out_rows] for h in range(heads)], axis=0)
    pre = x_ref[...].astype(F32) + (dot(spec, out_all) + bias_ref[...])
    u_scr[...] = pre
    for c in range(nctx):
        averages(c, pre[c * SEQ_LEN : (c + 1) * SEQ_LEN], av1_scr)

    def shares_of(u, avs, layer):
        logits = [
            u * (prm_ref[layer, 0, w] * LOG2E) + prm_ref[layer, 1, w] * LOG2E
            for w in range(KERNELS)
        ]
        top = logits[0]
        for v in logits[1:]:
            top = jnp.maximum(top, v)
        powers = [jnp.exp2(v - top) for v in logits]
        total = powers[0]
        for v in powers[1:]:
            total = total + v
        scale = 1.0 / total
        shares = [v * scale for v in powers]
        trend = shares[0] * avs[0]
        for s, a in zip(shares[1:], avs[1:]):
            trend = trend + s * a
        return shares, trend

    def read_averages(av, c, row, lanes):
        return [
            av[c, pl.ds(w * SEQ_LEN + row, chunk), lanes] * (1.0 / width)
            for w, width in enumerate(KERNEL_WIDTHS)
        ]

    def pull(shares, avs, trend, grad, u, layer, base, c, row, lanes, sums):
        rest = base
        slopes, offsets = [], []
        for w, width in enumerate(KERNEL_WIDTHS):
            d_avg = shares[w] * grad
            da_scr[c, pl.ds(w * SEQ_LEN + row, chunk), lanes] = (d_avg * (1.0 / width)).astype(BF)
            d_logit = d_avg * (avs[w] - trend)
            rest = rest + d_logit * prm_ref[layer, 0, w]
            slopes.append(sums[w] + fold(d_logit * u))
            offsets.append(sums[KERNELS + w] + fold(d_logit))
        return rest, slopes + offsets

    for c in range(nctx):
        for g in range(groups):
            lanes = slice(g * LANES, (g + 1) * LANES)

            def first_pass(r, _, c=c, lanes=lanes):
                row = pl.multiple_of(r * chunk, chunk)
                at = pl.ds(c * SEQ_LEN + row, chunk)
                u = u_scr[at, lanes]
                avs = read_averages(av1_scr, c, row, lanes)
                shares, trend = shares_of(u, avs, 0)
                for w in range(KERNELS):
                    share_scr[c, pl.ds(w * SEQ_LEN + row, chunk), lanes] = shares[w]
                season = u - trend
                trend_scr[at, lanes] = trend
                season_scr[at, lanes] = season
                low_ref[at, lanes] = season.astype(BF)
                return 0

            lax.fori_loop(0, loops, first_pass, 0)

    season_low = low_ref[...]
    feed = jnp.zeros((rows, d), F32)
    for h in range(heads):
        hid = dot(season_low, weights[h, up_rows], 1, 1)
        z = jnp.abs(hid) * (2.0**-0.5)
        t = 1.0 / (1.0 + ERF_P * z)
        e = jnp.exp2(hid * hid * (-0.5 * LOG2E))
        poly = ERF_A[4]
        for coef in ERF_A[3::-1]:
            poly = poly * t + coef
        tail = (0.5 * t) * poly * e
        phi = jnp.where(hid < 0, tail, 1.0 - tail)
        active = (hid * phi).astype(BF)
        slope_scr[h] = phi + hid * e * ((2.0 * math.pi) ** -0.5)
        act_ref[h] = active
        feed = feed + dot(active, weights[h, down_rows])

    pre = season_scr[...] + feed
    g_scr[...] = pre
    for c in range(nctx):
        averages(c, pre[c * SEQ_LEN : (c + 1) * SEQ_LEN], av2_scr)

    for c in range(nctx):
        for g in range(groups):
            lanes = slice(g * LANES, (g + 1) * LANES)

            def second_pass(r, sums, c=c, lanes=lanes):
                row = pl.multiple_of(r * chunk, chunk)
                at = pl.ds(c * SEQ_LEN + row, chunk)
                u = g_scr[at, lanes]
                avs = read_averages(av2_scr, c, row, lanes)
                shares, trend = shares_of(u, avs, 1)
                misfit = trend_scr[at, lanes] + trend - tgt_ref[at, lanes]
                weighted = val_ref[at, :] * misfit
                grad = 2.0 * weighted
                rest, new = pull(
                    shares, avs, trend, grad, u, 1, jnp.zeros_like(u), c, row, lanes, sums
                )
                part_scr[at, lanes] = rest
                g_scr[at, lanes] = grad
                return tuple(new) + (sums[2 * KERNELS] + fold(weighted * misfit),)

            zeros = tuple(jnp.zeros((8, LANES), F32) for _ in range(2 * KERNELS + 1))
            sums = lax.fori_loop(0, loops, second_pass, zeros)
            for k in range(KERNELS):
                sums_ref[SUM_SLOPE[1] + k, :, lanes] += sums[k]
                sums_ref[SUM_OFFSET[1] + k, :, lanes] += sums[KERNELS + k]
            sums_ref[SUM_LOSS, :, lanes] += sums[2 * KERNELS]

    for c in range(nctx):
        at = slice(c * SEQ_LEN, (c + 1) * SEQ_LEN)
        part_scr[at, :] += dot(at_scr[c], da_scr[c])

    d_pre = part_scr[...]
    d_feed = d_pre.astype(BF)
    dfeed_ref[...] = d_feed
    back = d_pre
    for h in range(heads):
        d_hid = (dot(d_feed, weights[h, down_rows], 1, 1) * slope_scr[h]).astype(BF)
        back = back + dot(d_hid, weights[h, up_rows])
        dhid_ref[h] = d_hid
    season_scr[...] = back

    for c in range(nctx):
        for g in range(groups):
            lanes = slice(g * LANES, (g + 1) * LANES)

            def third_pass(r, sums, c=c, lanes=lanes):
                row = pl.multiple_of(r * chunk, chunk)
                at = pl.ds(c * SEQ_LEN + row, chunk)
                u = u_scr[at, lanes]
                avs = read_averages(av1_scr, c, row, lanes)
                shares = [
                    share_scr[c, pl.ds(w * SEQ_LEN + row, chunk), lanes] for w in range(KERNELS)
                ]
                d_season = season_scr[at, lanes]
                rest, new = pull(
                    shares,
                    avs,
                    trend_scr[at, lanes],
                    g_scr[at, lanes] - d_season,
                    u,
                    0,
                    d_season,
                    c,
                    row,
                    lanes,
                    sums,
                )
                part_scr[at, lanes] = rest
                return tuple(new)

            zeros = tuple(jnp.zeros((8, LANES), F32) for _ in range(2 * KERNELS))
            sums = lax.fori_loop(0, loops, third_pass, zeros)
            for k in range(KERNELS):
                sums_ref[SUM_SLOPE[0] + k, :, lanes] += sums[k]
                sums_ref[SUM_OFFSET[0] + k, :, lanes] += sums[KERNELS + k]

    for c in range(nctx):
        at = slice(c * SEQ_LEN, (c + 1) * SEQ_LEN)
        part_scr[at, :] += dot(at_scr[c], da_scr[c])

    d_pre = part_scr[...]
    sums_ref[SUM_BIAS] += fold(d_pre)
    d_attn = d_pre.astype(BF)
    dattn_ref[...] = d_attn
    d_spec = dot(d_attn, out_all, 1, 1).astype(BF)
    for h in range(heads):
        dspec_refs[h][...] = d_spec[:, h * out_width : (h + 1) * out_width]


def up8(n):
    return -(-n // 8) * 8


def local_call(number, spec, waits, starts, prm, me, x, target, valid, bias, packed, hidden):
    rows_half = x.shape[0] // 2
    d = x.shape[1]
    heads = len(spec)
    width = spec[0].shape[1]
    nctx = 2 if rows_half % (2 * SEQ_LEN) == 0 else 1
    rows = nctx * SEQ_LEN
    steps = rows_half // rows
    smem = pl.BlockSpec(memory_space=pltpu.SMEM)
    whole = pl.BlockSpec(memory_space=pltpu.VMEM)
    anywhere = pl.BlockSpec(memory_space=pl.ANY)
    averages = (nctx, KERNELS * SEQ_LEN, d)
    count, shared, part, _ = packed[0].shape

    def row_block(columns, half=0):
        return pl.BlockSpec((rows, columns), lambda i: (half * steps + i, 0))

    def head_block(columns):
        return pl.BlockSpec((heads, rows, columns), lambda i: (0, i, 0))

    ctx_half = starts.shape[0] // 2
    res = pl.pallas_call(
        partial(local_kernel, chunk=16, hidden_width=hidden, heads=heads, waits=len(waits)),
        grid=(steps,),
        in_specs=[smem] * 3
        + [row_block(d, number), row_block(d, number), row_block(1, number), whole]
        + [row_block(width)] * heads
        + [anywhere] * (len(packed) + len(waits)),
        out_specs=[row_block(width)] * heads
        + [head_block(hidden), head_block(hidden), row_block(d), row_block(d)]
        + [head_block(width), row_block(d)]
        + [pl.BlockSpec((SUM_ROWS, 8, d), lambda i: (0, 0, 0))],
        out_shape=[jax.ShapeDtypeStruct((rows_half, width), BF)] * heads
        + [jax.ShapeDtypeStruct((heads, rows_half, hidden), BF)] * 2
        + [jax.ShapeDtypeStruct((rows_half, d), BF)] * 2
        + [
            jax.ShapeDtypeStruct((heads, rows_half, width), BF),
            jax.ShapeDtypeStruct((rows_half, d), BF),
            jax.ShapeDtypeStruct((SUM_ROWS, 8, d), F32),
        ],
        scratch_shapes=[
            pltpu.VMEM((rows, d), F32),
            pltpu.VMEM((rows, d), F32),
            pltpu.VMEM((rows, d), F32),
            pltpu.VMEM(averages, F32),
            pltpu.VMEM(averages, F32),
            pltpu.VMEM(averages, F32),
            pltpu.VMEM(averages, BF),
            pltpu.VMEM((rows, d), F32),
            pltpu.VMEM((rows, d), F32),
            pltpu.VMEM((heads, rows, hidden), F32),
            pltpu.VMEM((nctx, KERNELS * SEQ_LEN, 2 * SEQ_LEN), BF),
            pltpu.VMEM((nctx, SEQ_LEN, KERNELS * SEQ_LEN), BF),
            pltpu.VMEM((heads, len(packed) * count // 2 * part, d), BF),
            pltpu.SemaphoreType.DMA((len(packed), count * shared)),
        ],
        compiler_params=pltpu.CompilerParams(vmem_limit_bytes=56 * MIB),
        cost_estimate=cost(38, 24e6),
        name="local_layer",
    )(
        starts[number * ctx_half : (number + 1) * ctx_half],
        prm,
        me,
        x,
        target,
        valid,
        bias,
        *spec,
        *packed,
        *waits,
    )
    return res[:heads], res[heads:-1], res[-1]


def outer_kernel(me_ref, *refs, halves, outs, waits):
    count = len(halves)
    scratch = refs[-1]
    ins = refs[: 2 * sum(halves)]
    targets = refs[2 * sum(halves) + waits : -1]
    for k in range(count):
        total = None
        for n in range(halves[k]):
            left, right = ins[2 * (sum(halves[:k]) + n) : 2 * (sum(halves[:k]) + n) + 2]
            left = left[0] if len(left.shape) == 3 else left[...]
            right = right[0] if len(right.shape) == 3 else right[...]
            term = dot(left, right, 0, 0)
            total = term if total is None else total + term
        where, offset = outs[k]
        send, keep = targets[2 * where : 2 * where + 2]
        pieces = 2 * send.shape[0]
        size = total.shape[0] // pieces
        lanes = slice(0, total.shape[1])
        if size % 8 == 0:
            scratch[: total.shape[0], lanes] = total
            for j in range(pieces):
                row = pl.multiple_of((me_ref[0] ^ j) * size, size)
                (send if j % 2 else keep)[j // 2, 0, offset : offset + size, :] = scratch[
                    pl.ds(row, size), lanes
                ]
        else:
            scratch[: total.shape[0], lanes] = total
            for j in range(pieces):
                (send if j % 2 else keep)[j // 2, 0, offset:, :] = jnp.zeros(
                    (send.shape[2] - offset, total.shape[1]), F32
                )
                for i in range(size):
                    (send if j % 2 else keep)[j // 2, 0, offset + i : offset + i + 1, :] = scratch[
                        pl.ds((me_ref[0] ^ j) * size + i, 1), lanes
                    ]


def outer_call(me, products, shapes, outs, pieces, name, waits=()):
    heads = next(a.shape[0] for p in products for pair in p for a in pair if a.ndim == 3)
    operands = [a for p in products for pair in p for a in pair]

    def spec(a):
        if a.ndim == 3:
            return pl.BlockSpec((1,) + a.shape[1:], lambda h: (h, 0, 0))
        return pl.BlockSpec(a.shape, lambda h: (0, 0))

    out_specs = [
        pl.BlockSpec((pieces // 2, 1) + shape, lambda h: (0, h, 0, 0))
        for shape in shapes
        for _ in range(2)
    ]
    rows = max(pair[0].shape[-1] for p in products for pair in p)
    columns = max(pair[1].shape[-1] for p in products for pair in p)
    return pl.pallas_call(
        partial(outer_kernel, halves=[len(p) for p in products], outs=outs, waits=len(waits)),
        grid=(heads,),
        in_specs=[pl.BlockSpec(memory_space=pltpu.SMEM)]
        + [spec(a) for a in operands]
        + [pl.BlockSpec(memory_space=pl.ANY)] * len(waits),
        out_specs=out_specs,
        out_shape=[
            jax.ShapeDtypeStruct((pieces // 2, heads) + shape, F32)
            for shape in shapes
            for _ in range(2)
        ],
        scratch_shapes=[pltpu.VMEM((rows, columns), F32)],
        compiler_params=pltpu.CompilerParams(vmem_limit_bytes=48 * MIB),
        cost_estimate=cost(8, 20e6),
        name=name,
    )(me, *operands, *waits)


def adam_values(weight, gradient, first, second):
    m = BETA_ONE * first + (1.0 - BETA_ONE) * gradient
    v = BETA_TWO * second + (1.0 - BETA_TWO) * gradient * gradient
    first_hat = m * (1.0 / (1.0 - BETA_ONE**STEP))
    second_hat = v * (1.0 / (1.0 - BETA_TWO**STEP))
    return (
        weight - LEARN_RATE * (first_hat / (jnp.sqrt(second_hat) + EPSILON) + DECAY * weight),
        m,
        v,
    )


def adam_kernel(me_ref, scale_ref, *refs, views, leads, grads):
    scale = scale_ref[0]
    count = len(views)
    pairs = refs[: 2 * grads]
    states = refs[2 * grads : 2 * grads + 3 * count]
    outs = refs[2 * grads + 3 * count : 2 * grads + 6 * count]
    chosen = refs[2 * grads + 6 * count :]
    other = (pl.program_id(0) ^ me_ref[0]) & 1

    @pl.when(other == 0)
    def _():
        for k in range(grads):
            chosen[k][...] = pairs[2 * k][0]

    @pl.when(other == 1)
    def _():
        for k in range(grads):
            chosen[k][...] = pairs[2 * k + 1][0]

    for k, parts in enumerate(views):
        lead = leads[k]
        for which, source, place in parts:
            ins = [r.at[lead][place] for r in states[3 * k : 3 * k + 3]]
            g = chosen[which][source] * scale
            new = adam_values(ins[0], g, ins[1], ins[2])
            for r, value in zip(outs[3 * k : 3 * k + 3], new):
                r.at[lead][place] = value


def adam_call(me, scale, grads, views, states, axes):
    pieces = 2 * grads[0][0].shape[0]
    specs, out_specs, operands, shapes, leads = [], [], [], [], []
    for pair in grads:
        zeros = (0,) * (pair[0].ndim - 1)
        for grad in pair:
            specs.append(
                pl.BlockSpec(
                    (1,) + grad.shape[1:],
                    lambda i, me_ref, z=zeros: (lax.div(i ^ me_ref[0], 2),) + z,
                )
            )
            operands.append(grad)
    for group, axis in zip(states, axes):
        shape = group[0].shape
        size = shape[axis] // pieces
        direct = size % (LANES if axis == len(shape) - 1 else 8) == 0
        if not direct:
            shape = shape[:axis] + (pieces, size) + shape[axis + 1 :]
        block = shape[:axis] + (size if direct else 1,) + shape[axis + 1 :]
        leads.append((slice(None),) * axis + ((slice(None),) if direct else (0,)))
        for state in group:
            spec = pl.BlockSpec(
                block,
                lambda i, me_ref, a=axis, n=len(shape): (0,) * a + (i,) + (0,) * (n - a - 1),
            )
            specs.append(spec)
            out_specs.append(spec)
            operands.append(state.reshape(shape))
            shapes.append(jax.ShapeDtypeStruct(shape, F32))
    news = pl.pallas_call(
        partial(adam_kernel, views=views, leads=leads, grads=len(grads)),
        grid_spec=pltpu.PrefetchScalarGridSpec(
            num_scalar_prefetch=1,
            grid=(pieces,),
            in_specs=[pl.BlockSpec(memory_space=pltpu.SMEM)] + specs,
            out_specs=out_specs,
            scratch_shapes=[pltpu.VMEM(pair[0].shape[1:], F32) for pair in grads],
        ),
        out_shape=shapes,
        compiler_params=pltpu.CompilerParams(vmem_limit_bytes=48 * MIB),
        cost_estimate=cost(15, 48e6),
        name="adam",
    )(me, scale, *operands)
    return [n.reshape(states[k // 3][0].shape) for k, n in enumerate(news)]


def swap(value, axis, size, bit):
    return lax.ppermute(value, axis, [(i, i ^ (1 << bit)) for i in range(size)])


def split_add(items):
    specs, operands, shapes, out_specs = [], [], [], []
    half = items[0][0].shape[0] // 2
    heads = items[0][0].shape[1]
    for kept, got, lowest in items:
        block = (1, 1) + kept.shape[2:]
        away = (lambda i, h: (2 * i + 1, h, 0, 0)) if lowest else (lambda i, h: (half + i, h, 0, 0))
        stay = (lambda i, h: (2 * i, h, 0, 0)) if lowest else (lambda i, h: (i, h, 0, 0))
        for index in (away, stay):
            specs += [pl.BlockSpec(block, index)] * 2
            operands += [kept, got]
            out_specs.append(pl.BlockSpec(block, lambda i, h: (i, h, 0, 0)))
            shapes.append(jax.ShapeDtypeStruct((half,) + kept.shape[1:], F32))

    def body(*refs):
        outs = refs[len(operands) :]
        for k, out in enumerate(outs):
            out[...] = refs[2 * k][...] + refs[2 * k + 1][...]

    res = pl.pallas_call(
        body,
        grid=(half, heads),
        in_specs=specs,
        out_specs=out_specs,
        out_shape=shapes,
        compiler_params=pltpu.CompilerParams(vmem_limit_bytes=24 * MIB),
        cost_estimate=cost(3, 12e6),
        name="split_add",
    )(*operands)
    return [(res[2 * k], res[2 * k + 1]) for k in range(len(items))]


class Reduction:
    def __init__(self, pairs, orders, size):
        self.size = size
        self.orders = [list(order) for order in orders]
        self.lowest = [order == sorted(order) for order in orders]
        self.kept = [keep for _, keep in pairs]
        self.got = [swap(send, "dp", size, 0) for send, _ in pairs]

    def split(self):
        items = list(zip(self.kept, self.got, self.lowest))
        pairs = split_add(items)
        self.kept = [keep for _, keep in pairs]
        self.got = [
            swap(send, "dp", self.size, order.pop(0))
            for (send, _), order in zip(pairs, self.orders)
        ]

    def rest(self):
        while self.orders[0]:
            self.split()
        return [keep[0] + got[0] for keep, got in zip(self.kept, self.got)]


def gather_pieces(piece, size, order):
    have = []
    now = piece
    for bit in order:
        at = len([b for b in have if b > bit])
        now = jnp.stack([now, swap(now, "dp", size, bit)], axis=at)
        have = sorted(have + [bit], reverse=True)
    now = now.reshape((size // 2,) + piece.shape)
    return now, swap(now, "dp", size, 0)


def sum_everywhere(value, sizes):
    for axis, size in sizes:
        for bit in range(size.bit_length() - 1):
            value = value + swap(value, axis, size, bit)
    return value


def split_low(table):
    high = lax.reduce_precision(table, 8, 7)
    return high.astype(BF), (table - high).astype(BF)


def spectral_tables(mode_index):
    heads = mode_index.shape[0]
    steps = jnp.arange(SEQ_LEN, dtype=jnp.int32)
    angles = (mode_index[:, :, None] * steps % SEQ_LEN).astype(F32) * (2.0 * math.pi / SEQ_LEN)
    ahead = jnp.concatenate([jnp.cos(angles), -jnp.sin(angles)], axis=1)
    if heads == 1:
        ahead = jnp.concatenate([ahead, jnp.zeros_like(ahead)], axis=0)
    ahead = ahead.reshape(2 * SEQ_LEN, SEQ_LEN)
    orders = jnp.arange(MODES, dtype=jnp.int32)
    angles = (steps[:, None] * orders % SEQ_LEN).astype(F32) * (2.0 * math.pi / SEQ_LEN)
    weights = jnp.where(orders == 0, 1.0, 2.0).astype(F32) / SEQ_LEN
    back = jnp.concatenate([jnp.cos(angles) * weights, -jnp.sin(angles) * weights], axis=1)
    tables = [jnp.concatenate(split_low(t), axis=1) for t in (ahead, back, back.T, ahead.T)]
    tables[1] = jnp.concatenate([tables[1], tables[1][:, :SEQ_LEN]], axis=1)
    return tables


def on_device(
    sizes,
    series,
    target,
    valid,
    window_id,
    mode_index,
    query_weight,
    query_first,
    query_second,
    out_weight,
    out_first,
    out_second,
    mode_weight,
    mode_first,
    mode_second,
    up_weight,
    up_first,
    up_second,
    down_weight,
    down_first,
    down_second,
    bias_pair,
    bias_first,
    bias_second,
    decomp_params,
    decomp_first,
    decomp_second,
):
    ndp, nhead = sizes
    bits = ndp.bit_length() - 1
    order_a = list(range(1, bits))
    order_b = order_a[::-1]
    dp = lax.axis_index("dp")
    head = lax.axis_index("head")
    me = dp.astype(jnp.int32).reshape(1)
    rows, d = series.shape
    own_heads = mode_index.shape[0]
    width = query_weight.shape[1]
    hidden = up_weight.shape[1]

    everyone = (("dp", ndp), ("head", nhead))
    place = jnp.concatenate([me, head.astype(jnp.int32).reshape(1)])

    def shift(v, r):
        return lax.ppermute(v, "head", [(i, (i + r) % nhead) for i in range(nhead)])

    def exchange(v):
        return lax.all_to_all(v, "head", 0, 0, tiled=True)

    def wide(v):
        pad = LANES - v.shape[-1]
        return jnp.pad(v, [(0, 0)] * (v.ndim - 1) + [(0, pad)]) if pad else v

    query_low = query_weight.astype(BF)
    query_parts = [query_low] + [shift(query_low, r) for r in range(1, nhead)]
    packed = jnp.concatenate(
        [w.astype(BF) for w in (up_weight.T, down_weight, out_weight)], axis=0
    )
    part = -(-packed.shape[0] // (16 * ndp)) * 16
    packed = jnp.pad(packed, ((0, part * ndp - packed.shape[0]), (0, 0)))
    packed = lax.dynamic_slice_in_dim(packed, dp * part, part, 0)
    packed = [packed] + [shift(packed, r) for r in range(1, nhead)]

    tf, ti, tit, tft = spectral_tables(mode_index)
    wt = mode_weight.reshape(2, own_heads * HEAD_DIM, HEAD_DIM * MODES).transpose(0, 2, 1)
    wt = wide(wt).reshape(2 * HEAD_DIM * MODES, LANES)

    def rows_of(v):
        return v[:, :, :width].reshape(-1, width)

    def contexts_of(v):
        return wide(v.reshape(-1, SEQ_LEN, width))

    def send(parts, way=1):
        return [parts[0]] + [shift(parts[r], way * r) for r in range(1, nhead)]

    query_parts = [query_parts[-r % nhead] for r in range(nhead)]
    queries = query_call(place[1:], series, bias_pair[0], query_parts)
    queries = send(queries)
    *packed, queries[0] = lax.optimization_barrier((*packed, queries[0]))
    packed = [jnp.stack(packed[: nhead // 2]), jnp.stack(packed[nhead // 2 :])]
    packed = gather_pieces(packed[0], ndp, order_a) + gather_pieces(packed[1], ndp, order_b)
    first, second, modes_in = spectrum_call([contexts_of(q) for q in queries], wt, tf, ti)
    first = send([rows_of(v) for v in first], -1)
    second = send([rows_of(v) for v in second], -1)

    starts = jnp.sum(window_id[:, None, :] < jnp.arange(5)[None, :, None], axis=2).astype(jnp.int32)
    valid_float = valid.astype(F32)
    half_call = partial(
        local_call,
        starts=starts,
        prm=decomp_params,
        me=me,
        x=series,
        target=target,
        valid=valid_float[:, None],
        bias=bias_pair[1:],
        packed=packed,
        hidden=hidden,
    )
    d_first, kept_first, sums_first = half_call(0, first, [])
    d_first = send(d_first)
    d_second, kept_second, sums = half_call(1, second, [])
    d_second = send(d_second)
    sums = jnp.sum(sums + sums_first, axis=1)

    hidden_part, out_part = hidden // ndp, width // ndp
    both_halves = list(zip(kept_first, kept_second))
    active, d_hidden, season, d_feed, spectrum, d_attention = both_halves
    layer = outer_call(
        me,
        [
            list(zip(season, d_hidden)),
            list(zip(active, d_feed)),
            list(zip(spectrum, d_attention)),
        ],
        [(d // ndp, hidden), (hidden_part + up8(out_part), d)],
        [(0, 0), (1, 0), (1, hidden_part)],
        ndp,
        "layer_grads",
        d_first[1:],
    )
    layer = Reduction([layer[:2], layer[2:]], [order_a, order_b], ndp)
    layer.split()

    d_queries, d_modes, bias_part = query_grad_call(
        [contexts_of(v) for v in d_first],
        [contexts_of(v) for v in d_second],
        wt,
        tit,
        tft,
        layer.kept,
    )
    d_queries = send([rows_of(v) for v in d_queries], -1)
    mode_parts = mode_grad_call(me, d_modes, modes_in, ndp)
    mode_parts = [m.reshape(ndp // 2, nhead, -1, LANES) for m in mode_parts]
    modes = Reduction([mode_parts[:2], mode_parts[2:]], [order_a, order_b], ndp)
    query = outer_call(
        me,
        [[(series, jnp.stack(d_queries))]],
        [(d // ndp, width)],
        [(0, 0)],
        ndp,
        "query_weight_grads",
    )
    query = Reduction([query], [order_a], ndp)

    def over_heads(v):
        return sum(send([v[r] for r in range(nhead)]))

    up_piece, down_piece = [over_heads(v) for v in layer.rest()]
    down_piece = down_piece[: hidden_part + out_part]
    (query_piece,) = [over_heads(v) for v in query.rest()]
    lanes = HEAD_DIM * MODES // ndp
    mode_pieces = [v.reshape(lanes, LANES).T[: own_heads * HEAD_DIM] for v in modes.rest()]

    bias_zero = lax.dynamic_update_slice_in_dim(
        jnp.zeros((d,), F32), jnp.sum(bias_part, axis=0)[:width], head * width, 0
    )
    squares = sum(jnp.sum(p * p) for p in (query_piece, *mode_pieces, up_piece, down_piece))
    small = jnp.concatenate(
        [
            bias_zero,
            sums[SUM_BIAS],
            jnp.sum(sums[:SUM_BIAS], axis=1),
            jnp.stack([jnp.sum(valid_float), squares]),
        ]
    )
    small = jnp.pad(small, (0, -small.shape[0] % LANES)).reshape(-1, LANES)
    small = sum_everywhere(small, everyone).reshape(-1)
    loss_sum = small[2 * d + SUM_LOSS]
    valid_count = small[2 * d + SUM_LOSS + 1]
    inverse = 1.0 / valid_count
    bias_grad = small[: 2 * d].reshape(2, d) * inverse
    decomp_grad = small[2 * d : 2 * d + 4 * KERNELS].reshape(2, 2, KERNELS) * inverse
    grad_norm = jnp.sqrt(
        small[2 * d + SUM_LOSS + 2] * inverse * inverse
        + jnp.sum(bias_grad * bias_grad)
        + jnp.sum(decomp_grad * decomp_grad)
    )
    factor = jnp.minimum(1.0, CLIP_NORM / (grad_norm + 1e-06))

    everything = slice(None)

    def band(start, stop):
        return (slice(start, stop), everything)

    both = (everything, everything)
    if lanes == d and hidden == d and out_part % 8 == 0:
        ways = d // width
        per = d // ndp // ways
        query_flat = query_piece.reshape(ways, per, width).transpose(1, 0, 2).reshape(per, d)
        two = jnp.concatenate([down_piece, query_flat], axis=0)
        grads = [
            gather_pieces(mode_pieces[0], ndp, order_b),
            gather_pieces(mode_pieces[1], ndp, order_a),
            gather_pieces(up_piece, ndp, order_b),
            gather_pieces(two, ndp, order_a),
        ]
        out_end = hidden_part + out_part
        views = [
            [
                (
                    3,
                    (slice(out_end, out_end + per), slice(n * width, (n + 1) * width)),
                    band(n * per, (n + 1) * per),
                )
                for n in range(ways)
            ],
            [(3, band(hidden_part, out_end), both)],
            [
                (c, band(h * HEAD_DIM, (h + 1) * HEAD_DIM), (c, h) + both)
                for c in range(2)
                for h in range(own_heads)
            ],
            [(2, both, both)],
            [(3, band(0, hidden_part), both)],
        ]
    else:
        pieces = (
            query_piece,
            down_piece[hidden_part:],
            up_piece,
            down_piece[:hidden_part],
            *mode_pieces,
        )
        grads = [gather_pieces(p, ndp, order_b) for p in pieces]
        views = [[(k, both, both)] for k in (0, 1, 4, 2, 3)]
        views[2] = [
            (4 + c, band(h * HEAD_DIM, (h + 1) * HEAD_DIM), (c, h) + both)
            for c in range(2)
            for h in range(own_heads)
        ]

    states = (
        (query_weight, query_first, query_second),
        (out_weight, out_first, out_second),
        (mode_weight, mode_first, mode_second),
        (up_weight, up_first, up_second),
        (down_weight, down_first, down_second),
    )
    news = adam_call(me, (factor * inverse).reshape(1), grads, views, states, (0, 0, 3, 0, 0))
    news += adam_values(bias_pair, bias_grad * factor, bias_first, bias_second)
    news += adam_values(decomp_params, decomp_grad * factor, decomp_first, decomp_second)
    return (loss_sum, valid_count, grad_norm, *news)


def solution(mesh):
    rows = P(("dp", "head"), None)
    down = P("head", None)
    across = P(None, "head")
    modes = P(None, "head", None, None)
    weights = (across,) * 3 + (down,) * 3 + (modes,) * 3 + (across,) * 3 + (down,) * 3 + (P(),) * 6
    sizes = (mesh.shape["dp"], mesh.shape["head"])
    return jax.shard_map(
        partial(on_device, sizes),
        mesh=mesh,
        in_specs=(rows, rows, P(("dp", "head")), rows, down) + weights,
        out_specs=(P(), P(), P()) + weights,
        check_vma=False,
    )
```

time: 551 us -> 438 us (0.79)
  blocking collectives: 43.8 us -> 0 us
  other arithmetic: 57 us -> 25.8 us
  local copies, waits for them, and re-layouts: 61.2 us -> 31.5 us
  Pallas kernels: 127 us -> 155 us
  starting transfers between devices: 111 us -> 84.9 us
  between operations: 22.1 us -> 8.78 us
  waiting for transfers between devices: 121 us -> 131 us
    ppermute x43 -> x38, starting transfers between devices: 80.1 us -> 30.3 us  [swap(): return lax.ppermute(value, axis, [(i, i ^ 1 << bit) for i in range(size)])]
    ppermute x3 -> x33, starting transfers between devices: 4.9 us -> 54.6 us  [shift(): return lax.ppermute(v, 'head', [(i, (i + r) % nhead) for i in range(nhead)])]
    ppermute x3 -> x33, waiting for transfers between devices: 10.2 us -> 58.7 us  [shift(): return lax.ppermute(v, 'head', [(i, (i + r) % nhead) for i in range(nhead)])]
    all_to_all x6 -> x0, waiting for transfers between devices: 35.5 us -> none  [the longest x5 32.3 us: exchange(): return lax.all_to_all(v, 'head', 0, 0, tiled=True)]
    all_gather x2 -> x0, blocking collectives: 34.8 us -> none  [the longest x1 18.6 us: on_device(): packed = lax.all_gather(lax.all_gather(packed, 'head'), 'dp')]
    pallas_call x4 -> x13, Pallas kernels: 116 us -> 145 us  [the longest x2 79.9 us: local_call(): pl.pallas_call(partial(local_kernel, chunk=16, hidden_width=hidden, heads...]
    all_to_all x6 -> x0, starting transfers between devices: 25.7 us -> none  [the longest x5 21.9 us: exchange(): return lax.all_to_all(v, 'head', 0, 0, tiled=True)]
    reshape x4 -> x2, local copies, waits for them, and re-layouts: 24.6 us -> 5.61 us  [the longest x1 5.6 us: on_device(): mode_weight.reshape(2, own_heads * HEAD_DIM, HEAD_DIM * MODES)]
  transfers between devices with their start and end apart: 53 -> 71, of which waited for: 21 -> 26; matrix products, arithmetic and copies ran while one was open for 18% -> 9% of each run, Pallas kernels for 5% -> 26%
where the time goes in v2:
time: 438 us; the launch traced here: 436 us
  Pallas kernels  155 us (35%)
  waiting for transfers between devices  131 us (30%)
  starting transfers between devices  84.9 us (19%)
  local copies, waits for them, and re-layouts  31.5 us (7%)
  other arithmetic  25.8 us (6%)
  between operations  8.78 us (2%)
    pallas_call x2, Pallas kernels, local_call(): pl.pallas_call(partial(local_kernel, chunk=16, hidden_width=hidden, heads...  79.9 us
    ppermute x38, waiting for transfers between devices, swap(): return lax.ppermute(value, axis, [(i, i ^ 1 << bit) for i in range(size)])  71.8 us
    ppermute x33, waiting for transfers between devices, shift(): return lax.ppermute(v, 'head', [(i, (i + r) % nhead) for i in range(nhead)])  58.7 us
    ppermute x33, starting transfers between devices, shift(): return lax.ppermute(v, 'head', [(i, (i + r) % nhead) for i in range(nhead)])  54.6 us
    ppermute x38, starting transfers between devices, swap(): return lax.ppermute(value, axis, [(i, i ^ 1 << bit) for i in range(size)])  30.3 us
    unnamed x114, local copies, waits for them, and re-layouts  20.1 us
    pallas_call x1, Pallas kernels, adam_call(): pl.pallas_call(partial(adam_kernel, views=views, leads=leads, grads=len(g...  18.6 us
    pallas_call x1, Pallas kernels, spectrum_call(): pl.pallas_call(spectrum_kernel, out_shape=[out] * (2 * owners) + [jax.Sha...  14.8 us
  transfers between devices with their start and end apart: 71, of which 26 were waited for; matrix products, arithmetic and copies ran while one was open for 9% of the time, Pallas kernels for 26%

profile of v2, /device:TPU:0, one launch (start us, length us, event | category | flops | bytes accessed | tf_op | source)
XLA Modules:
  0.0 436.3 jit_solution(5870799707764615015)
XLA Ops:
  1.6 3.1 collective-permute-start.5
  16.1 5.5 %collective-permute-start = (bf16[144,512]{1,0:T(8,128)(2,1)S(1)}, bf16[144,512]{1,0:T(8,128)(2,1)S(1)}, u32[]{:S(2)}, u32[]{:S(2)}) collective-permute-start(bf16[144,512]{1,0:T(8,128)(2,1)S(1)} %fusion.4), channel_id=1, source_target_pairs={{0,1},{1,2},{2,3},{3,0},{4,5},{5,6},{6,7},{7,4},{8,9},{9,10},{10,1... | collective-permute-start | bytes 442376 | tf_op jit(solution)/shard_map/ppermute | solution.py:1000
  23.3 8.0 %collective-permute-done.1 = bf16[144,512]{1,0:T(8,128)(2,1)S(1)} collective-permute-done((bf16[144,512]{1,0:T(8,128)(2,1)S(1)}, bf16[144,512]{1,0:T(8,128)(2,1)S(1)}, u32[]{:S(2)}, u32[]{:S(2)}) %collective-permute-start.1) | collective-permute-done | bytes 147488 | tf_op jit(solution)/shard_map/ppermute | solution.py:1000
  35.2 5.1 %collective-permute-done.15 = bf16[2,144,512]{2,1,0:T(8,128)(2,1)S(1)} collective-permute-done((bf16[2,144,512]{2,1,0:T(8,128)(2,1)S(1)}, bf16[2,144,512]{2,1,0:T(8,128)(2,1)S(1)}, u32[]{:S(2)}, u32[]{:S(2)}) %collective-permute-start.15) | collective-permute-done | bytes 294944 | tf_op jit(solution)/shard_map/ppermute | solution.py:857
  46.5 5.6 %copy.86 = f32[2,128,4096]{1,2,0:T(8,128)} copy(f32[2,128,4096]{2,1,0:T(8,128)} %bitcast.204) | data formatting | bytes 8388608 | tf_op jit(solution)/shard_map/reshape | solution.py:1020
  52.9 3.2 collective-permute-start.8
  63.5 8.9 %collective-permute-done.7 = bf16[1024,128]{1,0:T(8,128)(2,1)S(1)} collective-permute-done((bf16[1024,128]{1,0:T(8,128)(2,1)S(1)}, bf16[1024,128]{1,0:T(8,128)(2,1)S(1)}, u32[]{:S(2)}, u32[]{:S(2)}) %collective-permute-start.7) | collective-permute-done | bytes 262176 | tf_op jit(solution)/shard_map/ppermute | solution.py:1000
  72.4 14.8 %spectrum.1 = (bf16[4,128,128]{2,1,0:T(8,128)(2,1)S(1)}, bf16[4,128,128]{2,1,0:T(8,128)(2,1)S(1)}, bf16[4,128,128]{2,1,0:T(8,128)(2,1)S(1)}, bf16[4,128,128]{2,1...) custom-call(f32[8192,128]{1,0:T(8,128)S(1)} %bitcast.168, ...), custom_call_target="tpu_custom_call" | custom-call | flops 16499999744 | bytes 7000000 | tf_op jit(solution)/shard_map/spectrum/pallas_call | solution.py:164
  89.5 3.9 collective-permute-start.9
  98.6 3.8 collective-permute-start.21
  102.4 7.6 %collective-permute-done.10.refs_9_ = bf16[512,128]{1,0:T(8,128)(2,1)S(1)} collective-permute-done((bf16[512,128]{1,0:T(8,128)(2,1)S(1)}, bf16[512,128]{1,0:T(8,128)(2,1)S(1)}, u32[]{:S(2)}, u32[]{:S(2)}) %collective-permute-start.10) | collective-permute-done | bytes 131104 | tf_op jit(solution)/shard_map/ppermute | solution.py:1000
  110.7 39.9 %local_layer.2 = (bf16[512,128]{1,0:T(8,128)(2,1)}, bf16[512,128]{1,0:T(8,128)(2,1)}, bf16[512,128]{1,0:T(8,128)(2,1)}, bf16[512,128]{1,0:T(8,128)(2,1)}, bf16[4...) custom-call(s32[4,5]{1,0:T(4,128)} %copy.102.refs_0_, ...), custom_call_target="tpu_custom_call" | custom-call | flops 41799999488 | bytes 24000000 | tf_op jit(solution)/shard_map/local_layer/pallas_call | solution.py:643
  157.2 40.0 %local_layer.3 = (bf16[512,128]{1,0:T(8,128)(2,1)}, bf16[512,128]{1,0:T(8,128)(2,1)}, bf16[512,128]{1,0:T(8,128)(2,1)}, bf16[512,128]{1,0:T(8,128)(2,1)}, bf16[4...) custom-call(s32[4,5]{1,0:T(4,128)} %copy.103.refs_0_, ...), custom_call_target="tpu_custom_call" | custom-call | flops 41799999488 | bytes 24000000 | tf_op jit(solution)/shard_map/local_layer/pallas_call | solution.py:643
  201.5 9.9 %layer_grads.1 = (f32[4,4,64,512]{3,2,1,0:T(8,128)}, f32[4,4,64,512]{3,2,1,0:T(8,128)}, f32[4,4,80,512]{3,2,1,0:T(8,128)}, f32[4,4,80,512]{3,2,1,0:T(8,128)}) custom-call(s32[1]{0:T(128)} %bitcast.6.refs_2_.me_ref, bf16[512,512]{1,0:T(8,128)(2,1)S(1)} %copy-done.23, bf16[4,512,512]{2,1,0:T(8,128)(2,1)} %get-tuple-element.141.refs_1_, ...), custom_call_target="tpu_custom_call" | custom-call | flops 8800000000 | bytes 20000000 | tf_op jit(solution)/shard_map/layer_grads/pallas_call | solution.py:749
  215.9 3.6 collective-permute-done.27.refs_1_.refs_3_
  225.7 12.1 %query_grads.1 = (bf16[8,128,128]{2,1,0:T(8,128)(2,1)S(1)}, bf16[8,128,128]{2,1,0:T(8,128)(2,1)S(1)}, bf16[8,128,128]{2,1,0:T(8,128)(2,1)S(1)}, bf16[8,128,128]{...) custom-call(f32[8192,128]{1,0:T(8,128)S(1)} %bitcast.169, ...), custom_call_target="tpu_custom_call" | custom-call | flops 12099999744 | bytes 7000000 | tf_op jit(solution)/shard_map/query_grads/pallas_call | solution.py:252
  241.2 5.5 %collective-permute-done.29 = bf16[1024,128]{1,0:T(8,128)(2,1)S(1)} collective-permute-done((bf16[1024,128]{1,0:T(8,128)(2,1)S(1)}, bf16[1024,128]{1,0:T(8,128)(2,1)S(1)}, u32[]{:S(2)}, u32[]{:S(2)}) %collective-permute-start.29) | collective-permute-done | bytes 262176 | tf_op jit(solution)/shard_map/ppermute | solution.py:1000
  246.6 16.8 %collective-permute-done.30 = bf16[1024,128]{1,0:T(8,128)(2,1)S(1)} collective-permute-done((bf16[1024,128]{1,0:T(8,128)(2,1)S(1)}, bf16[1024,128]{1,0:T(8,128)(2,1)S(1)}, u32[]{:S(2)}, u32[]{:S(2)}) %collective-permute-start.30) | collective-permute-done | bytes 262176 | tf_op jit(solution)/shard_map/ppermute | solution.py:1000
  265.8 7.7 %mode_grads.1 = (f32[4,512,128]{2,1,0:T(8,128)}, f32[4,512,128]{2,1,0:T(8,128)S(1)}, f32[4,512,128]{2,1,0:T(8,128)}, f32[4,512,128]{2,1,0:T(8,128)S(1)}) custom-call(s32[1]{0:T(128)} %bitcast.6.refs_2_.me_ref, bf16[64,32,256]{2,1,0:T(8,128)(2,1)S(1)} %get-tuple-element.171.dy_ref, bf16[64,64,128]{2,1,0:T(8,128)(2,1)S(1)} %copy-done.32), custom_call_target="tpu_custom_call" | custom-call | flops 9900000256 | bytes 8000000 | tf_op jit(solution)/shard_map/mode_grads/pallas_call | solution.py:315
  279.5 4.9 %collective-permute-done.33.refs_1_.refs_3_ = f32[2,4,64,128]{3,2,1,0:T(8,128)S(1)} collective-permute-done((f32[2,4,64,128]{3,2,1,0:T(8,128)S(1)}, f32[2,4,64,128]{3,2,1,0:T(8,128)S(1)}, u32[]{:S(2)}, u32[]{:S(2)}) %collective-permute-start.33) | collective-permute-done | bytes 262176 | tf_op jit(solution)/shard_map/ppermute | solution.py:857
  285.9 4.3 split_add.9
  292.4 16.1 %collective-permute-done.34 = f32[1,4,64,128]{3,2,1,0:T(8,128)S(1)} collective-permute-done((f32[1,4,64,128]{3,2,1,0:T(8,128)S(1)}, f32[1,4,64,128]{3,2,1,0:T(8,128)S(1)}, u32[]{:S(2)}, u32[]{:S(2)}) %collective-permute-start.34) | collective-permute-done | bytes 131104 | tf_op jit(solution)/shard_map/ppermute | solution.py:857
  308.6 3.8 collective-permute-start.37
  323.6 8.5 %collective-permute-done.46 = f32[1,4,64,512]{3,2,1,0:T(8,128)S(1)} collective-permute-done((f32[1,4,64,512]{3,2,1,0:T(8,128)S(1)}, f32[1,4,64,512]{3,2,1,0:T(8,128)S(1)}, u32[]{:S(2)}, u32[]{:S(2)}) %collective-permute-start.46) | collective-permute-done | bytes 524320 | tf_op jit(solution)/shard_map/ppermute | solution.py:857
  333.0 3.8 collective-permute-start.49
  337.5 3.8 collective-permute-done.43
  346.0 3.8 collective-permute-start.53
  355.0 7.2 %collective-permute-done.52 = f32[80,512]{1,0:T(8,128)S(1)} collective-permute-done((f32[80,512]{1,0:T(8,128)S(1)}, f32[80,512]{1,0:T(8,128)S(1)}, u32[]{:S(2)}, u32[]{:S(2)}) %collective-permute-start.52) | collective-permute-done | bytes 163872 | tf_op jit(solution)/shard_map/ppermute | solution.py:1000
  368.5 7.4 %collective-permute-done.65 = f32[64,512]{1,0:T(8,128)S(1)} collective-permute-done((f32[64,512]{1,0:T(8,128)S(1)}, f32[64,512]{1,0:T(8,128)S(1)}, u32[]{:S(2)}, u32[]{:S(2)}) %collective-permute-start.65) | collective-permute-done | bytes 131104 | tf_op jit(solution)/shard_map/ppermute | solution.py:857
  393.3 6.1 %collective-permute-done.68 = f32[96,512]{1,0:T(8,128)S(1)} collective-permute-done((f32[96,512]{1,0:T(8,128)S(1)}, f32[96,512]{1,0:T(8,128)S(1)}, u32[]{:S(2)}, u32[]{:S(2)}) %collective-permute-start.68) | collective-permute-done | bytes 196640 | tf_op jit(solution)/shard_map/ppermute | solution.py:857
  404.3 5.1 %collective-permute-done.69 = f32[2,96,512]{2,1,0:T(8,128)S(1)} collective-permute-done((f32[2,96,512]{2,1,0:T(8,128)S(1)}, f32[2,96,512]{2,1,0:T(8,128)S(1)}, u32[]{:S(2)}, u32[]{:S(2)}) %collective-permute-start.69) | collective-permute-done | bytes 393248 | tf_op jit(solution)/shard_map/ppermute | solution.py:857
  416.5 18.6 %adam.1 = (f32[512,128]{1,0:T(8,128)}, f32[512,128]{1,0:T(8,128)}, f32[512,128]{1,0:T(8,128)}, f32[128,512]{1,0:T(8,128)}, f32[128,512]{1,0:T(8,128)}, /*index=5...) custom-call(s32[1]{0:T(128)} %bitcast.6.refs_2_.me_ref, ...), custom_call_target="tpu_custom_call" | custom-call | flops 16499999744 | bytes 48000000 | tf_op jit(solution)/shard_map/adam/pallas_call | solution.py:839
  (321 shorter events, 129.1 us)
Async XLA Ops:
  4.7 16.9 %collective-permute-start.4 = (bf16[512,128]{1,0:T(8,128)(2,1)S(1)}, bf16[512,128]{1,0:T(8,128)(2,1)S(1)}, u32[]{:S(2)}, u32[]{:S(2)}) collective-permute-start(bf16[512,128]{1,0:T(8,128)(2,1)S(1)} %convert_element_type.71.refs_0_), channel_id=1, source_target_pairs={{0,2},{1,3},{2,0},{3,1},{4,6},{5,7},{6,4},{7,5},{8,10},{9,11},{10,... | collective-permute-start | bytes 393224 | tf_op jit(solution)/shard_map/ppermute | solution.py:1000
  13.3 18.0 %collective-permute-start.1 = (bf16[144,512]{1,0:T(8,128)(2,1)S(1)}, bf16[144,512]{1,0:T(8,128)(2,1)S(1)}, u32[]{:S(2)}, u32[]{:S(2)}) collective-permute-start(bf16[144,512]{1,0:T(8,128)(2,1)S(1)} %fusion.4), channel_id=1, source_target_pairs={{0,2},{1,3},{2,0},{3,1},{4,6},{5,7},{6,4},{7,5},{8,10},{9,11},{10,... | collective-permute-start | bytes 442376 | tf_op jit(solution)/shard_map/ppermute | solution.py:1000
  16.1 15.2 %collective-permute-start = (bf16[144,512]{1,0:T(8,128)(2,1)S(1)}, bf16[144,512]{1,0:T(8,128)(2,1)S(1)}, u32[]{:S(2)}, u32[]{:S(2)}) collective-permute-start(bf16[144,512]{1,0:T(8,128)(2,1)S(1)} %fusion.4), channel_id=1, source_target_pairs={{0,1},{1,2},{2,3},{3,0},{4,5},{5,6},{6,7},{7,4},{8,9},{9,10},{10,1... | collective-permute-start | bytes 442376 | tf_op jit(solution)/shard_map/ppermute | solution.py:1000
  40.4 15.7 %collective-permute-start.16 = (bf16[2,2,144,512]{3,2,1,0:T(8,128)(2,1)S(1)}, bf16[2,2,144,512]{3,2,1,0:T(8,128)(2,1)}, u32[]{:S(2)}, u32[]{:S(2)}) collective-permute-start(bf16[2,2,144,512]{3,2,1,0:T(8,128)(2,1)S(1)} %get-tuple-element.222), channel_id=1, source_target_pairs={{0,8},{4,12},{8,0},{12,4},{16,24},{20,28},{24,16},{28,20},{1,9},{5... | collective-permute-start | bytes 1769480 | tf_op jit(solution)/shard_map/ppermute | solution.py:857
  52.3 20.0 %collective-permute-start.7 = (bf16[1024,128]{1,0:T(8,128)(2,1)S(1)}, bf16[1024,128]{1,0:T(8,128)(2,1)S(1)}, u32[]{:S(2)}, u32[]{:S(2)}) collective-permute-start(bf16[1024,128]{1,0:T(8,128)(2,1)S(1)} %get-tuple-element.118), channel_id=1, source_target_pairs={{0,2},{1,3},{2,0},{3,1},{4,6},{5,7},{6,4},{7,5},{8,10},{9,11},{10,... | collective-permute-start | bytes 786440 | tf_op jit(solution)/shard_map/ppermute | solution.py:1000
  52.9 19.4 %collective-permute-start.8 = (bf16[1024,128]{1,0:T(8,128)(2,1)S(1)}, bf16[1024,128]{1,0:T(8,128)(2,1)S(1)}, u32[]{:S(2)}, u32[]{:S(2)}) collective-permute-start(bf16[1024,128]{1,0:T(8,128)(2,1)S(1)} %get-tuple-element.119), channel_id=1, source_target_pairs={{0,3},{1,0},{2,1},{3,2},{4,7},{5,4},{6,5},{7,6},{8,11},{9,8},{10,9... | collective-permute-start | bytes 786440 | tf_op jit(solution)/shard_map/ppermute | solution.py:1000
  61.7 48.6 %collective-permute-start.14 = (bf16[4,2,144,512]{3,2,1,0:T(8,128)(2,1)}, bf16[4,2,144,512]{3,2,1,0:T(8,128)(2,1)}, u32[]{:S(2)}, u32[]{:S(2)}) collective-permute-start(bf16[4,2,144,512]{3,2,1,0:T(8,128)(2,1)} %bitcast.26.refs_11_), channel_id=1, source_target_pairs={{0,4},{4,0},{8,12},{12,8},{16,20},{20,16},{24,28},{28,24},{1,5},{5... | collective-permute-start | bytes 3538952 | tf_op jit(solution)/shard_map/ppermute | solution.py:857
  61.7 48.6 %collective-permute-start.17 = (bf16[4,2,144,512]{3,2,1,0:T(8,128)(2,1)}, bf16[4,2,144,512]{3,2,1,0:T(8,128)(2,1)}, u32[]{:S(2)}, u32[]{:S(2)}) collective-permute-start(bf16[4,2,144,512]{3,2,1,0:T(8,128)(2,1)} %bitcast.33.refs_13_), channel_id=1, source_target_pairs={{0,4},{4,0},{8,12},{12,8},{16,20},{20,16},{24,28},{28,24},{1,5},{5... | collective-permute-start | bytes 3538952 | tf_op jit(solution)/shard_map/ppermute | solution.py:857
  93.4 16.6 %collective-permute-start.10 = (bf16[512,128]{1,0:T(8,128)(2,1)S(1)}, bf16[512,128]{1,0:T(8,128)(2,1)S(1)}, u32[]{:S(2)}, u32[]{:S(2)}) collective-permute-start(bf16[512,128]{1,0:T(8,128)(2,1)S(1)} %bitcast.193), channel_id=1, source_target_pairs={{0,2},{1,3},{2,0},{3,1},{4,6},{5,7},{6,4},{7,5},{8,10},{9,11},{10,... | collective-permute-start | bytes 393224 | tf_op jit(solution)/shard_map/ppermute | solution.py:1000
  98.6 56.0 %collective-permute-start.21 = (bf16[512,128]{1,0:T(8,128)(2,1)S(1)}, bf16[512,128]{1,0:T(8,128)(2,1)S(1)}, u32[]{:S(2)}, u32[]{:S(2)}) collective-permute-start(bf16[512,128]{1,0:T(8,128)(2,1)S(1)} %bitcast.188), channel_id=1, source_target_pairs={{0,3},{1,0},{2,1},{3,2},{4,7},{5,4},{6,5},{7,6},{8,11},{9,8},{10,9... | collective-permute-start | bytes 393224 | tf_op jit(solution)/shard_map/ppermute | solution.py:1000
  110.0 46.4 %collective-permute-start.22 = (bf16[512,128]{1,0:T(8,128)(2,1)S(1)}, bf16[512,128]{1,0:T(8,128)(2,1)S(1)}, u32[]{:S(2)}, u32[]{:S(2)}) collective-permute-start(bf16[512,128]{1,0:T(8,128)(2,1)S(1)} %bitcast.187), channel_id=1, source_target_pairs={{0,2},{1,3},{2,0},{3,1},{4,6},{5,7},{6,4},{7,5},{8,10},{9,11},{10,... | collective-permute-start | bytes 393224 | tf_op jit(solution)/shard_map/ppermute | solution.py:1000
  110.0 46.4 %collective-permute-start.23 = (bf16[512,128]{1,0:T(8,128)(2,1)S(1)}, bf16[512,128]{1,0:T(8,128)(2,1)S(1)}, u32[]{:S(2)}, u32[]{:S(2)}) collective-permute-start(bf16[512,128]{1,0:T(8,128)(2,1)S(1)} %bitcast.186), channel_id=1, source_target_pairs={{0,1},{1,2},{2,3},{3,0},{4,5},{5,6},{6,7},{7,4},{8,9},{9,10},{10,1... | collective-permute-start | bytes 393224 | tf_op jit(solution)/shard_map/ppermute | solution.py:1000
  150.6 46.6 %collective-permute-start.18 = (bf16[512,128]{1,0:T(8,128)(2,1)}, bf16[512,128]{1,0:T(8,128)(2,1)S(1)}, u32[]{:S(2)}, u32[]{:S(2)}) collective-permute-start(bf16[512,128]{1,0:T(8,128)(2,1)} %get-tuple-element.129), channel_id=1, source_target_pairs={{0,1},{1,2},{2,3},{3,0},{4,5},{5,6},{6,7},{7,4},{8,9},{9,10},{10,1... | collective-permute-start | bytes 393224 | tf_op jit(solution)/shard_map/ppermute | solution.py:1000
  153.5 43.7 %collective-permute-start.19 = (bf16[512,128]{1,0:T(8,128)(2,1)}, bf16[512,128]{1,0:T(8,128)(2,1)S(1)}, u32[]{:S(2)}, u32[]{:S(2)}) collective-permute-start(bf16[512,128]{1,0:T(8,128)(2,1)} %get-tuple-element.130), channel_id=1, source_target_pairs={{0,2},{1,3},{2,0},{3,1},{4,6},{5,7},{6,4},{7,5},{8,10},{9,11},{10,... | collective-permute-start | bytes 393224 | tf_op jit(solution)/shard_map/ppermute | solution.py:1000
  154.6 42.6 %collective-permute-start.20 = (bf16[512,128]{1,0:T(8,128)(2,1)}, bf16[512,128]{1,0:T(8,128)(2,1)S(1)}, u32[]{:S(2)}, u32[]{:S(2)}) collective-permute-start(bf16[512,128]{1,0:T(8,128)(2,1)} %get-tuple-element.131), channel_id=1, source_target_pairs={{0,3},{1,0},{2,1},{3,2},{4,7},{5,4},{6,5},{7,6},{8,11},{9,8},{10,9... | collective-permute-start | bytes 393224 | tf_op jit(solution)/shard_map/ppermute | solution.py:1000
  239.6 23.8 %collective-permute-start.30 = (bf16[1024,128]{1,0:T(8,128)(2,1)S(1)}, bf16[1024,128]{1,0:T(8,128)(2,1)S(1)}, u32[]{:S(2)}, u32[]{:S(2)}) collective-permute-start(bf16[1024,128]{1,0:T(8,128)(2,1)S(1)} %bitcast.181), channel_id=1, source_target_pairs={{0,2},{1,3},{2,0},{3,1},{4,6},{5,7},{6,4},{7,5},{8,10},{9,11},{10,... | collective-permute-start | bytes 786440 | tf_op jit(solution)/shard_map/ppermute | solution.py:1000
  241.2 22.2 %collective-permute-start.31 = (bf16[1024,128]{1,0:T(8,128)(2,1)S(1)}, bf16[1024,128]{1,0:T(8,128)(2,1)S(1)}, u32[]{:S(2)}, u32[]{:S(2)}) collective-permute-start(bf16[1024,128]{1,0:T(8,128)(2,1)S(1)} %bitcast.180), channel_id=1, source_target_pairs={{0,1},{1,2},{2,3},{3,0},{4,5},{5,6},{6,7},{7,4},{8,9},{9,10},{10,1... | collective-permute-start | bytes 786440 | tf_op jit(solution)/shard_map/ppermute | solution.py:1000
  274.1 38.3 %collective-permute-start.45 = (f32[2,4,80,512]{3,2,1,0:T(8,128)S(1)}, f32[2,4,80,512]{3,2,1,0:T(8,128)}, u32[]{:S(2)}, u32[]{:S(2)}) collective-permute-start(f32[2,4,80,512]{3,2,1,0:T(8,128)S(1)} %get-tuple-element.186), channel_id=1, source_target_pairs={{0,16},{4,20},{8,24},{12,28},{16,0},{20,4},{24,8},{28,12},{1,17},{... | collective-permute-start | bytes 3932168 | tf_op jit(solution)/shard_map/ppermute | solution.py:857
  277.3 31.4 %collective-permute-start.44 = (f32[2,4,64,512]{3,2,1,0:T(8,128)}, f32[2,4,64,512]{3,2,1,0:T(8,128)}, u32[]{:S(2)}, u32[]{:S(2)}) collective-permute-start(f32[2,4,64,512]{3,2,1,0:T(8,128)} %copy-done.10), channel_id=1, source_target_pairs={{0,8},{4,12},{8,0},{12,4},{16,24},{20,28},{24,16},{28,20},{1,9},{5... | collective-permute-start | bytes 3145736 | tf_op jit(solution)/shard_map/ppermute | solution.py:857
  284.4 24.1 %collective-permute-start.34 = (f32[1,4,64,128]{3,2,1,0:T(8,128)S(1)}, f32[1,4,64,128]{3,2,1,0:T(8,128)S(1)}, u32[]{:S(2)}, u32[]{:S(2)}) collective-permute-start(f32[1,4,64,128]{3,2,1,0:T(8,128)S(1)} %get-tuple-element.170), channel_id=1, source_target_pairs={{0,16},{4,20},{8,24},{12,28},{16,0},{20,4},{24,8},{28,12},{1,17},{... | collective-permute-start | bytes 393224 | tf_op jit(solution)/shard_map/ppermute | solution.py:857
  290.1 27.1 %collective-permute-start.40 = (f32[2,4,128,128]{3,2,1,0:T(8,128)S(1)}, f32[2,4,128,128]{3,2,1,0:T(8,128)S(1)}, u32[]{:S(2)}, u32[]{:S(2)}) collective-permute-start(f32[2,4,128,128]{3,2,1,0:T(8,128)S(1)} %get-tuple-element.178), channel_id=1, source_target_pairs={{0,8},{4,12},{8,0},{12,4},{16,24},{20,28},{24,16},{28,20},{1,9},{5... | collective-permute-start | bytes 1572872 | tf_op jit(solution)/shard_map/ppermute | solution.py:857
  291.7 27.7 %collective-permute-start.41 = (f32[2,4,128,128]{3,2,1,0:T(8,128)S(1)}, f32[2,4,128,128]{3,2,1,0:T(8,128)S(1)}, u32[]{:S(2)}, u32[]{:S(2)}) collective-permute-start(f32[2,4,128,128]{3,2,1,0:T(8,128)S(1)} %get-tuple-element.180), channel_id=1, source_target_pairs={{0,16},{4,20},{8,24},{12,28},{16,0},{20,4},{24,8},{28,12},{1,17},{... | collective-permute-start | bytes 1572872 | tf_op jit(solution)/shard_map/ppermute | solution.py:857
  319.4 26.4 %collective-permute-start.50 = (f32[1,4,80,512]{3,2,1,0:T(8,128)S(1)}, f32[1,4,80,512]{3,2,1,0:T(8,128)S(1)}, u32[]{:S(2)}, u32[]{:S(2)}) collective-permute-start(f32[1,4,80,512]{3,2,1,0:T(8,128)S(1)} %get-tuple-element.190), channel_id=1, source_target_pairs={{0,8},{4,12},{8,0},{12,4},{16,24},{20,28},{24,16},{28,20},{1,9},{5... | collective-permute-start | bytes 1966088 | tf_op jit(solution)/shard_map/ppermute | solution.py:857
  320.2 16.6 %collective-permute-start.42 = (f32[1,4,128,128]{3,2,1,0:T(8,128)S(1)}, f32[1,4,128,128]{3,2,1,0:T(8,128)S(1)}, u32[]{:S(2)}, u32[]{:S(2)}) collective-permute-start(f32[1,4,128,128]{3,2,1,0:T(8,128)S(1)} %get-tuple-element.182), channel_id=1, source_target_pairs={{0,16},{4,20},{8,24},{12,28},{16,0},{20,4},{24,8},{28,12},{1,17},{... | collective-permute-start | bytes 786440 | tf_op jit(solution)/shard_map/ppermute | solution.py:857
  321.8 19.5 %collective-permute-start.43 = (f32[1,4,128,128]{3,2,1,0:T(8,128)S(1)}, f32[1,4,128,128]{3,2,1,0:T(8,128)}, u32[]{:S(2)}, u32[]{:S(2)}) collective-permute-start(f32[1,4,128,128]{3,2,1,0:T(8,128)S(1)} %get-tuple-element.184), channel_id=1, source_target_pairs={{0,8},{4,12},{8,0},{12,4},{16,24},{20,28},{24,16},{28,20},{1,9},{5... | collective-permute-start | bytes 786440 | tf_op jit(solution)/shard_map/ppermute | solution.py:857
  333.0 16.8 %collective-permute-start.47 = (f32[64,512]{1,0:T(8,128)}, f32[64,512]{1,0:T(8,128)}, u32[]{:S(2)}, u32[]{:S(2)}) collective-permute-start(f32[64,512]{1,0:T(8,128)} %get-tuple-element.229), channel_id=1, source_target_pairs={{0,1},{1,2},{2,3},{3,0},{4,5},{5,6},{6,7},{7,4},{8,9},{9,10},{10,1... | collective-permute-start | bytes 393224 | tf_op jit(solution)/shard_map/ppermute | solution.py:1000
  333.0 16.8 %collective-permute-start.49 = (f32[64,512]{1,0:T(8,128)}, f32[64,512]{1,0:T(8,128)}, u32[]{:S(2)}, u32[]{:S(2)}) collective-permute-start(f32[64,512]{1,0:T(8,128)} %get-tuple-element.230), channel_id=1, source_target_pairs={{0,3},{1,0},{2,1},{3,2},{4,7},{5,4},{6,5},{7,6},{8,11},{9,8},{10,9... | collective-permute-start | bytes 393224 | tf_op jit(solution)/shard_map/ppermute | solution.py:1000
  365.2 15.3 %collective-permute-start.62 = (f32[128,512]{1,0:T(8,128)S(1)}, f32[128,512]{1,0:T(8,128)S(1)}, u32[]{:S(2)}, u32[]{:S(2)}) collective-permute-start(f32[128,512]{1,0:T(8,128)S(1)} %bitcast.205), channel_id=1, source_target_pairs={{0,8},{4,12},{8,0},{12,4},{16,24},{20,28},{24,16},{28,20},{1,9},{5... | collective-permute-start | bytes 786440 | tf_op jit(solution)/shard_map/ppermute | solution.py:857
  376.0 33.6 %collective-permute-start.66 = (f32[2,64,512]{2,1,0:T(8,128)S(1)}, f32[2,64,512]{2,1,0:T(8,128)}, u32[]{:S(2)}, u32[]{:S(2)}) collective-permute-start(f32[2,64,512]{2,1,0:T(8,128)S(1)} %get-tuple-element.239), channel_id=1, source_target_pairs={{0,8},{4,12},{8,0},{12,4},{16,24},{20,28},{24,16},{28,20},{1,9},{5... | collective-permute-start | bytes 786440 | tf_op jit(solution)/shard_map/ppermute | solution.py:857
  378.6 24.0 %collective-permute-start.60 = (f32[2,128,512]{2,1,0:T(8,128)S(1)}, f32[2,128,512]{2,1,0:T(8,128)}, u32[]{:S(2)}, u32[]{:S(2)}) collective-permute-start(f32[2,128,512]{2,1,0:T(8,128)S(1)} %get-tuple-element.228), channel_id=1, source_target_pairs={{0,8},{4,12},{8,0},{12,4},{16,24},{20,28},{24,16},{28,20},{1,9},{5... | collective-permute-start | bytes 1572872 | tf_op jit(solution)/shard_map/ppermute | solution.py:857
  380.7 19.7 %collective-permute-start.63 = (f32[2,128,512]{2,1,0:T(8,128)S(1)}, f32[2,128,512]{2,1,0:T(8,128)}, u32[]{:S(2)}, u32[]{:S(2)}) collective-permute-start(f32[2,128,512]{2,1,0:T(8,128)S(1)} %get-tuple-element.226), channel_id=1, source_target_pairs={{0,16},{4,20},{8,24},{12,28},{16,0},{20,4},{24,8},{28,12},{1,17},{... | collective-permute-start | bytes 1572872 | tf_op jit(solution)/shard_map/ppermute | solution.py:857
  384.5 14.9 %collective-permute-start.68 = (f32[96,512]{1,0:T(8,128)S(1)}, f32[96,512]{1,0:T(8,128)S(1)}, u32[]{:S(2)}, u32[]{:S(2)}) collective-permute-start(f32[96,512]{1,0:T(8,128)S(1)} %get-tuple-element.241), channel_id=1, source_target_pairs={{0,8},{4,12},{8,0},{12,4},{16,24},{20,28},{24,16},{28,20},{1,9},{5... | collective-permute-start | bytes 589832 | tf_op jit(solution)/shard_map/ppermute | solution.py:857
  (94 other events, 840.5 us)

commit v3 on v2

--- a/solution.py
+++ b/solution.py
@@ -269,8 +269,8 @@
 
 
 def mode_grad_kernel(me_ref, dy_ref, xs_ref, *refs):
-    outs = refs[:4]
-    dw_scr, sems = refs[4:]
+    outs = refs[-7:-3]
+    dw_scr, low_scr, sems = refs[-3:]
     pieces, depth = 2 * outs[0].shape[0], outs[0].shape[1]
     total = HEAD_DIM * MODES
     low = lane_low(HEAD_DIM)
@@ -292,13 +292,17 @@
         return 0
 
     lax.fori_loop(0, MODES, mix, 0, unroll=4)
+    for j in range(1, pieces, 2):
+        for c in range(2):
+            start = pl.multiple_of(c * total + (me ^ j) * depth, depth)
+            low_scr[c, j // 2] = dw_scr[pl.ds(start, depth), :].astype(BF)
     copies = []
     for j in range(pieces):
         for c in range(2):
             start = pl.multiple_of(c * total + (me ^ j) * depth, depth)
             copies.append(
                 pltpu.make_async_copy(
-                    dw_scr.at[pl.ds(start, depth), :],
+                    low_scr.at[c, j // 2] if j % 2 else dw_scr.at[pl.ds(start, depth), :],
                     outs[2 * c + (j + 1) % 2].at[j // 2],
                     sems.at[c, j],
                 )
@@ -309,22 +313,25 @@
         copy.wait()
 
 
-def mode_grad_call(me, dy, xs, pieces):
+def mode_grad_call(me, dy, xs, pieces, waits):
     part = jax.ShapeDtypeStruct((pieces // 2, HEAD_DIM * MODES // pieces, LANES), F32)
     whole = pl.BlockSpec(memory_space=pltpu.VMEM)
     return pl.pallas_call(
         mode_grad_kernel,
-        in_specs=[pl.BlockSpec(memory_space=pltpu.SMEM)] + [whole] * 2,
+        in_specs=[pl.BlockSpec(memory_space=pltpu.SMEM)]
+        + [whole] * 2
+        + [pl.BlockSpec(memory_space=pl.ANY)] * len(waits),
         out_specs=[pl.BlockSpec(memory_space=pl.ANY)] * 4,
-        out_shape=[part] * 4,
+        out_shape=[jax.ShapeDtypeStruct(part.shape, BF), part] * 2,
         scratch_shapes=[
             pltpu.VMEM((2 * HEAD_DIM * MODES, LANES), F32),
+            pltpu.VMEM((2,) + part.shape, BF),
             pltpu.SemaphoreType.DMA((2, pieces)),
         ],
         compiler_params=pltpu.CompilerParams(vmem_limit_bytes=40 * MIB),
         cost_estimate=cost(9, 8e6),
         name="mode_grads",
-    )(me, dy, xs)
+    )(me, dy, xs, *waits)
 
 
 SUM_SLOPE = (0, 10)
@@ -694,43 +701,41 @@
 
 
 def outer_kernel(me_ref, *refs, halves, outs, waits):
-    count = len(halves)
     scratch = refs[-1]
-    ins = refs[: 2 * sum(halves)]
-    targets = refs[2 * sum(halves) + waits : -1]
-    for k in range(count):
+    ins = list(refs[: 2 * sum(halves)])
+    targets = list(refs[2 * sum(halves) + waits : -1])
+    for count, cuts in zip(halves, outs):
         total = None
-        for n in range(halves[k]):
-            left, right = ins[2 * (sum(halves[:k]) + n) : 2 * (sum(halves[:k]) + n) + 2]
-            left = left[0] if len(left.shape) == 3 else left[...]
-            right = right[0] if len(right.shape) == 3 else right[...]
+        for _ in range(count):
+            left, right = (r[0] if len(r.shape) == 3 else r[...] for r in ins[:2])
+            del ins[:2]
             term = dot(left, right, 0, 0)
             total = term if total is None else total + term
-        where, offset = outs[k]
-        send, keep = targets[2 * where : 2 * where + 2]
-        pieces = 2 * send.shape[0]
-        size = total.shape[0] // pieces
-        lanes = slice(0, total.shape[1])
-        if size % 8 == 0:
-            scratch[: total.shape[0], lanes] = total
+        rows, columns = total.shape
+        lanes = slice(0, columns)
+        scratch[:rows, lanes] = total
+        offset = 0
+        for cut in cuts:
+            send, keep = targets[:2]
+            del targets[:2]
+            pieces = 2 * send.shape[0]
+            size = rows // pieces
             for j in range(pieces):
-                row = pl.multiple_of((me_ref[0] ^ j) * size, size)
-                (send if j % 2 else keep)[j // 2, 0, offset : offset + size, :] = scratch[
-                    pl.ds(row, size), lanes
-                ]
-        else:
-            scratch[: total.shape[0], lanes] = total
-            for j in range(pieces):
-                (send if j % 2 else keep)[j // 2, 0, offset:, :] = jnp.zeros(
-                    (send.shape[2] - offset, total.shape[1]), F32
-                )
-                for i in range(size):
-                    (send if j % 2 else keep)[j // 2, 0, offset + i : offset + i + 1, :] = scratch[
-                        pl.ds((me_ref[0] ^ j) * size + i, 1), lanes
-                    ]
-
-
-def outer_call(me, products, shapes, outs, pieces, name, waits=()):
+                target = send if j % 2 else keep
+                start = (me_ref[0] ^ j) * size + offset
+                if cut % 8 == 0:
+                    part = scratch[pl.ds(pl.multiple_of(start, 8), cut), lanes]
+                    target[j // 2, 0] = part.astype(target.dtype)
+                else:
+                    row = lax.broadcasted_iota(jnp.int32, (target.shape[2], 1), 0)
+                    part = jnp.zeros((target.shape[2], columns), F32)
+                    for i in range(cut):
+                        part = jnp.where(row == i, scratch[pl.ds(start + i, 1), lanes], part)
+                    target[j // 2, 0] = part.astype(target.dtype)
+            offset += cut
+
+
+def outer_call(me, products, outs, pieces, name, waits=()):
     heads = next(a.shape[0] for p in products for pair in p for a in pair if a.ndim == 3)
     operands = [a for p in products for pair in p for a in pair]
 
@@ -739,30 +744,36 @@
             return pl.BlockSpec((1,) + a.shape[1:], lambda h: (h, 0, 0))
         return pl.BlockSpec(a.shape, lambda h: (0, 0))
 
-    out_specs = [
-        pl.BlockSpec((pieces // 2, 1) + shape, lambda h: (0, h, 0, 0))
-        for shape in shapes
-        for _ in range(2)
-    ]
+    shapes = []
+    for p, cuts in zip(products, outs):
+        for cut, kind in cuts:
+            tail = (cut if cut % 8 == 0 else 16, p[0][1].shape[-1])
+            shapes += [
+                jax.ShapeDtypeStruct((pieces // 2, heads) + tail, t) for t in (kind, F32)
+            ]
     rows = max(pair[0].shape[-1] for p in products for pair in p)
     columns = max(pair[1].shape[-1] for p in products for pair in p)
-    return pl.pallas_call(
-        partial(outer_kernel, halves=[len(p) for p in products], outs=outs, waits=len(waits)),
+    res = pl.pallas_call(
+        partial(
+            outer_kernel,
+            halves=[len(p) for p in products],
+            outs=[[cut for cut, _ in cuts] for cuts in outs],
+            waits=len(waits),
+        ),
         grid=(heads,),
         in_specs=[pl.BlockSpec(memory_space=pltpu.SMEM)]
         + [spec(a) for a in operands]
         + [pl.BlockSpec(memory_space=pl.ANY)] * len(waits),
-        out_specs=out_specs,
-        out_shape=[
-            jax.ShapeDtypeStruct((pieces // 2, heads) + shape, F32)
-            for shape in shapes
-            for _ in range(2)
+        out_specs=[
+            pl.BlockSpec((s.shape[0], 1) + s.shape[2:], lambda h: (0, h, 0, 0)) for s in shapes
         ],
+        out_shape=shapes,
         scratch_shapes=[pltpu.VMEM((rows, columns), F32)],
-        compiler_params=pltpu.CompilerParams(vmem_limit_bytes=48 * MIB),
+        compiler_params=pltpu.CompilerParams(vmem_limit_bytes=60 * MIB),
         cost_estimate=cost(8, 20e6),
         name=name,
     )(me, *operands, *waits)
+    return [(res[2 * k], res[2 * k + 1]) for k in range(len(res) // 2)]
 
 
 def adam_values(weight, gradient, first, second):
@@ -846,7 +857,7 @@
             scratch_shapes=[pltpu.VMEM(pair[0].shape[1:], F32) for pair in grads],
         ),
         out_shape=shapes,
-        compiler_params=pltpu.CompilerParams(vmem_limit_bytes=48 * MIB),
+        compiler_params=pltpu.CompilerParams(vmem_limit_bytes=60 * MIB),
         cost_estimate=cost(15, 48e6),
         name="adam",
     )(me, scale, *operands)
@@ -860,25 +871,30 @@
 def split_add(items):
     specs, operands, shapes, out_specs = [], [], [], []
     half = items[0][0].shape[0] // 2
-    heads = items[0][0].shape[1]
+    splits = 4
     for kept, got, lowest in items:
-        block = (1, 1) + kept.shape[2:]
-        away = (lambda i, h: (2 * i + 1, h, 0, 0)) if lowest else (lambda i, h: (half + i, h, 0, 0))
-        stay = (lambda i, h: (2 * i, h, 0, 0)) if lowest else (lambda i, h: (i, h, 0, 0))
-        for index in (away, stay):
+        cut = kept.shape[2] % (16 * splits) == 0
+        block = (1, kept.shape[1], kept.shape[2] // (splits if cut else 1), kept.shape[3])
+
+        def at(index, cut=cut):
+            return lambda i, s: (index(i), 0, s if cut else 0, 0)
+
+        away = at((lambda i: 2 * i + 1) if lowest else (lambda i: half + i))
+        stay = at((lambda i: 2 * i) if lowest else (lambda i: i))
+        for index, kind in ((away, got.dtype), (stay, F32)):
             specs += [pl.BlockSpec(block, index)] * 2
             operands += [kept, got]
-            out_specs.append(pl.BlockSpec(block, lambda i, h: (i, h, 0, 0)))
-            shapes.append(jax.ShapeDtypeStruct((half,) + kept.shape[1:], F32))
+            out_specs.append(pl.BlockSpec(block, at(lambda i: i)))
+            shapes.append(jax.ShapeDtypeStruct((half,) + kept.shape[1:], kind))
 
     def body(*refs):
         outs = refs[len(operands) :]
         for k, out in enumerate(outs):
-            out[...] = refs[2 * k][...] + refs[2 * k + 1][...]
+            out[...] = (refs[2 * k][...] + refs[2 * k + 1][...].astype(F32)).astype(out.dtype)
 
     res = pl.pallas_call(
         body,
-        grid=(half, heads),
+        grid=(half, splits),
         in_specs=specs,
         out_specs=out_specs,
         out_shape=shapes,
@@ -909,24 +925,52 @@
     def rest(self):
         while self.orders[0]:
             self.split()
-        return [keep[0] + got[0] for keep, got in zip(self.kept, self.got)]
-
-
-def gather_pieces(piece, size, order):
-    have = []
-    now = piece
-    for bit in order:
-        at = len([b for b in have if b > bit])
-        now = jnp.stack([now, swap(now, "dp", size, bit)], axis=at)
-        have = sorted(have + [bit], reverse=True)
-    now = now.reshape((size // 2,) + piece.shape)
-    return now, swap(now, "dp", size, 0)
-
-
-def sum_everywhere(value, sizes):
-    for axis, size in sizes:
-        for bit in range(size.bit_length() - 1):
-            value = value + swap(value, axis, size, bit)
+        return [keep[0] + got[0].astype(F32) for keep, got in zip(self.kept, self.got)]
+
+
+class Gathering:
+    def __init__(self, pieces, orders, size):
+        self.size = size
+        self.now = list(pieces)
+        self.shapes = [p.shape for p in pieces]
+        self.orders = [list(order) for order in orders]
+        self.have = [[] for _ in pieces]
+
+    def start(self):
+        self.other = [
+            swap(now, "dp", self.size, order[0]) for now, order in zip(self.now, self.orders)
+        ]
+
+    def finish(self):
+        for k, order in enumerate(self.orders):
+            bit = order.pop(0)
+            at = len([b for b in self.have[k] if b > bit])
+            self.now[k] = jnp.stack([self.now[k], self.other[k]], axis=at)
+            self.have[k] = sorted(self.have[k] + [bit], reverse=True)
+
+    def double(self):
+        self.start()
+        self.finish()
+
+    def across(self):
+        while self.orders[0]:
+            self.double()
+
+    def pairs(self):
+        self.across()
+        own = [n.reshape((self.size // 2,) + s) for n, s in zip(self.now, self.shapes)]
+        return [(n, swap(n, "dp", self.size, 0)) for n in own]
+
+
+def together(*groups):
+    flat, tree = jax.tree.flatten(groups)
+    return jax.tree.unflatten(tree, lax.optimization_barrier(flat))
+
+
+def sum_steps(value, sizes, steps):
+    every = [(axis, size, bit) for axis, size in sizes for bit in range(size.bit_length() - 1)]
+    for axis, size, bit in every[steps]:
+        value = value + swap(value, axis, size, bit)
     return value
 
 
@@ -1029,18 +1073,30 @@
     def send(parts, way=1):
         return [parts[0]] + [shift(parts[r], way * r) for r in range(1, nhead)]
 
+    starts = jnp.sum(window_id[:, None, :] < jnp.arange(5)[None, :, None], axis=2).astype(jnp.int32)
+    valid_float = valid.astype(F32)
+    valid_rows = valid_float[:, None]
+    query_parts, wt, tf, ti, tit, tft, starts, valid_rows = together(
+        query_parts, wt, tf, ti, tit, tft, starts, valid_rows
+    )
+
     query_parts = [query_parts[-r % nhead] for r in range(nhead)]
     queries = query_call(place[1:], series, bias_pair[0], query_parts)
     queries = send(queries)
-    *packed, queries[0] = lax.optimization_barrier((*packed, queries[0]))
+    queries[1], packed = together(queries[1], packed)
     packed = [jnp.stack(packed[: nhead // 2]), jnp.stack(packed[nhead // 2 :])]
-    packed = gather_pieces(packed[0], ndp, order_a) + gather_pieces(packed[1], ndp, order_b)
+    packed = Gathering(packed, [order_a, order_b], ndp)
+    packed.start()
+    queries, packed.other = together(queries, packed.other)
+    packed.finish()
+    packed.start()
     first, second, modes_in = spectrum_call([contexts_of(q) for q in queries], wt, tf, ti)
+    first, second, packed.other = together(first, second, packed.other)
+    packed.finish()
+    packed = [half for pair in packed.pairs() for half in pair]
     first = send([rows_of(v) for v in first], -1)
     second = send([rows_of(v) for v in second], -1)
 
-    starts = jnp.sum(window_id[:, None, :] < jnp.arange(5)[None, :, None], axis=2).astype(jnp.int32)
-    valid_float = valid.astype(F32)
     half_call = partial(
         local_call,
         starts=starts,
@@ -1048,7 +1104,7 @@
         me=me,
         x=series,
         target=target,
-        valid=valid_float[:, None],
+        valid=valid_rows,
         bias=bias_pair[1:],
         packed=packed,
         hidden=hidden,
@@ -1062,6 +1118,8 @@
     hidden_part, out_part = hidden // ndp, width // ndp
     both_halves = list(zip(kept_first, kept_second))
     active, d_hidden, season, d_feed, spectrum, d_attention = both_halves
+    first_cut = hidden_part // 4 if hidden_part % 64 == 0 else 0
+    down_cuts = [(c, F32) for c in (first_cut, hidden_part - first_cut) if c]
     layer = outer_call(
         me,
         [
@@ -1069,13 +1127,12 @@
             list(zip(active, d_feed)),
             list(zip(spectrum, d_attention)),
         ],
-        [(d // ndp, hidden), (hidden_part + up8(out_part), d)],
-        [(0, 0), (1, 0), (1, hidden_part)],
+        [[(d // ndp, BF)], down_cuts, [(out_part, BF)]],
         ndp,
         "layer_grads",
         d_first[1:],
     )
-    layer = Reduction([layer[:2], layer[2:]], [order_a, order_b], ndp)
+    layer = Reduction(layer, ([order_a] * 2 + [order_b] * 2)[: len(layer)], ndp)
     layer.split()
 
     d_queries, d_modes, bias_part = query_grad_call(
@@ -1087,32 +1144,48 @@
         layer.kept,
     )
     d_queries = send([rows_of(v) for v in d_queries], -1)
-    mode_parts = mode_grad_call(me, d_modes, modes_in, ndp)
+    layer.split()
+    mode_parts = mode_grad_call(me, d_modes, modes_in, ndp, layer.kept)
     mode_parts = [m.reshape(ndp // 2, nhead, -1, LANES) for m in mode_parts]
-    modes = Reduction([mode_parts[:2], mode_parts[2:]], [order_a, order_b], ndp)
+    d_queries, mode_parts = together(d_queries, mode_parts)
     query = outer_call(
         me,
         [[(series, jnp.stack(d_queries))]],
-        [(d // ndp, width)],
-        [(0, 0)],
+        [[(d // ndp, BF)]],
         ndp,
         "query_weight_grads",
     )
-    query = Reduction([query], [order_a], ndp)
-
-    def over_heads(v):
-        return sum(send([v[r] for r in range(nhead)]))
-
-    up_piece, down_piece = [over_heads(v) for v in layer.rest()]
-    down_piece = down_piece[: hidden_part + out_part]
-    (query_piece,) = [over_heads(v) for v in query.rest()]
+    late = Reduction(
+        [mode_parts[:2], mode_parts[2:], *query], [order_a, order_b, order_a], ndp
+    )
+
+    def over_heads(v, kind=F32):
+        parts = send([v[r].astype(kind) for r in range(nhead)])
+        return sum([p.astype(F32) for p in parts[1:]], v[0])
+
     lanes = HEAD_DIM * MODES // ndp
-    mode_pieces = [v.reshape(lanes, LANES).T[: own_heads * HEAD_DIM] for v in modes.rest()]
+    up_piece, *down_pieces, out_piece = layer.rest()
+    down_piece = over_heads(jnp.concatenate(down_pieces, axis=1))
+    if hidden == d and out_part % 8 == 0:
+        both_pieces = over_heads(jnp.concatenate([up_piece, out_piece], axis=1), BF)
+        up_piece, out_piece = both_pieces[: d // ndp], both_pieces[d // ndp :]
+    else:
+        up_piece, out_piece = over_heads(up_piece, BF), over_heads(out_piece, BF)[:out_part]
+    *mode_pieces, query_piece = late.rest()
+    query_piece = over_heads(query_piece, BF)
+    mode_pieces = [v.reshape(lanes, LANES).T[: own_heads * HEAD_DIM] for v in mode_pieces]
+    mode_all = Gathering(mode_pieces, [order_b, order_a], ndp)
+    mode_all.across()
+    (up_piece, down_piece, out_piece, query_piece), mode_all.now = together(
+        (up_piece, down_piece, out_piece, query_piece), mode_all.now
+    )
 
     bias_zero = lax.dynamic_update_slice_in_dim(
         jnp.zeros((d,), F32), jnp.sum(bias_part, axis=0)[:width], head * width, 0
     )
-    squares = sum(jnp.sum(p * p) for p in (query_piece, *mode_pieces, up_piece, down_piece))
+    squares = sum(
+        jnp.sum(p * p) for p in (query_piece, *mode_pieces, up_piece, down_piece, out_piece)
+    )
     small = jnp.concatenate(
         [
             bias_zero,
@@ -1122,7 +1195,25 @@
         ]
     )
     small = jnp.pad(small, (0, -small.shape[0] % LANES)).reshape(-1, LANES)
-    small = sum_everywhere(small, everyone).reshape(-1)
+    small_steps = (ndp * nhead).bit_length() - 1
+    small = sum_steps(small, everyone, slice(0, 2))
+
+    if HEAD_DIM * MODES // ndp == d and hidden == d and out_part % 8 == 0:
+        ways = d // width
+        per = d // ndp // ways
+        query_flat = query_piece.reshape(ways, per, width).transpose(1, 0, 2).reshape(per, d)
+        rest = [up_piece, jnp.concatenate([down_piece, out_piece, query_flat], axis=0)]
+    else:
+        rest = [up_piece, down_piece, out_piece, query_piece]
+    rest_all = Gathering(rest, [order_b, order_a, order_b, order_a][: len(rest)], ndp)
+    rest_all.double()
+    small, rest_all.now, mode_all.now = together(small, rest_all.now, mode_all.now)
+    small = sum_steps(small, everyone, slice(2, small_steps - 1))
+    rest_all.across()
+    grads = mode_all.pairs()
+    small, rest_all.now, grads = together(small, rest_all.now, grads)
+    small = sum_steps(small, everyone, slice(small_steps - 1, small_steps)).reshape(-1)
+    grads += rest_all.pairs()
     loss_sum = small[2 * d + SUM_LOSS]
     valid_count = small[2 * d + SUM_LOSS + 1]
     inverse = 1.0 / valid_count
@@ -1141,17 +1232,12 @@
         return (slice(start, stop), everything)
 
     both = (everything, everything)
-    if lanes == d and hidden == d and out_part % 8 == 0:
-        ways = d // width
-        per = d // ndp // ways
-        query_flat = query_piece.reshape(ways, per, width).transpose(1, 0, 2).reshape(per, d)
-        two = jnp.concatenate([down_piece, query_flat], axis=0)
-        grads = [
-            gather_pieces(mode_pieces[0], ndp, order_b),
-            gather_pieces(mode_pieces[1], ndp, order_a),
-            gather_pieces(up_piece, ndp, order_b),
-            gather_pieces(two, ndp, order_a),
-        ]
+    mode_view = [
+        (c, band(h * HEAD_DIM, (h + 1) * HEAD_DIM), (c, h) + both)
+        for c in range(2)
+        for h in range(own_heads)
+    ]
+    if len(rest) == 2:
         out_end = hidden_part + out_part
         views = [
             [
@@ -1163,29 +1249,12 @@
                 for n in range(ways)
             ],
             [(3, band(hidden_part, out_end), both)],
-            [
-                (c, band(h * HEAD_DIM, (h + 1) * HEAD_DIM), (c, h) + both)
-                for c in range(2)
-                for h in range(own_heads)
-            ],
+            mode_view,
             [(2, both, both)],
             [(3, band(0, hidden_part), both)],
         ]
     else:
-        pieces = (
-            query_piece,
-            down_piece[hidden_part:],
-            up_piece,
-            down_piece[:hidden_part],
-            *mode_pieces,
-        )
-        grads = [gather_pieces(p, ndp, order_b) for p in pieces]
-        views = [[(k, both, both)] for k in (0, 1, 4, 2, 3)]
-        views[2] = [
-            (4 + c, band(h * HEAD_DIM, (h + 1) * HEAD_DIM), (c, h) + both)
-            for c in range(2)
-            for h in range(own_heads)
-        ]
+        views = [[(5, both, both)], [(4, both, both)], mode_view, [(2, both, both)], [(3, both, both)]]
 
     states = (
         (query_weight, query_first, query_second),

time: 438 us -> 398 us (0.909)
  waiting for transfers between devices: 131 us -> 95.5 us
  other arithmetic: 25.8 us -> 20.3 us
    ppermute x38 -> x44, waiting for transfers between devices: 71.8 us -> 47.5 us  [swap(): return lax.ppermute(value, axis, [(i, i ^ 1 << bit) for i in range(size)])]
    ppermute x33, waiting for transfers between devices: 58.7 us -> 48 us  [shift(): return lax.ppermute(v, 'head', [(i, (i + r) % nhead) for i in range(nhead)])]
    another operation x15 -> x16, other arithmetic: 10.8 us -> 3.45 us  [the longest x14 3.38 us: finish(): self.now[k] = jnp.stack([self.now[k], self.other[k]], axis=at)]
    unnamed x114 -> x133, local copies, waits for them, and re-layouts: 20.1 us -> 19.1 us
    ppermute x38 -> x44, starting transfers between devices: 30.3 us -> 30 us  [swap(): return lax.ppermute(value, axis, [(i, i ^ 1 << bit) for i in range(size)])]
  transfers between devices with their start and end apart: 71 -> 77, of which waited for: 26 -> 26; matrix products, arithmetic and copies ran while one was open for 9% -> 7% of each run, Pallas kernels for 26% -> 32%
where the time goes in v3:
time: 398 us; the launch traced here: 397 us
  Pallas kernels  159 us (40%)
  waiting for transfers between devices  95.5 us (24%)
  starting transfers between devices  80.7 us (20%)
  local copies, waits for them, and re-layouts  31.5 us (8%)
  other arithmetic  20.3 us (5%)
  between operations  9.65 us (2%)
    pallas_call x2, Pallas kernels, local_call(): pl.pallas_call(partial(local_kernel, chunk=16, hidden_width=hidden, heads...  79.8 us
    ppermute x33, starting transfers between devices, shift(): return lax.ppermute(v, 'head', [(i, (i + r) % nhead) for i in range(nhead)])  50.7 us
    ppermute x33, waiting for transfers between devices, shift(): return lax.ppermute(v, 'head', [(i, (i + r) % nhead) for i in range(nhead)])  48 us
    ppermute x44, waiting for transfers between devices, swap(): return lax.ppermute(value, axis, [(i, i ^ 1 << bit) for i in range(size)])  47.5 us
    ppermute x44, starting transfers between devices, swap(): return lax.ppermute(value, axis, [(i, i ^ 1 << bit) for i in range(size)])  30 us
    pallas_call x1, Pallas kernels, adam_call(): pl.pallas_call(partial(adam_kernel, views=views, leads=leads, grads=len(g...  19.7 us
    unnamed x133, local copies, waits for them, and re-layouts  19.1 us
    pallas_call x2, Pallas kernels, outer_call(): pl.pallas_call(partial(outer_kernel, halves=[len(p) for p in products], o...  15.7 us
  transfers between devices with their start and end apart: 77, of which 26 were waited for; matrix products, arithmetic and copies ran while one was open for 7% of the time, Pallas kernels for 32%

profile of v3, /device:TPU:0, one launch (start us, length us, event | category | flops | bytes accessed | tf_op | source)
XLA Modules:
  0.0 396.7 jit_solution(3332770689504146582)
XLA Ops:
  1.7 5.1 %collective-permute-start.2 = (bf16[512,128]{1,0:T(8,128)(2,1)S(1)}, bf16[512,128]{1,0:T(8,128)(2,1)S(1)}, u32[]{:S(2)}, u32[]{:S(2)}) collective-permute-start(bf16[512,128]{1,0:T(8,128)(2,1)S(1)} %convert_element_type.122.refs_0_), channel_id=1, source_target_pairs={{0,3},{1,0},{2,1},{3,2},{4,7},{5,4},{6,5},{7,6},{8,11},{9,8},{10,9... | collective-permute-start | bytes 393224 | tf_op jit(solution)/shard_map/ppermute | solution.py:1044
  13.1 5.7 %copy.86 = f32[2,128,4096]{1,2,0:T(8,128)} copy(f32[2,128,4096]{2,1,0:T(8,128)} %bitcast.203) | data formatting | bytes 8388608 | tf_op jit(solution)/shard_map/reshape | solution.py:1064
  26.3 6.7 %collective-permute-done.6 = bf16[144,512]{1,0:T(8,128)(2,1)S(1)} collective-permute-done((bf16[144,512]{1,0:T(8,128)(2,1)S(1)}, bf16[144,512]{1,0:T(8,128)(2,1)S(1)}, u32[]{:S(2)}, u32[]{:S(2)}) %collective-permute-start.6) | collective-permute-done | bytes 147488 | tf_op jit(solution)/shard_map/ppermute | solution.py:1044
  33.1 9.2 %collective-permute-done.5 = bf16[144,512]{1,0:T(8,128)(2,1)S(1)} collective-permute-done((bf16[144,512]{1,0:T(8,128)(2,1)S(1)}, bf16[144,512]{1,0:T(8,128)(2,1)S(1)}, u32[]{:S(2)}, u32[]{:S(2)}) %collective-permute-start.5) | collective-permute-done | bytes 147488 | tf_op jit(solution)/shard_map/ppermute | solution.py:1044
  47.9 9.9 %collective-permute-done.7 = bf16[1024,128]{1,0:T(8,128)(2,1)S(1)} collective-permute-done((bf16[1024,128]{1,0:T(8,128)(2,1)S(1)}, bf16[1024,128]{1,0:T(8,128)(2,1)S(1)}, u32[]{:S(2)}, u32[]{:S(2)}) %collective-permute-start.7) | collective-permute-done | bytes 262176 | tf_op jit(solution)/shard_map/ppermute | solution.py:1044
  65.3 14.8 %spectrum.1 = (bf16[4,128,128]{2,1,0:T(8,128)(2,1)S(1)}, bf16[4,128,128]{2,1,0:T(8,128)(2,1)S(1)}, bf16[4,128,128]{2,1,0:T(8,128)(2,1)S(1)}, bf16[4,128,128]{2,1...) custom-call(f32[8192,128]{1,0:T(8,128)S(1)} %bitcast.171, ...), custom_call_target="tpu_custom_call" | custom-call | flops 16499999744 | bytes 7000000 | tf_op jit(solution)/shard_map/spectrum/pallas_call | solution.py:164
  83.6 4.9 %collective-permute-start.13 = (bf16[512,128]{1,0:T(8,128)(2,1)S(1)}, bf16[512,128]{1,0:T(8,128)(2,1)S(1)}, u32[]{:S(2)}, u32[]{:S(2)}) collective-permute-start(bf16[512,128]{1,0:T(8,128)(2,1)S(1)} %bitcast.193), channel_id=1, source_target_pairs={{0,3},{1,0},{2,1},{3,2},{4,7},{5,4},{6,5},{7,6},{8,11},{9,8},{10,9... | collective-permute-start | bytes 393224 | tf_op jit(solution)/shard_map/ppermute | solution.py:1044
  92.4 4.3 %collective-permute-start.21 = (bf16[512,128]{1,0:T(8,128)(2,1)S(1)}, bf16[512,128]{1,0:T(8,128)(2,1)S(1)}, u32[]{:S(2)}, u32[]{:S(2)}) collective-permute-start(bf16[512,128]{1,0:T(8,128)(2,1)S(1)} %bitcast.187), channel_id=1, source_target_pairs={{0,3},{1,0},{2,1},{3,2},{4,7},{5,4},{6,5},{7,6},{8,11},{9,8},{10,9... | collective-permute-start | bytes 393224 | tf_op jit(solution)/shard_map/ppermute | solution.py:1044
  96.8 4.9 %collective-permute-done.14.refs_9_ = bf16[512,128]{1,0:T(8,128)(2,1)S(1)} collective-permute-done((bf16[512,128]{1,0:T(8,128)(2,1)S(1)}, bf16[512,128]{1,0:T(8,128)(2,1)S(1)}, u32[]{:S(2)}, u32[]{:S(2)}) %collective-permute-start.14) | collective-permute-done | bytes 131104 | tf_op jit(solution)/shard_map/ppermute | solution.py:1044
  101.7 4.7 %collective-permute-start.23 = (bf16[512,128]{1,0:T(8,128)(2,1)S(1)}, bf16[512,128]{1,0:T(8,128)(2,1)S(1)}, u32[]{:S(2)}, u32[]{:S(2)}) collective-permute-start(bf16[512,128]{1,0:T(8,128)(2,1)S(1)} %bitcast.185), channel_id=1, source_target_pairs={{0,1},{1,2},{2,3},{3,0},{4,5},{5,6},{6,7},{7,4},{8,9},{9,10},{10,1... | collective-permute-start | bytes 393224 | tf_op jit(solution)/shard_map/ppermute | solution.py:1044
  106.4 39.9 %local_layer.2 = (bf16[512,128]{1,0:T(8,128)(2,1)}, bf16[512,128]{1,0:T(8,128)(2,1)}, bf16[512,128]{1,0:T(8,128)(2,1)}, bf16[512,128]{1,0:T(8,128)(2,1)}, bf16[4...) custom-call(s32[4,5]{1,0:T(4,128)} %get-tuple-element.381.refs_0_, ...), custom_call_target="tpu_custom_call" | custom-call | flops 41799999488 | bytes 24000000 | tf_op jit(solution)/shard_map/local_layer/pallas_call | solution.py:650
  146.3 3.1 collective-permute-start.18
  149.5 2.8 collective-permute-start.20
  153.1 39.9 %local_layer.3 = (bf16[512,128]{1,0:T(8,128)(2,1)}, bf16[512,128]{1,0:T(8,128)(2,1)}, bf16[512,128]{1,0:T(8,128)(2,1)}, bf16[512,128]{1,0:T(8,128)(2,1)}, bf16[4...) custom-call(s32[4,5]{1,0:T(4,128)} %get-tuple-element.380.refs_0_, ...), custom_call_target="tpu_custom_call" | custom-call | flops 41799999488 | bytes 24000000 | tf_op jit(solution)/shard_map/local_layer/pallas_call | solution.py:650
  193.7 11.1 %layer_grads.1 = (bf16[4,4,64,512]{3,2,1,0:T(8,128)(2,1)}, f32[4,4,64,512]{3,2,1,0:T(8,128)}, f32[4,4,16,512]{3,2,1,0:T(8,128)}, f32[4,4,16,512]{3,2,1,0:T(8,128...) custom-call(s32[1]{0:T(128)} %bitcast.7.refs_2_.me_ref, ...), custom_call_target="tpu_custom_call" | custom-call | flops 8800000000 | bytes 20000000 | tf_op jit(solution)/shard_map/layer_grads/pallas_call | solution.py:756
  207.9 3.2 collective-permute-done.30.refs_13_.refs_15_
  218.0 4.0 %split_add.4 = (bf16[2,4,64,512]{3,2,1,0:T(8,128)(2,1)}, f32[2,4,64,512]{3,2,1,0:T(8,128)S(1)}, f32[2,4,16,512]{3,2,1,0:T(8,128)}, f32[2,4,16,512]{3,2,1,0:T(8,1...) custom-call(f32[4,4,64,512]{3,2,1,0:T(8,128)S(1)} %copy-done, ...), custom_call_target="tpu_custom_call" | custom-call | flops 3300000000 | bytes 12000000 | tf_op jit(solution)/shard_map/split_add/pallas_call | solution.py:895
  226.2 12.1 %query_grads.1 = (bf16[8,128,128]{2,1,0:T(8,128)(2,1)S(1)}, bf16[8,128,128]{2,1,0:T(8,128)(2,1)S(1)}, bf16[8,128,128]{2,1,0:T(8,128)(2,1)S(1)}, bf16[8,128,128]{...) custom-call(f32[8192,128]{1,0:T(8,128)S(1)} %bitcast.172, ...), custom_call_target="tpu_custom_call" | custom-call | flops 12099999744 | bytes 7000000 | tf_op jit(solution)/shard_map/query_grads/pallas_call | solution.py:252
  252.6 8.0 %mode_grads.1 = (bf16[4,512,128]{2,1,0:T(8,128)(2,1)S(1)}, f32[4,512,128]{2,1,0:T(8,128)S(1)}, bf16[4,512,128]{2,1,0:T(8,128)(2,1)S(1)}, f32[4,512,128]{2,1,0:T(8,128)S(1)}) custom-call(s32[1]{0:T(128)} %bitcast.7.refs_2_.me_ref, bf16[64,32,256]{2,1,0:T(8,128)(2,1)S(1)} %copy-done.34, bf16[64,64,128]{2,1,0:T(8,128)(2,1)S(1)} %copy-done.32, ...), custom_call_target="tpu_custom_call" | custom-call | flops 9900000256 | bytes 8000000 | tf_op jit(solution)/shard_map/mode_grads/pallas_call | solution.py:319
  269.6 4.6 %query_weight_grads.1 = (bf16[4,4,64,128]{3,2,1,0:T(8,128)(2,1)}, f32[4,4,64,128]{3,2,1,0:T(8,128)}) custom-call(s32[1]{0:T(128)} %bitcast.7.refs_2_.me_ref, bf16[1024,512]{1,0:T(8,128)(2,1)} %refs_0_.1, bf16[4,1024,128]{2,1,0:T(8,128)(2,1)} %pad_maximum_fusion.2.refs_1_), custom_call_target="tpu_custom_call" | custom-call | flops 8800000000 | bytes 20000000 | tf_op jit(solution)/shard_map/query_weight_grads/pallas_call | solution.py:756
  280.4 3.5 collective-permute-done.38
  291.9 3.1 collective-permute-start.44
  295.6 3.7 collective-permute-done.51.refs_1_.refs_3_
  300.5 4.7 %collective-permute-done.43 = f32[64,512]{1,0:T(8,128)S(1)} collective-permute-done((f32[64,512]{1,0:T(8,128)S(1)}, f32[64,512]{1,0:T(8,128)S(1)}, u32[]{:S(2)}, u32[]{:S(2)}) %collective-permute-start.43) | collective-permute-done | bytes 131104 | tf_op jit(solution)/shard_map/ppermute | solution.py:1044
  307.4 4.7 %collective-permute-done.61 = bf16[1,4,128,128]{3,2,1,0:T(8,128)(2,1)S(1)} collective-permute-done((bf16[1,4,128,128]{3,2,1,0:T(8,128)(2,1)S(1)}, bf16[1,4,128,128]{3,2,1,0:T(8,128)(2,1)S(1)}, u32[]{:S(2)}, u32[]{:S(2)}) %collective-permute-start.61) | collective-permute-done | bytes 131104 | tf_op jit(solution)/shard_map/ppermute | solution.py:868
  313.7 3.8 collective-permute-start.57
  325.4 5.4 %collective-permute-done.63 = f32[2,128,512]{2,1,0:T(8,128)S(1)} collective-permute-done((f32[2,128,512]{2,1,0:T(8,128)S(1)}, f32[2,128,512]{2,1,0:T(8,128)S(1)}, u32[]{:S(2)}, u32[]{:S(2)}) %collective-permute-start.63) | collective-permute-done | bytes 524320 | tf_op jit(solution)/shard_map/ppermute | solution.py:868
  344.6 3.8 collective-permute-done.67
  351.5 8.8 %collective-permute-done.68 = f32[9,128]{1,0:T(8,128)S(1)} collective-permute-done((f32[9,128]{1,0:T(8,128)S(1)}, f32[9,128]{1,0:T(8,128)S(1)}, u32[]{:S(2)}, u32[]{:S(2)}) %collective-permute-start.68) | collective-permute-done | bytes 4640 | tf_op jit(solution)/shard_map/ppermute | solution.py:868
  360.3 3.6 collective-permute-done.69
  365.2 3.7 collective-permute-done.74
  375.8 19.7 %adam.1 = (f32[512,128]{1,0:T(8,128)}, f32[512,128]{1,0:T(8,128)}, f32[512,128]{1,0:T(8,128)}, f32[128,512]{1,0:T(8,128)}, f32[128,512]{1,0:T(8,128)}, /*index=5...) custom-call(s32[1]{0:T(128)} %bitcast.7.refs_2_.me_ref, ...), custom_call_target="tpu_custom_call" | custom-call | flops 16499999744 | bytes 48000000 | tf_op jit(solution)/shard_map/adam/pallas_call | solution.py:850
  (360 shorter events, 119.4 us)
Async XLA Ops:
  1.7 17.1 %collective-permute-start.2 = (bf16[512,128]{1,0:T(8,128)(2,1)S(1)}, bf16[512,128]{1,0:T(8,128)(2,1)S(1)}, u32[]{:S(2)}, u32[]{:S(2)}) collective-permute-start(bf16[512,128]{1,0:T(8,128)(2,1)S(1)} %convert_element_type.122.refs_0_), channel_id=1, source_target_pairs={{0,3},{1,0},{2,1},{3,2},{4,7},{5,4},{6,5},{7,6},{8,11},{9,8},{10,9... | collective-permute-start | bytes 393224 | tf_op jit(solution)/shard_map/ppermute | solution.py:1044
  20.6 21.7 %collective-permute-start.3 = (bf16[1024,128]{1,0:T(8,128)(2,1)S(1)}, bf16[1024,128]{1,0:T(8,128)(2,1)S(1)}, u32[]{:S(2)}, u32[]{:S(2)}) collective-permute-start(bf16[1024,128]{1,0:T(8,128)(2,1)S(1)} %get-tuple-element.192), channel_id=1, source_target_pairs={{0,1},{1,2},{2,3},{3,0},{4,5},{5,6},{6,7},{7,4},{8,9},{9,10},{10,1... | collective-permute-start | bytes 786440 | tf_op jit(solution)/shard_map/ppermute | solution.py:1044
  24.8 17.5 %collective-permute-start.5 = (bf16[144,512]{1,0:T(8,128)(2,1)S(1)}, bf16[144,512]{1,0:T(8,128)(2,1)S(1)}, u32[]{:S(2)}, u32[]{:S(2)}) collective-permute-start(bf16[144,512]{1,0:T(8,128)(2,1)S(1)} %fusion.7), channel_id=1, source_target_pairs={{0,2},{1,3},{2,0},{3,1},{4,6},{5,7},{6,4},{7,5},{8,10},{9,11},{10,... | collective-permute-start | bytes 442376 | tf_op jit(solution)/shard_map/ppermute | solution.py:1044
  24.9 17.3 %collective-permute-start.4 = (bf16[144,512]{1,0:T(8,128)(2,1)S(1)}, bf16[144,512]{1,0:T(8,128)(2,1)S(1)}, u32[]{:S(2)}, u32[]{:S(2)}) collective-permute-start(bf16[144,512]{1,0:T(8,128)(2,1)S(1)} %fusion.7), channel_id=1, source_target_pairs={{0,1},{1,2},{2,3},{3,0},{4,5},{5,6},{6,7},{7,4},{8,9},{9,10},{10,1... | collective-permute-start | bytes 442376 | tf_op jit(solution)/shard_map/ppermute | solution.py:1044
  43.0 17.1 %collective-permute-start.9 = (bf16[2,144,512]{2,1,0:T(8,128)(2,1)}, bf16[2,144,512]{2,1,0:T(8,128)(2,1)}, u32[]{:S(2)}, u32[]{:S(2)}) collective-permute-start(bf16[2,144,512]{2,1,0:T(8,128)(2,1)} %get-tuple-element.361), channel_id=1, source_target_pairs={{0,8},{4,12},{8,0},{12,4},{16,24},{20,28},{24,16},{28,20},{1,9},{5... | collective-permute-start | bytes 884744 | tf_op jit(solution)/shard_map/ppermute | solution.py:868
  45.3 14.8 %collective-permute-start.10 = (bf16[2,144,512]{2,1,0:T(8,128)(2,1)}, bf16[2,144,512]{2,1,0:T(8,128)(2,1)S(1)}, u32[]{:S(2)}, u32[]{:S(2)}) collective-permute-start(bf16[2,144,512]{2,1,0:T(8,128)(2,1)} %get-tuple-element.359), channel_id=1, source_target_pairs={{0,16},{4,20},{8,24},{12,28},{16,0},{20,4},{24,8},{28,12},{1,17},{... | collective-permute-start | bytes 884744 | tf_op jit(solution)/shard_map/ppermute | solution.py:868
  61.9 18.3 %collective-permute-start.11 = (bf16[2,2,144,512]{3,2,1,0:T(8,128)(2,1)S(1)}, bf16[2,2,144,512]{3,2,1,0:T(8,128)(2,1)S(1)}, u32[]{:S(2)}, u32[]{:S(2)}) collective-permute-start(bf16[2,2,144,512]{3,2,1,0:T(8,128)(2,1)S(1)} %get-tuple-element.347), channel_id=1, source_target_pairs={{0,16},{4,20},{8,24},{12,28},{16,0},{20,4},{24,8},{28,12},{1,17},{... | collective-permute-start | bytes 1769480 | tf_op jit(solution)/shard_map/ppermute | solution.py:868
  62.5 17.7 %collective-permute-start.12 = (bf16[2,2,144,512]{3,2,1,0:T(8,128)(2,1)S(1)}, bf16[2,2,144,512]{3,2,1,0:T(8,128)(2,1)S(1)}, u32[]{:S(2)}, u32[]{:S(2)}) collective-permute-start(bf16[2,2,144,512]{3,2,1,0:T(8,128)(2,1)S(1)} %get-tuple-element.345), channel_id=1, source_target_pairs={{0,8},{4,12},{8,0},{12,4},{16,24},{20,28},{24,16},{28,20},{1,9},{5... | collective-permute-start | bytes 1769480 | tf_op jit(solution)/shard_map/ppermute | solution.py:868
  81.7 24.7 %collective-permute-start.17 = (bf16[4,2,144,512]{3,2,1,0:T(8,128)(2,1)}, bf16[4,2,144,512]{3,2,1,0:T(8,128)(2,1)}, u32[]{:S(2)}, u32[]{:S(2)}) collective-permute-start(bf16[4,2,144,512]{3,2,1,0:T(8,128)(2,1)} %bitcast.32.refs_13_), channel_id=1, source_target_pairs={{0,4},{4,0},{8,12},{12,8},{16,20},{20,16},{24,28},{28,24},{1,5},{5... | collective-permute-start | bytes 3538952 | tf_op jit(solution)/shard_map/ppermute | solution.py:868
  81.9 24.5 %collective-permute-start.16 = (bf16[4,2,144,512]{3,2,1,0:T(8,128)(2,1)S(1)}, bf16[4,2,144,512]{3,2,1,0:T(8,128)(2,1)}, u32[]{:S(2)}, u32[]{:S(2)}) collective-permute-start(bf16[4,2,144,512]{3,2,1,0:T(8,128)(2,1)S(1)} %bitcast.210), channel_id=1, source_target_pairs={{0,4},{4,0},{8,12},{12,8},{16,20},{20,16},{24,28},{28,24},{1,5},{5... | collective-permute-start | bytes 3538952 | tf_op jit(solution)/shard_map/ppermute | solution.py:868
  92.4 57.1 %collective-permute-start.21 = (bf16[512,128]{1,0:T(8,128)(2,1)S(1)}, bf16[512,128]{1,0:T(8,128)(2,1)S(1)}, u32[]{:S(2)}, u32[]{:S(2)}) collective-permute-start(bf16[512,128]{1,0:T(8,128)(2,1)S(1)} %bitcast.187), channel_id=1, source_target_pairs={{0,3},{1,0},{2,1},{3,2},{4,7},{5,4},{6,5},{7,6},{8,11},{9,8},{10,9... | collective-permute-start | bytes 393224 | tf_op jit(solution)/shard_map/ppermute | solution.py:1044
  101.7 50.7 %collective-permute-start.22 = (bf16[512,128]{1,0:T(8,128)(2,1)S(1)}, bf16[512,128]{1,0:T(8,128)(2,1)S(1)}, u32[]{:S(2)}, u32[]{:S(2)}) collective-permute-start(bf16[512,128]{1,0:T(8,128)(2,1)S(1)} %bitcast.186), channel_id=1, source_target_pairs={{0,2},{1,3},{2,0},{3,1},{4,6},{5,7},{6,4},{7,5},{8,10},{9,11},{10,... | collective-permute-start | bytes 393224 | tf_op jit(solution)/shard_map/ppermute | solution.py:1044
  101.7 50.7 %collective-permute-start.23 = (bf16[512,128]{1,0:T(8,128)(2,1)S(1)}, bf16[512,128]{1,0:T(8,128)(2,1)S(1)}, u32[]{:S(2)}, u32[]{:S(2)}) collective-permute-start(bf16[512,128]{1,0:T(8,128)(2,1)S(1)} %bitcast.185), channel_id=1, source_target_pairs={{0,1},{1,2},{2,3},{3,0},{4,5},{5,6},{6,7},{7,4},{8,9},{9,10},{10,1... | collective-permute-start | bytes 393224 | tf_op jit(solution)/shard_map/ppermute | solution.py:1044
  146.3 46.7 %collective-permute-start.18 = (bf16[512,128]{1,0:T(8,128)(2,1)}, bf16[512,128]{1,0:T(8,128)(2,1)S(1)}, u32[]{:S(2)}, u32[]{:S(2)}) collective-permute-start(bf16[512,128]{1,0:T(8,128)(2,1)} %get-tuple-element.221), channel_id=1, source_target_pairs={{0,1},{1,2},{2,3},{3,0},{4,5},{5,6},{6,7},{7,4},{8,9},{9,10},{10,1... | collective-permute-start | bytes 393224 | tf_op jit(solution)/shard_map/ppermute | solution.py:1044
  149.5 43.6 %collective-permute-start.19 = (bf16[512,128]{1,0:T(8,128)(2,1)}, bf16[512,128]{1,0:T(8,128)(2,1)S(1)}, u32[]{:S(2)}, u32[]{:S(2)}) collective-permute-start(bf16[512,128]{1,0:T(8,128)(2,1)} %get-tuple-element.222), channel_id=1, source_target_pairs={{0,2},{1,3},{2,0},{3,1},{4,6},{5,7},{6,4},{7,5},{8,10},{9,11},{10,... | collective-permute-start | bytes 393224 | tf_op jit(solution)/shard_map/ppermute | solution.py:1044
  149.5 43.5 %collective-permute-start.20 = (bf16[512,128]{1,0:T(8,128)(2,1)}, bf16[512,128]{1,0:T(8,128)(2,1)S(1)}, u32[]{:S(2)}, u32[]{:S(2)}) collective-permute-start(bf16[512,128]{1,0:T(8,128)(2,1)} %get-tuple-element.223), channel_id=1, source_target_pairs={{0,3},{1,0},{2,1},{3,2},{4,7},{5,4},{6,5},{7,6},{8,11},{9,8},{10,9... | collective-permute-start | bytes 393224 | tf_op jit(solution)/shard_map/ppermute | solution.py:1044
  206.5 18.6 %collective-permute-start.24 = (bf16[512,128]{1,0:T(8,128)(2,1)}, bf16[512,128]{1,0:T(8,128)(2,1)S(1)}, u32[]{:S(2)}, u32[]{:S(2)}) collective-permute-start(bf16[512,128]{1,0:T(8,128)(2,1)} %get-tuple-element.229), channel_id=1, source_target_pairs={{0,1},{1,2},{2,3},{3,0},{4,5},{5,6},{6,7},{7,4},{8,9},{9,10},{10,1... | collective-permute-start | bytes 393224 | tf_op jit(solution)/shard_map/ppermute | solution.py:1044
  211.2 15.0 %collective-permute-start.26 = (bf16[512,128]{1,0:T(8,128)(2,1)}, bf16[512,128]{1,0:T(8,128)(2,1)S(1)}, u32[]{:S(2)}, u32[]{:S(2)}) collective-permute-start(bf16[512,128]{1,0:T(8,128)(2,1)} %get-tuple-element.231), channel_id=1, source_target_pairs={{0,3},{1,0},{2,1},{3,2},{4,7},{5,4},{6,5},{7,6},{8,11},{9,8},{10,9... | collective-permute-start | bytes 393224 | tf_op jit(solution)/shard_map/ppermute | solution.py:1044
  222.0 20.2 %collective-permute-start.34 = (bf16[2,4,16,512]{3,2,1,0:T(8,128)(2,1)}, bf16[2,4,16,512]{3,2,1,0:T(8,128)(2,1)S(1)}, u32[]{:S(2)}, u32[]{:S(2)}) collective-permute-start(bf16[2,4,16,512]{3,2,1,0:T(8,128)(2,1)} %get-tuple-element.262), channel_id=1, source_target_pairs={{0,16},{4,20},{8,24},{12,28},{16,0},{20,4},{24,8},{28,12},{1,17},{... | collective-permute-start | bytes 393224 | tf_op jit(solution)/shard_map/ppermute | solution.py:868
  223.6 18.7 %collective-permute-start.32 = (f32[2,4,16,512]{3,2,1,0:T(8,128)}, f32[2,4,16,512]{3,2,1,0:T(8,128)S(1)}, u32[]{:S(2)}, u32[]{:S(2)}) collective-permute-start(f32[2,4,16,512]{3,2,1,0:T(8,128)} %get-tuple-element.260), channel_id=1, source_target_pairs={{0,8},{4,12},{8,0},{12,4},{16,24},{20,28},{24,16},{28,20},{1,9},{5... | collective-permute-start | bytes 786440 | tf_op jit(solution)/shard_map/ppermute | solution.py:868
  225.1 18.3 %collective-permute-start.31 = (bf16[2,4,64,512]{3,2,1,0:T(8,128)(2,1)}, bf16[2,4,64,512]{3,2,1,0:T(8,128)(2,1)S(1)}, u32[]{:S(2)}, u32[]{:S(2)}) collective-permute-start(bf16[2,4,64,512]{3,2,1,0:T(8,128)(2,1)} %get-tuple-element.259), channel_id=1, source_target_pairs={{0,8},{4,12},{8,0},{12,4},{16,24},{20,28},{24,16},{28,20},{1,9},{5... | collective-permute-start | bytes 1572872 | tf_op jit(solution)/shard_map/ppermute | solution.py:868
  225.6 18.5 %collective-permute-start.33 = (f32[2,4,48,512]{3,2,1,0:T(8,128)}, f32[2,4,48,512]{3,2,1,0:T(8,128)S(1)}, u32[]{:S(2)}, u32[]{:S(2)}) collective-permute-start(f32[2,4,48,512]{3,2,1,0:T(8,128)} %get-tuple-element.261), channel_id=1, source_target_pairs={{0,16},{4,20},{8,24},{12,28},{16,0},{20,4},{24,8},{28,12},{1,17},{... | collective-permute-start | bytes 2359304 | tf_op jit(solution)/shard_map/ppermute | solution.py:868
  239.3 21.2 %collective-permute-start.45 = (bf16[1024,128]{1,0:T(8,128)(2,1)S(1)}, bf16[1024,128]{1,0:T(8,128)(2,1)}, u32[]{:S(2)}, u32[]{:S(2)}) collective-permute-start(bf16[1024,128]{1,0:T(8,128)(2,1)S(1)} %bitcast.179), channel_id=1, source_target_pairs={{0,3},{1,0},{2,1},{3,2},{4,7},{5,4},{6,5},{7,6},{8,11},{9,8},{10,9... | collective-permute-start | bytes 786440 | tf_op jit(solution)/shard_map/ppermute | solution.py:1044
  242.3 20.6 %collective-permute-start.46 = (bf16[1024,128]{1,0:T(8,128)(2,1)S(1)}, bf16[1024,128]{1,0:T(8,128)(2,1)S(1)}, u32[]{:S(2)}, u32[]{:S(2)}) collective-permute-start(bf16[1024,128]{1,0:T(8,128)(2,1)S(1)} %bitcast.178), channel_id=1, source_target_pairs={{0,2},{1,3},{2,0},{3,1},{4,6},{5,7},{6,4},{7,5},{8,10},{9,11},{10,... | collective-permute-start | bytes 786440 | tf_op jit(solution)/shard_map/ppermute | solution.py:1044
  242.3 20.6 %collective-permute-start.47 = (bf16[1024,128]{1,0:T(8,128)(2,1)S(1)}, bf16[1024,128]{1,0:T(8,128)(2,1)S(1)}, u32[]{:S(2)}, u32[]{:S(2)}) collective-permute-start(bf16[1024,128]{1,0:T(8,128)(2,1)S(1)} %bitcast.177), channel_id=1, source_target_pairs={{0,1},{1,2},{2,3},{3,0},{4,5},{5,6},{6,7},{7,4},{8,9},{9,10},{10,1... | collective-permute-start | bytes 786440 | tf_op jit(solution)/shard_map/ppermute | solution.py:1044
  249.5 16.0 %collective-permute-start.36 = (bf16[1,4,16,512]{3,2,1,0:T(8,128)(2,1)S(1)}, bf16[1,4,16,512]{3,2,1,0:T(8,128)(2,1)S(1)}, u32[]{:S(2)}, u32[]{:S(2)}) collective-permute-start(bf16[1,4,16,512]{3,2,1,0:T(8,128)(2,1)S(1)} %get-tuple-element.266), channel_id=1, source_target_pairs={{0,8},{4,12},{8,0},{12,4},{16,24},{20,28},{24,16},{28,20},{1,9},{5... | collective-permute-start | bytes 196616 | tf_op jit(solution)/shard_map/ppermute | solution.py:868
  251.0 23.3 %collective-permute-start.40 = (f32[1,4,16,512]{3,2,1,0:T(8,128)S(1)}, f32[1,4,16,512]{3,2,1,0:T(8,128)}, u32[]{:S(2)}, u32[]{:S(2)}) collective-permute-start(f32[1,4,16,512]{3,2,1,0:T(8,128)S(1)} %get-tuple-element.268), channel_id=1, source_target_pairs={{0,16},{4,20},{8,24},{12,28},{16,0},{20,4},{24,8},{28,12},{1,17},{... | collective-permute-start | bytes 393224 | tf_op jit(solution)/shard_map/ppermute | solution.py:868
  262.9 22.0 %collective-permute-start.48 = (bf16[4,4,128,128]{3,2,1,0:T(8,128)(2,1)S(1)}, bf16[4,4,128,128]{3,2,1,0:T(8,128)(2,1)S(1)}, u32[]{:S(2)}, u32[]{:S(2)}) collective-permute-start(bf16[4,4,128,128]{3,2,1,0:T(8,128)(2,1)S(1)} %bitcast.175), channel_id=1, source_target_pairs={{0,4},{4,0},{8,12},{12,8},{16,20},{20,16},{24,28},{28,24},{1,5},{5... | collective-permute-start | bytes 1572872 | tf_op jit(solution)/shard_map/ppermute | solution.py:868
  262.9 22.1 %collective-permute-start.49 = (bf16[4,4,128,128]{3,2,1,0:T(8,128)(2,1)S(1)}, bf16[4,4,128,128]{3,2,1,0:T(8,128)(2,1)S(1)}, u32[]{:S(2)}, u32[]{:S(2)}) collective-permute-start(bf16[4,4,128,128]{3,2,1,0:T(8,128)(2,1)S(1)} %bitcast.174), channel_id=1, source_target_pairs={{0,4},{4,0},{8,12},{12,8},{16,20},{20,16},{24,28},{28,24},{1,5},{5... | collective-permute-start | bytes 1572872 | tf_op jit(solution)/shard_map/ppermute | solution.py:868
  348.5 15.7 %collective-permute-start.73 = (f32[4,128,512]{2,1,0:T(8,128)S(1)}, f32[4,128,512]{2,1,0:T(8,128)S(1)}, u32[]{:S(2)}, u32[]{:S(2)}) collective-permute-start(f32[4,128,512]{2,1,0:T(8,128)S(1)} %bitcast.214), channel_id=1, source_target_pairs={{0,4},{4,0},{8,12},{12,8},{16,20},{20,16},{24,28},{28,24},{1,5},{5... | collective-permute-start | bytes 3145736 | tf_op jit(solution)/shard_map/ppermute | solution.py:868
  348.6 15.7 %collective-permute-start.72 = (f32[4,128,512]{2,1,0:T(8,128)S(1)}, f32[4,128,512]{2,1,0:T(8,128)S(1)}, u32[]{:S(2)}, u32[]{:S(2)}) collective-permute-start(f32[4,128,512]{2,1,0:T(8,128)S(1)} %bitcast.216), channel_id=1, source_target_pairs={{0,4},{4,0},{8,12},{12,8},{16,20},{20,16},{24,28},{28,24},{1,5},{5... | collective-permute-start | bytes 3145736 | tf_op jit(solution)/shard_map/ppermute | solution.py:868
  349.1 15.1 %collective-permute-start.71 = (f32[2,96,512]{2,1,0:T(8,128)S(1)}, f32[2,96,512]{2,1,0:T(8,128)S(1)}, u32[]{:S(2)}, u32[]{:S(2)}) collective-permute-start(f32[2,96,512]{2,1,0:T(8,128)S(1)} %pad_maximum_fusion.12), channel_id=1, source_target_pairs={{0,16},{4,20},{8,24},{12,28},{16,0},{20,4},{24,8},{28,12},{1,17},{... | collective-permute-start | bytes 1179656 | tf_op jit(solution)/shard_map/ppermute | solution.py:868
  (112 other events, 835.3 us)

commit v4 on v3

--- a/solution.py
+++ b/solution.py
@@ -25,6 +25,8 @@
 BF = jnp.bfloat16
 F32 = jnp.float32
 MIB = 1 << 20
+CHUNK = 128
+UNROLL = 1
 
 ERF_P = 0.3275911
 ERF_A = (0.254829592, -0.284496736, 1.421413741, -1.453152027, 1.061405429)
@@ -269,8 +271,8 @@
 
 
 def mode_grad_kernel(me_ref, dy_ref, xs_ref, *refs):
-    outs = refs[-7:-3]
-    dw_scr, low_scr, sems = refs[-3:]
+    outs = refs[-6:-2]
+    dw_scr, sems = refs[-2:]
     pieces, depth = 2 * outs[0].shape[0], outs[0].shape[1]
     total = HEAD_DIM * MODES
     low = lane_low(HEAD_DIM)
@@ -292,17 +294,13 @@
         return 0
 
     lax.fori_loop(0, MODES, mix, 0, unroll=4)
-    for j in range(1, pieces, 2):
-        for c in range(2):
-            start = pl.multiple_of(c * total + (me ^ j) * depth, depth)
-            low_scr[c, j // 2] = dw_scr[pl.ds(start, depth), :].astype(BF)
     copies = []
     for j in range(pieces):
         for c in range(2):
             start = pl.multiple_of(c * total + (me ^ j) * depth, depth)
             copies.append(
                 pltpu.make_async_copy(
-                    low_scr.at[c, j // 2] if j % 2 else dw_scr.at[pl.ds(start, depth), :],
+                    dw_scr.at[pl.ds(start, depth), :],
                     outs[2 * c + (j + 1) % 2].at[j // 2],
                     sems.at[c, j],
                 )
@@ -322,10 +320,9 @@
         + [whole] * 2
         + [pl.BlockSpec(memory_space=pl.ANY)] * len(waits),
         out_specs=[pl.BlockSpec(memory_space=pl.ANY)] * 4,
-        out_shape=[jax.ShapeDtypeStruct(part.shape, BF), part] * 2,
+        out_shape=[part] * 4,
         scratch_shapes=[
             pltpu.VMEM((2 * HEAD_DIM * MODES, LANES), F32),
-            pltpu.VMEM((2,) + part.shape, BF),
             pltpu.SemaphoreType.DMA((2, pieces)),
         ],
         compiler_params=pltpu.CompilerParams(vmem_limit_bytes=40 * MIB),
@@ -404,27 +401,29 @@
     groups = d // LANES
     loops = SEQ_LEN // chunk
 
-    @pl.when(step == 0)
-    def _():
+    def weight_copies():
         count, shared, part, _ = packed_refs[0].shape
-        copies = []
         for number, ref in enumerate(packed_refs):
             group, bit = number // 2, number % 2
             for k in range(count):
                 for r in range(shared):
                     row = pl.multiple_of((me_ref[0] ^ (2 * k + bit)) * part, part)
-                    copies.append(
-                        pltpu.make_async_copy(
-                            ref.at[k, r],
-                            weights.at[(heads - group * shared - r) % heads, pl.ds(row, part), :],
-                            weight_sems.at[number, k * shared + r],
-                        )
+                    yield pltpu.make_async_copy(
+                        ref.at[k, r],
+                        weights.at[(heads - group * shared - r) % heads, pl.ds(row, part), :],
+                        weight_sems.at[number, k * shared + r],
                     )
-        for copy in copies:
+
+    @pl.when(step == 0)
+    def _():
+        for copy in weight_copies():
             copy.start()
         sums_ref[...] = jnp.zeros_like(sums_ref)
-        for copy in copies:
-            copy.wait()
+
+    def repeat(body, start):
+        if loops == 1:
+            return body(0, start)
+        return lax.fori_loop(0, loops, body, start, unroll=UNROLL)
 
     row_ids = lax.broadcasted_iota(jnp.int32, (SEQ_LEN, SEQ_LEN), 0)
     col_ids = lax.broadcasted_iota(jnp.int32, (SEQ_LEN, SEQ_LEN), 1)
@@ -439,6 +438,11 @@
             at_scr[c, :, w * SEQ_LEN : (w + 1) * SEQ_LEN] = window_counts(
                 first_t, last_t, col_ids, row_ids, width
             ).astype(BF)
+
+    @pl.when(step == 0)
+    def _():
+        for copy in weight_copies():
+            copy.wait()
 
     def averages(c, u, av):
         high = u.astype(BF)
@@ -496,7 +500,7 @@
             lanes = slice(g * LANES, (g + 1) * LANES)
 
             def first_pass(r, _, c=c, lanes=lanes):
-                row = pl.multiple_of(r * chunk, chunk)
+                row = r * chunk if loops == 1 else pl.multiple_of(r * chunk, chunk)
                 at = pl.ds(c * SEQ_LEN + row, chunk)
                 u = u_scr[at, lanes]
                 avs = read_averages(av1_scr, c, row, lanes)
@@ -509,7 +513,7 @@
                 low_ref[at, lanes] = season.astype(BF)
                 return 0
 
-            lax.fori_loop(0, loops, first_pass, 0)
+            repeat(first_pass, 0)
 
     season_low = low_ref[...]
     feed = jnp.zeros((rows, d), F32)
@@ -538,7 +542,7 @@
             lanes = slice(g * LANES, (g + 1) * LANES)
 
             def second_pass(r, sums, c=c, lanes=lanes):
-                row = pl.multiple_of(r * chunk, chunk)
+                row = r * chunk if loops == 1 else pl.multiple_of(r * chunk, chunk)
                 at = pl.ds(c * SEQ_LEN + row, chunk)
                 u = g_scr[at, lanes]
                 avs = read_averages(av2_scr, c, row, lanes)
@@ -554,7 +558,7 @@
                 return tuple(new) + (sums[2 * KERNELS] + fold(weighted * misfit),)
 
             zeros = tuple(jnp.zeros((8, LANES), F32) for _ in range(2 * KERNELS + 1))
-            sums = lax.fori_loop(0, loops, second_pass, zeros)
+            sums = repeat(second_pass, zeros)
             for k in range(KERNELS):
                 sums_ref[SUM_SLOPE[1] + k, :, lanes] += sums[k]
                 sums_ref[SUM_OFFSET[1] + k, :, lanes] += sums[KERNELS + k]
@@ -579,7 +583,7 @@
             lanes = slice(g * LANES, (g + 1) * LANES)
 
             def third_pass(r, sums, c=c, lanes=lanes):
-                row = pl.multiple_of(r * chunk, chunk)
+                row = r * chunk if loops == 1 else pl.multiple_of(r * chunk, chunk)
                 at = pl.ds(c * SEQ_LEN + row, chunk)
                 u = u_scr[at, lanes]
                 avs = read_averages(av1_scr, c, row, lanes)
@@ -604,7 +608,7 @@
                 return tuple(new)
 
             zeros = tuple(jnp.zeros((8, LANES), F32) for _ in range(2 * KERNELS))
-            sums = lax.fori_loop(0, loops, third_pass, zeros)
+            sums = repeat(third_pass, zeros)
             for k in range(KERNELS):
                 sums_ref[SUM_SLOPE[0] + k, :, lanes] += sums[k]
                 sums_ref[SUM_OFFSET[0] + k, :, lanes] += sums[KERNELS + k]
@@ -648,7 +652,7 @@
 
     ctx_half = starts.shape[0] // 2
     res = pl.pallas_call(
-        partial(local_kernel, chunk=16, hidden_width=hidden, heads=heads, waits=len(waits)),
+        partial(local_kernel, chunk=CHUNK, hidden_width=hidden, heads=heads, waits=len(waits)),
         grid=(steps,),
         in_specs=[smem] * 3
         + [row_block(d, number), row_block(d, number), row_block(1, number), whole]
@@ -683,7 +687,7 @@
             pltpu.SemaphoreType.DMA((len(packed), count * shared)),
         ],
         compiler_params=pltpu.CompilerParams(vmem_limit_bytes=56 * MIB),
-        cost_estimate=cost(38, 24e6),
+        cost_estimate=cost(26, 24e6),
         name="local_layer",
     )(
         starts[number * ctx_half : (number + 1) * ctx_half],
@@ -770,7 +774,7 @@
         out_shape=shapes,
         scratch_shapes=[pltpu.VMEM((rows, columns), F32)],
         compiler_params=pltpu.CompilerParams(vmem_limit_bytes=60 * MIB),
-        cost_estimate=cost(8, 20e6),
+        cost_estimate=cost(0.3, 1e5),
         name=name,
     )(me, *operands, *waits)
     return [(res[2 * k], res[2 * k + 1]) for k in range(len(res) // 2)]
@@ -899,7 +903,7 @@
         out_specs=out_specs,
         out_shape=shapes,
         compiler_params=pltpu.CompilerParams(vmem_limit_bytes=24 * MIB),
-        cost_estimate=cost(3, 12e6),
+        cost_estimate=cost(0.3, 1e5),
         name="split_add",
     )(*operands)
     return [(res[2 * k], res[2 * k + 1]) for k in range(len(items))]
@@ -1095,6 +1099,7 @@
     packed.finish()
     packed = [half for pair in packed.pairs() for half in pair]
     first = send([rows_of(v) for v in first], -1)
+    first, second = together(first, second)
     second = send([rows_of(v) for v in second], -1)
 
     half_call = partial(
@@ -1127,7 +1132,7 @@
             list(zip(active, d_feed)),
             list(zip(spectrum, d_attention)),
         ],
-        [[(d // ndp, BF)], down_cuts, [(out_part, BF)]],
+        [[(d // ndp, BF)], down_cuts, [(out_part, F32)]],
         ndp,
         "layer_grads",
         d_first[1:],
@@ -1155,9 +1160,11 @@
         ndp,
         "query_weight_grads",
     )
-    late = Reduction(
-        [mode_parts[:2], mode_parts[2:], *query], [order_a, order_b, order_a], ndp
-    )
+    query = Reduction(query, [order_a], ndp)
+    query.split()
+    modes = Reduction([mode_parts[:2], mode_parts[2:]], [order_a, order_b], ndp)
+    query.got, modes.got = together(query.got, modes.got)
+    modes.split()
 
     def over_heads(v, kind=F32):
         parts = send([v[r].astype(kind) for r in range(nhead)])
@@ -1165,14 +1172,11 @@
 
     lanes = HEAD_DIM * MODES // ndp
     up_piece, *down_pieces, out_piece = layer.rest()
-    down_piece = over_heads(jnp.concatenate(down_pieces, axis=1))
-    if hidden == d and out_part % 8 == 0:
-        both_pieces = over_heads(jnp.concatenate([up_piece, out_piece], axis=1), BF)
-        up_piece, out_piece = both_pieces[: d // ndp], both_pieces[d // ndp :]
-    else:
-        up_piece, out_piece = over_heads(up_piece, BF), over_heads(out_piece, BF)[:out_part]
-    *mode_pieces, query_piece = late.rest()
-    query_piece = over_heads(query_piece, BF)
+    down_piece = over_heads(jnp.concatenate([*down_pieces, out_piece], axis=1))
+    down_piece, out_piece = down_piece[:hidden_part], down_piece[hidden_part:][:out_part]
+    up_piece = over_heads(up_piece, BF)
+    (query_piece,) = [over_heads(v, BF) for v in query.rest()]
+    mode_pieces = modes.rest()
     mode_pieces = [v.reshape(lanes, LANES).T[: own_heads * HEAD_DIM] for v in mode_pieces]
     mode_all = Gathering(mode_pieces, [order_b, order_a], ndp)
     mode_all.across()

time: 398 us -> 374 us (0.940); the launches traced: 397 us -> 368 us
  Pallas kernels: 159 us -> 133 us
  waiting for transfers between devices: 95.5 us -> 87.5 us
    pallas_call x2, Pallas kernels: 79.8 us -> 50.6 us  [local_call(): pl.pallas_call(partial(local_kernel, chunk=CHUNK, hidden_width=hidden, he...]
    ppermute x44, starting transfers between devices: 30 us -> 38.3 us  [swap(): return lax.ppermute(value, axis, [(i, i ^ 1 << bit) for i in range(size)])]
    ppermute x33, waiting for transfers between devices: 48 us -> 41.3 us  [shift(): return lax.ppermute(v, 'head', [(i, (i + r) % nhead) for i in range(nhead)])]
    ppermute x33, starting transfers between devices: 50.7 us -> 45.7 us  [shift(): return lax.ppermute(v, 'head', [(i, (i + r) % nhead) for i in range(nhead)])]
    pallas_call x4 -> x6, Pallas kernels: 7.23 us -> 10.1 us  [split_add(): pl.pallas_call(body, grid=(half, splits), in_specs=specs, out_specs=out_s...]
    unnamed x133 -> x141, local copies, waits for them, and re-layouts: 19.1 us -> 19.7 us
  transfers between devices with their start and end apart: 77 -> 77, of which waited for: 26 -> 24; matrix products, arithmetic and copies ran while one was open for 7% -> 8% of each run, Pallas kernels for 32% -> 27%
where the time goes in v4:
time: 374 us; the launch traced here: 368 us
  Pallas kernels  133 us (36%)
  waiting for transfers between devices  87.5 us (23%)
  starting transfers between devices  84 us (22%)
  local copies, waits for them, and re-layouts  30.1 us (8%)
  other arithmetic  23.3 us (6%)
  between operations  10 us (3%)
    pallas_call x2, Pallas kernels, local_call(): pl.pallas_call(partial(local_kernel, chunk=CHUNK, hidden_width=hidden, he...  50.6 us
    ppermute x44, waiting for transfers between devices, swap(): return lax.ppermute(value, axis, [(i, i ^ 1 << bit) for i in range(size)])  46.2 us
    ppermute x33, starting transfers between devices, shift(): return lax.ppermute(v, 'head', [(i, (i + r) % nhead) for i in range(nhead)])  45.7 us
    ppermute x33, waiting for transfers between devices, shift(): return lax.ppermute(v, 'head', [(i, (i + r) % nhead) for i in range(nhead)])  41.3 us
    ppermute x44, starting transfers between devices, swap(): return lax.ppermute(value, axis, [(i, i ^ 1 << bit) for i in range(size)])  38.3 us
    pallas_call x1, Pallas kernels, adam_call(): pl.pallas_call(partial(adam_kernel, views=views, leads=leads, grads=len(g...  19.7 us
    unnamed x141, local copies, waits for them, and re-layouts  19.7 us
    pallas_call x2, Pallas kernels, outer_call(): pl.pallas_call(partial(outer_kernel, halves=[len(p) for p in products], o...  15.8 us
  transfers between devices with their start and end apart: 77, of which 24 were waited for; matrix products, arithmetic and copies ran while one was open for 8% of the time, Pallas kernels for 27%

profile of v4, /device:TPU:0, one launch (start us, length us, event | category | flops | bytes accessed | tf_op | source)
XLA Modules:
  0.0 367.7 jit_solution(10695976283948950296)
XLA Ops:
  1.7 5.1 %collective-permute-start.2 = (bf16[512,128]{1,0:T(8,128)(2,1)S(1)}, bf16[512,128]{1,0:T(8,128)(2,1)S(1)}, u32[]{:S(2)}, u32[]{:S(2)}) collective-permute-start(bf16[512,128]{1,0:T(8,128)(2,1)S(1)} %convert_element_type.111.refs_0_), channel_id=1, source_target_pairs={{0,3},{1,0},{2,1},{3,2},{4,7},{5,4},{6,5},{7,6},{8,11},{9,8},{10,9... | collective-permute-start | bytes 393224 | tf_op jit(solution)/shard_map/ppermute | solution.py:1048
  14.1 5.7 %copy.86 = f32[2,128,4096]{1,2,0:T(8,128)} copy(f32[2,128,4096]{2,1,0:T(8,128)} %bitcast.199) | data formatting | bytes 8388608 | tf_op jit(solution)/shard_map/reshape | solution.py:1068
  22.2 2.5 collective-permute-start.3
  28.0 6.7 %collective-permute-done.6 = bf16[144,512]{1,0:T(8,128)(2,1)S(1)} collective-permute-done((bf16[144,512]{1,0:T(8,128)(2,1)S(1)}, bf16[144,512]{1,0:T(8,128)(2,1)S(1)}, u32[]{:S(2)}, u32[]{:S(2)}) %collective-permute-start.6) | collective-permute-done | bytes 147488 | tf_op jit(solution)/shard_map/ppermute | solution.py:1048
  34.7 9.2 %collective-permute-done.5 = bf16[144,512]{1,0:T(8,128)(2,1)S(1)} collective-permute-done((bf16[144,512]{1,0:T(8,128)(2,1)S(1)}, bf16[144,512]{1,0:T(8,128)(2,1)S(1)}, u32[]{:S(2)}, u32[]{:S(2)}) %collective-permute-start.5) | collective-permute-done | bytes 147488 | tf_op jit(solution)/shard_map/ppermute | solution.py:1048
  48.9 9.9 %collective-permute-done.7 = bf16[1024,128]{1,0:T(8,128)(2,1)S(1)} collective-permute-done((bf16[1024,128]{1,0:T(8,128)(2,1)S(1)}, bf16[1024,128]{1,0:T(8,128)(2,1)S(1)}, u32[]{:S(2)}, u32[]{:S(2)}) %collective-permute-start.7) | collective-permute-done | bytes 262176 | tf_op jit(solution)/shard_map/ppermute | solution.py:1048
  58.8 2.3 collective-permute-done.8
  62.5 2.2 copy-done.2
  64.6 14.8 %spectrum.1 = (bf16[4,128,128]{2,1,0:T(8,128)(2,1)S(1)}, bf16[4,128,128]{2,1,0:T(8,128)(2,1)S(1)}, bf16[4,128,128]{2,1,0:T(8,128)(2,1)S(1)}, bf16[4,128,128]{2,1...) custom-call(f32[8192,128]{1,0:T(8,128)S(1)} %bitcast.169, ...), custom_call_target="tpu_custom_call" | custom-call | flops 16499999744 | bytes 7000000 | tf_op jit(solution)/shard_map/spectrum/pallas_call | solution.py:166
  83.3 4.9 %collective-permute-start.13 = (bf16[512,128]{1,0:T(8,128)(2,1)S(1)}, bf16[512,128]{1,0:T(8,128)(2,1)S(1)}, u32[]{:S(2)}, u32[]{:S(2)}) collective-permute-start(bf16[512,128]{1,0:T(8,128)(2,1)S(1)} %bitcast.193), channel_id=1, source_target_pairs={{0,3},{1,0},{2,1},{3,2},{4,7},{5,4},{6,5},{7,6},{8,11},{9,8},{10,9... | collective-permute-start | bytes 393224 | tf_op jit(solution)/shard_map/ppermute | solution.py:1048
  89.3 2.8 collective-permute-done.13.refs_8_
  92.1 8.3 %collective-permute-done.14.refs_9_ = bf16[512,128]{1,0:T(8,128)(2,1)S(1)} collective-permute-done((bf16[512,128]{1,0:T(8,128)(2,1)S(1)}, bf16[512,128]{1,0:T(8,128)(2,1)S(1)}, u32[]{:S(2)}, u32[]{:S(2)}) %collective-permute-start.14) | collective-permute-done | bytes 131104 | tf_op jit(solution)/shard_map/ppermute | solution.py:1048
  104.4 25.3 %local_layer.2 = (bf16[512,128]{1,0:T(8,128)(2,1)}, bf16[512,128]{1,0:T(8,128)(2,1)}, bf16[512,128]{1,0:T(8,128)(2,1)}, bf16[512,128]{1,0:T(8,128)(2,1)}, bf16[4...) custom-call(s32[4,5]{1,0:T(4,128)} %get-tuple-element.405.refs_0_, ...), custom_call_target="tpu_custom_call" | custom-call | flops 28600000512 | bytes 24000000 | tf_op jit(solution)/shard_map/local_layer/pallas_call | solution.py:654
  134.8 25.3 %local_layer.3 = (bf16[512,128]{1,0:T(8,128)(2,1)}, bf16[512,128]{1,0:T(8,128)(2,1)}, bf16[512,128]{1,0:T(8,128)(2,1)}, bf16[512,128]{1,0:T(8,128)(2,1)}, bf16[4...) custom-call(s32[4,5]{1,0:T(4,128)} %get-tuple-element.404.refs_0_, ...), custom_call_target="tpu_custom_call" | custom-call | flops 28600000512 | bytes 24000000 | tf_op jit(solution)/shard_map/local_layer/pallas_call | solution.py:654
  160.9 11.1 %layer_grads.1 = (bf16[4,4,64,512]{3,2,1,0:T(8,128)(2,1)}, f32[4,4,64,512]{3,2,1,0:T(8,128)}, f32[4,4,16,512]{3,2,1,0:T(8,128)}, f32[4,4,16,512]{3,2,1,0:T(8,128...) custom-call(s32[1]{0:T(128)} %bitcast.7.refs_2_.me_ref, ...), custom_call_target="tpu_custom_call" | custom-call | flops 330000000 | bytes 100000 | tf_op jit(solution)/shard_map/layer_grads/pallas_call | solution.py:760
  175.2 3.5 collective-permute-done.28.refs_5_.refs_7_
  188.6 5.4 %split_add.6 = (bf16[2,4,64,512]{3,2,1,0:T(8,128)(2,1)}, f32[2,4,64,512]{3,2,1,0:T(8,128)S(1)}, f32[2,4,16,512]{3,2,1,0:T(8,128)}, f32[2,4,16,512]{3,2,1,0:T(8,1...) custom-call(f32[4,4,64,512]{3,2,1,0:T(8,128)S(1)} %copy-done, ...), custom_call_target="tpu_custom_call" | custom-call | flops 330000000 | bytes 100000 | tf_op jit(solution)/shard_map/split_add/pallas_call | solution.py:899
  198.2 12.6 %query_grads.1 = (bf16[8,128,128]{2,1,0:T(8,128)(2,1)S(1)}, bf16[8,128,128]{2,1,0:T(8,128)(2,1)}, bf16[8,128,128]{2,1,0:T(8,128)(2,1)S(1)}, bf16[8,128,128]{2,1,...) custom-call(f32[8192,128]{1,0:T(8,128)S(1)} %bitcast.170, bf16[128,256]{1,0:T(8,128)(2,1)S(1)} %copy-done.31, ...), custom_call_target="tpu_custom_call" | custom-call | flops 12099999744 | bytes 7000000 | tf_op jit(solution)/shard_map/query_grads/pallas_call | solution.py:254
  215.4 4.7 %collective-permute-done.33.refs_9_.refs_11_ = f32[2,4,48,512]{3,2,1,0:T(8,128)S(1)} collective-permute-done((f32[2,4,48,512]{3,2,1,0:T(8,128)}, f32[2,4,48,512]{3,2,1,0:T(8,128)S(1)}, u32[]{:S(2)}, u32[]{:S(2)}) %collective-permute-start.33) | collective-permute-done | bytes 786464 | tf_op jit(solution)/shard_map/ppermute | solution.py:872
  227.6 7.3 %mode_grads.1 = (f32[4,512,128]{2,1,0:T(8,128)}, f32[4,512,128]{2,1,0:T(8,128)S(1)}, f32[4,512,128]{2,1,0:T(8,128)S(1)}, f32[4,512,128]{2,1,0:T(8,128)S(1)}) custom-call(s32[1]{0:T(128)} %bitcast.7.refs_2_.me_ref, bf16[64,32,256]{2,1,0:T(8,128)(2,1)S(1)} %copy-done.40, bf16[64,64,128]{2,1,0:T(8,128)(2,1)S(1)} %copy-done.38, ...), custom_call_target="tpu_custom_call" | custom-call | flops 9900000256 | bytes 8000000 | tf_op jit(solution)/shard_map/mode_grads/pallas_call | solution.py:317
  240.4 4.7 %query_weight_grads.1 = (bf16[4,4,64,128]{3,2,1,0:T(8,128)(2,1)}, f32[4,4,64,128]{3,2,1,0:T(8,128)}) custom-call(s32[1]{0:T(128)} %bitcast.7.refs_2_.me_ref, bf16[1024,512]{1,0:T(8,128)(2,1)} %refs_0_.1, bf16[4,1024,128]{2,1,0:T(8,128)(2,1)} %pad_maximum_fusion.2.refs_1_), custom_call_target="tpu_custom_call" | custom-call | flops 330000000 | bytes 100000 | tf_op jit(solution)/shard_map/query_weight_grads/pallas_call | solution.py:760
  249.6 3.1 collective-permute-start.38
  254.9 3.7 %collective-permute-done.49.refs_1_.refs_3_ = bf16[2,4,64,128]{3,2,1,0:T(8,128)(2,1)S(1)} collective-permute-done((bf16[2,4,64,128]{3,2,1,0:T(8,128)(2,1)S(1)}, bf16[2,4,64,128]{3,2,1,0:T(8,128)(2,1)S(1)}, u32[]{:S(2)}, u32[]{:S(2)}) %collective-permute-start.49) | collective-permute-done | bytes 131104 | tf_op jit(solution)/shard_map/ppermute | solution.py:872
  263.1 3.0 collective-permute-start.44
  267.2 5.7 %collective-permute-done.56.refs_1_.refs_3_ = f32[2,4,128,128]{3,2,1,0:T(8,128)S(1)} collective-permute-done((f32[2,4,128,128]{3,2,1,0:T(8,128)S(1)}, f32[2,4,128,128]{3,2,1,0:T(8,128)S(1)}, u32[]{:S(2)}, u32[]{:S(2)}) %collective-permute-start.56) | collective-permute-done | bytes 524320 | tf_op jit(solution)/shard_map/ppermute | solution.py:872
  285.7 3.0 collective-permute-start.55
  295.5 5.1 %collective-permute-done.60 = f32[2,128,512]{2,1,0:T(8,128)S(1)} collective-permute-done((f32[2,128,512]{2,1,0:T(8,128)S(1)}, f32[2,128,512]{2,1,0:T(8,128)S(1)}, u32[]{:S(2)}, u32[]{:S(2)}) %collective-permute-start.60) | collective-permute-done | bytes 524320 | tf_op jit(solution)/shard_map/ppermute | solution.py:872
  315.1 4.0 %collective-permute-done.67 = f32[96,512]{1,0:T(8,128)S(1)} collective-permute-done((f32[96,512]{1,0:T(8,128)S(1)}, f32[96,512]{1,0:T(8,128)S(1)}, u32[]{:S(2)}, u32[]{:S(2)}) %collective-permute-start.67) | collective-permute-done | bytes 196640 | tf_op jit(solution)/shard_map/ppermute | solution.py:872
  322.3 8.7 %collective-permute-done.68 = f32[9,128]{1,0:T(8,128)S(1)} collective-permute-done((f32[9,128]{1,0:T(8,128)S(1)}, f32[9,128]{1,0:T(8,128)S(1)}, u32[]{:S(2)}, u32[]{:S(2)}) %collective-permute-start.68) | collective-permute-done | bytes 4640 | tf_op jit(solution)/shard_map/ppermute | solution.py:872
  331.8 2.7 collective-permute-done.69
  334.8 3.1 collective-permute-start.74
  346.4 19.7 %adam.1 = (f32[512,128]{1,0:T(8,128)}, f32[512,128]{1,0:T(8,128)}, f32[512,128]{1,0:T(8,128)}, f32[128,512]{1,0:T(8,128)}, f32[128,512]{1,0:T(8,128)}, /*index=5...) custom-call(s32[1]{0:T(128)} %bitcast.7.refs_2_.me_ref, ...), custom_call_target="tpu_custom_call" | custom-call | flops 16499999744 | bytes 48000000 | tf_op jit(solution)/shard_map/adam/pallas_call | solution.py:854
  (371 shorter events, 121.7 us)
Async XLA Ops:
  1.7 18.8 %collective-permute-start.2 = (bf16[512,128]{1,0:T(8,128)(2,1)S(1)}, bf16[512,128]{1,0:T(8,128)(2,1)S(1)}, u32[]{:S(2)}, u32[]{:S(2)}) collective-permute-start(bf16[512,128]{1,0:T(8,128)(2,1)S(1)} %convert_element_type.111.refs_0_), channel_id=1, source_target_pairs={{0,3},{1,0},{2,1},{3,2},{4,7},{5,4},{6,5},{7,6},{8,11},{9,8},{10,9... | collective-permute-start | bytes 393224 | tf_op jit(solution)/shard_map/ppermute | solution.py:1048
  22.2 21.7 %collective-permute-start.3 = (bf16[1024,128]{1,0:T(8,128)(2,1)S(1)}, bf16[1024,128]{1,0:T(8,128)(2,1)S(1)}, u32[]{:S(2)}, u32[]{:S(2)}) collective-permute-start(bf16[1024,128]{1,0:T(8,128)(2,1)S(1)} %get-tuple-element.203), channel_id=1, source_target_pairs={{0,1},{1,2},{2,3},{3,0},{4,5},{5,6},{6,7},{7,4},{8,9},{9,10},{10,1... | collective-permute-start | bytes 786440 | tf_op jit(solution)/shard_map/ppermute | solution.py:1048
  26.4 17.5 %collective-permute-start.5 = (bf16[144,512]{1,0:T(8,128)(2,1)S(1)}, bf16[144,512]{1,0:T(8,128)(2,1)S(1)}, u32[]{:S(2)}, u32[]{:S(2)}) collective-permute-start(bf16[144,512]{1,0:T(8,128)(2,1)S(1)} %fusion.4), channel_id=1, source_target_pairs={{0,2},{1,3},{2,0},{3,1},{4,6},{5,7},{6,4},{7,5},{8,10},{9,11},{10,... | collective-permute-start | bytes 442376 | tf_op jit(solution)/shard_map/ppermute | solution.py:1048
  26.6 17.3 %collective-permute-start.4 = (bf16[144,512]{1,0:T(8,128)(2,1)S(1)}, bf16[144,512]{1,0:T(8,128)(2,1)S(1)}, u32[]{:S(2)}, u32[]{:S(2)}) collective-permute-start(bf16[144,512]{1,0:T(8,128)(2,1)S(1)} %fusion.4), channel_id=1, source_target_pairs={{0,1},{1,2},{2,3},{3,0},{4,5},{5,6},{6,7},{7,4},{8,9},{9,10},{10,1... | collective-permute-start | bytes 442376 | tf_op jit(solution)/shard_map/ppermute | solution.py:1048
  44.0 17.1 %collective-permute-start.9 = (bf16[2,144,512]{2,1,0:T(8,128)(2,1)S(1)}, bf16[2,144,512]{2,1,0:T(8,128)(2,1)S(1)}, u32[]{:S(2)}, u32[]{:S(2)}) collective-permute-start(bf16[2,144,512]{2,1,0:T(8,128)(2,1)S(1)} %get-tuple-element.382), channel_id=1, source_target_pairs={{0,8},{4,12},{8,0},{12,4},{16,24},{20,28},{24,16},{28,20},{1,9},{5... | collective-permute-start | bytes 884744 | tf_op jit(solution)/shard_map/ppermute | solution.py:872
  61.2 18.3 %collective-permute-start.11 = (bf16[2,2,144,512]{3,2,1,0:T(8,128)(2,1)S(1)}, bf16[2,2,144,512]{3,2,1,0:T(8,128)(2,1)S(1)}, u32[]{:S(2)}, u32[]{:S(2)}) collective-permute-start(bf16[2,2,144,512]{3,2,1,0:T(8,128)(2,1)S(1)} %get-tuple-element.374), channel_id=1, source_target_pairs={{0,16},{4,20},{8,24},{12,28},{16,0},{20,4},{24,8},{28,12},{1,17},{... | collective-permute-start | bytes 1769480 | tf_op jit(solution)/shard_map/ppermute | solution.py:872
  61.8 17.7 %collective-permute-start.12 = (bf16[2,2,144,512]{3,2,1,0:T(8,128)(2,1)S(1)}, bf16[2,2,144,512]{3,2,1,0:T(8,128)(2,1)S(1)}, u32[]{:S(2)}, u32[]{:S(2)}) collective-permute-start(bf16[2,2,144,512]{3,2,1,0:T(8,128)(2,1)S(1)} %get-tuple-element.372), channel_id=1, source_target_pairs={{0,8},{4,12},{8,0},{12,4},{16,24},{20,28},{24,16},{28,20},{1,9},{5... | collective-permute-start | bytes 1769480 | tf_op jit(solution)/shard_map/ppermute | solution.py:872
  80.6 23.8 %collective-permute-start.17 = (bf16[4,2,144,512]{3,2,1,0:T(8,128)(2,1)S(1)}, bf16[4,2,144,512]{3,2,1,0:T(8,128)(2,1)}, u32[]{:S(2)}, u32[]{:S(2)}) collective-permute-start(bf16[4,2,144,512]{3,2,1,0:T(8,128)(2,1)S(1)} %bitcast.206), channel_id=1, source_target_pairs={{0,4},{4,0},{8,12},{12,8},{16,20},{20,16},{24,28},{28,24},{1,5},{5... | collective-permute-start | bytes 3538952 | tf_op jit(solution)/shard_map/ppermute | solution.py:872
  81.8 22.6 %collective-permute-start.16 = (bf16[4,2,144,512]{3,2,1,0:T(8,128)(2,1)}, bf16[4,2,144,512]{3,2,1,0:T(8,128)(2,1)}, u32[]{:S(2)}, u32[]{:S(2)}) collective-permute-start(bf16[4,2,144,512]{3,2,1,0:T(8,128)(2,1)} %bitcast.29.refs_11_), channel_id=1, source_target_pairs={{0,4},{4,0},{8,12},{12,8},{16,20},{20,16},{24,28},{28,24},{1,5},{5... | collective-permute-start | bytes 3538952 | tf_op jit(solution)/shard_map/ppermute | solution.py:872
  100.4 31.7 %collective-permute-start.21 = (bf16[512,128]{1,0:T(8,128)(2,1)S(1)}, bf16[512,128]{1,0:T(8,128)(2,1)S(1)}, u32[]{:S(2)}, u32[]{:S(2)}) collective-permute-start(bf16[512,128]{1,0:T(8,128)(2,1)S(1)} %bitcast.187), channel_id=1, source_target_pairs={{0,3},{1,0},{2,1},{3,2},{4,7},{5,4},{6,5},{7,6},{8,11},{9,8},{10,9... | collective-permute-start | bytes 393224 | tf_op jit(solution)/shard_map/ppermute | solution.py:1048
  101.1 33.0 %collective-permute-start.22 = (bf16[512,128]{1,0:T(8,128)(2,1)S(1)}, bf16[512,128]{1,0:T(8,128)(2,1)S(1)}, u32[]{:S(2)}, u32[]{:S(2)}) collective-permute-start(bf16[512,128]{1,0:T(8,128)(2,1)S(1)} %bitcast.186), channel_id=1, source_target_pairs={{0,2},{1,3},{2,0},{3,1},{4,6},{5,7},{6,4},{7,5},{8,10},{9,11},{10,... | collective-permute-start | bytes 393224 | tf_op jit(solution)/shard_map/ppermute | solution.py:1048
  102.1 32.0 %collective-permute-start.23 = (bf16[512,128]{1,0:T(8,128)(2,1)S(1)}, bf16[512,128]{1,0:T(8,128)(2,1)S(1)}, u32[]{:S(2)}, u32[]{:S(2)}) collective-permute-start(bf16[512,128]{1,0:T(8,128)(2,1)S(1)} %bitcast.185), channel_id=1, source_target_pairs={{0,1},{1,2},{2,3},{3,0},{4,5},{5,6},{6,7},{7,4},{8,9},{9,10},{10,1... | collective-permute-start | bytes 393224 | tf_op jit(solution)/shard_map/ppermute | solution.py:1048
  129.7 30.4 %collective-permute-start.18 = (bf16[512,128]{1,0:T(8,128)(2,1)}, bf16[512,128]{1,0:T(8,128)(2,1)S(1)}, u32[]{:S(2)}, u32[]{:S(2)}) collective-permute-start(bf16[512,128]{1,0:T(8,128)(2,1)} %get-tuple-element.240), channel_id=1, source_target_pairs={{0,1},{1,2},{2,3},{3,0},{4,5},{5,6},{6,7},{7,4},{8,9},{9,10},{10,1... | collective-permute-start | bytes 393224 | tf_op jit(solution)/shard_map/ppermute | solution.py:1048
  130.2 29.9 %collective-permute-start.19 = (bf16[512,128]{1,0:T(8,128)(2,1)}, bf16[512,128]{1,0:T(8,128)(2,1)S(1)}, u32[]{:S(2)}, u32[]{:S(2)}) collective-permute-start(bf16[512,128]{1,0:T(8,128)(2,1)} %get-tuple-element.241), channel_id=1, source_target_pairs={{0,2},{1,3},{2,0},{3,1},{4,6},{5,7},{6,4},{7,5},{8,10},{9,11},{10,... | collective-permute-start | bytes 393224 | tf_op jit(solution)/shard_map/ppermute | solution.py:1048
  132.1 28.0 %collective-permute-start.20 = (bf16[512,128]{1,0:T(8,128)(2,1)}, bf16[512,128]{1,0:T(8,128)(2,1)S(1)}, u32[]{:S(2)}, u32[]{:S(2)}) collective-permute-start(bf16[512,128]{1,0:T(8,128)(2,1)} %get-tuple-element.242), channel_id=1, source_target_pairs={{0,3},{1,0},{2,1},{3,2},{4,7},{5,4},{6,5},{7,6},{8,11},{9,8},{10,9... | collective-permute-start | bytes 393224 | tf_op jit(solution)/shard_map/ppermute | solution.py:1048
  173.7 23.4 %collective-permute-start.24 = (bf16[512,128]{1,0:T(8,128)(2,1)}, bf16[512,128]{1,0:T(8,128)(2,1)S(1)}, u32[]{:S(2)}, u32[]{:S(2)}) collective-permute-start(bf16[512,128]{1,0:T(8,128)(2,1)} %get-tuple-element.248), channel_id=1, source_target_pairs={{0,1},{1,2},{2,3},{3,0},{4,5},{5,6},{6,7},{7,4},{8,9},{9,10},{10,1... | collective-permute-start | bytes 393224 | tf_op jit(solution)/shard_map/ppermute | solution.py:1048
  179.5 18.2 %collective-permute-start.25 = (bf16[512,128]{1,0:T(8,128)(2,1)}, bf16[512,128]{1,0:T(8,128)(2,1)S(1)}, u32[]{:S(2)}, u32[]{:S(2)}) collective-permute-start(bf16[512,128]{1,0:T(8,128)(2,1)} %get-tuple-element.249), channel_id=1, source_target_pairs={{0,2},{1,3},{2,0},{3,1},{4,6},{5,7},{6,4},{7,5},{8,10},{9,11},{10,... | collective-permute-start | bytes 393224 | tf_op jit(solution)/shard_map/ppermute | solution.py:1048
  181.2 17.0 %collective-permute-start.26 = (bf16[512,128]{1,0:T(8,128)(2,1)}, bf16[512,128]{1,0:T(8,128)(2,1)S(1)}, u32[]{:S(2)}, u32[]{:S(2)}) collective-permute-start(bf16[512,128]{1,0:T(8,128)(2,1)} %get-tuple-element.250), channel_id=1, source_target_pairs={{0,3},{1,0},{2,1},{3,2},{4,7},{5,4},{6,5},{7,6},{8,11},{9,8},{10,9... | collective-permute-start | bytes 393224 | tf_op jit(solution)/shard_map/ppermute | solution.py:1048
  194.0 20.5 %collective-permute-start.32 = (f32[2,4,16,512]{3,2,1,0:T(8,128)}, f32[2,4,16,512]{3,2,1,0:T(8,128)S(1)}, u32[]{:S(2)}, u32[]{:S(2)}) collective-permute-start(f32[2,4,16,512]{3,2,1,0:T(8,128)} %get-tuple-element.279), channel_id=1, source_target_pairs={{0,8},{4,12},{8,0},{12,4},{16,24},{20,28},{24,16},{28,20},{1,9},{5... | collective-permute-start | bytes 786440 | tf_op jit(solution)/shard_map/ppermute | solution.py:872
  195.6 19.8 %collective-permute-start.34 = (f32[2,4,16,512]{3,2,1,0:T(8,128)}, f32[2,4,16,512]{3,2,1,0:T(8,128)S(1)}, u32[]{:S(2)}, u32[]{:S(2)}) collective-permute-start(f32[2,4,16,512]{3,2,1,0:T(8,128)} %get-tuple-element.281), channel_id=1, source_target_pairs={{0,16},{4,20},{8,24},{12,28},{16,0},{20,4},{24,8},{28,12},{1,17},{... | collective-permute-start | bytes 786440 | tf_op jit(solution)/shard_map/ppermute | solution.py:872
  197.1 18.3 %collective-permute-start.31 = (bf16[2,4,64,512]{3,2,1,0:T(8,128)(2,1)}, bf16[2,4,64,512]{3,2,1,0:T(8,128)(2,1)S(1)}, u32[]{:S(2)}, u32[]{:S(2)}) collective-permute-start(bf16[2,4,64,512]{3,2,1,0:T(8,128)(2,1)} %get-tuple-element.278), channel_id=1, source_target_pairs={{0,8},{4,12},{8,0},{12,4},{16,24},{20,28},{24,16},{28,20},{1,9},{5... | collective-permute-start | bytes 1572872 | tf_op jit(solution)/shard_map/ppermute | solution.py:872
  197.6 22.5 %collective-permute-start.33 = (f32[2,4,48,512]{3,2,1,0:T(8,128)}, f32[2,4,48,512]{3,2,1,0:T(8,128)S(1)}, u32[]{:S(2)}, u32[]{:S(2)}) collective-permute-start(f32[2,4,48,512]{3,2,1,0:T(8,128)} %get-tuple-element.280), channel_id=1, source_target_pairs={{0,16},{4,20},{8,24},{12,28},{16,0},{20,4},{24,8},{28,12},{1,17},{... | collective-permute-start | bytes 2359304 | tf_op jit(solution)/shard_map/ppermute | solution.py:872
  212.5 23.4 %collective-permute-start.45 = (bf16[1024,128]{1,0:T(8,128)(2,1)}, bf16[1024,128]{1,0:T(8,128)(2,1)}, u32[]{:S(2)}, u32[]{:S(2)}) collective-permute-start(bf16[1024,128]{1,0:T(8,128)(2,1)} %bitcast.59), channel_id=1, source_target_pairs={{0,3},{1,0},{2,1},{3,2},{4,7},{5,4},{6,5},{7,6},{8,11},{9,8},{10,9... | collective-permute-start | bytes 786440 | tf_op jit(solution)/shard_map/ppermute | solution.py:1048
  214.6 22.3 %collective-permute-start.46 = (bf16[1024,128]{1,0:T(8,128)(2,1)S(1)}, bf16[1024,128]{1,0:T(8,128)(2,1)S(1)}, u32[]{:S(2)}, u32[]{:S(2)}) collective-permute-start(bf16[1024,128]{1,0:T(8,128)(2,1)S(1)} %bitcast.182), channel_id=1, source_target_pairs={{0,2},{1,3},{2,0},{3,1},{4,6},{5,7},{6,4},{7,5},{8,10},{9,11},{10,... | collective-permute-start | bytes 786440 | tf_op jit(solution)/shard_map/ppermute | solution.py:1048
  215.4 22.9 %collective-permute-start.47 = (bf16[1024,128]{1,0:T(8,128)(2,1)S(1)}, bf16[1024,128]{1,0:T(8,128)(2,1)S(1)}, u32[]{:S(2)}, u32[]{:S(2)}) collective-permute-start(bf16[1024,128]{1,0:T(8,128)(2,1)S(1)} %bitcast.181), channel_id=1, source_target_pairs={{0,1},{1,2},{2,3},{3,0},{4,5},{5,6},{6,7},{7,4},{8,9},{9,10},{10,1... | collective-permute-start | bytes 786440 | tf_op jit(solution)/shard_map/ppermute | solution.py:1048
  225.4 19.6 %collective-permute-start.39 = (f32[1,4,16,512]{3,2,1,0:T(8,128)}, f32[1,4,16,512]{3,2,1,0:T(8,128)}, u32[]{:S(2)}, u32[]{:S(2)}) collective-permute-start(f32[1,4,16,512]{3,2,1,0:T(8,128)} %get-tuple-element.285), channel_id=1, source_target_pairs={{0,16},{4,20},{8,24},{12,28},{16,0},{20,4},{24,8},{28,12},{1,17},{... | collective-permute-start | bytes 393224 | tf_op jit(solution)/shard_map/ppermute | solution.py:872
  227.0 19.6 %collective-permute-start.41 = (f32[1,4,16,512]{3,2,1,0:T(8,128)}, f32[1,4,16,512]{3,2,1,0:T(8,128)}, u32[]{:S(2)}, u32[]{:S(2)}) collective-permute-start(f32[1,4,16,512]{3,2,1,0:T(8,128)} %get-tuple-element.289), channel_id=1, source_target_pairs={{0,8},{4,12},{8,0},{12,4},{16,24},{20,28},{24,16},{28,20},{1,9},{5... | collective-permute-start | bytes 393224 | tf_op jit(solution)/shard_map/ppermute | solution.py:872
  236.8 16.4 %collective-permute-start.40 = (f32[1,4,48,512]{3,2,1,0:T(8,128)}, f32[1,4,48,512]{3,2,1,0:T(8,128)}, u32[]{:S(2)}, u32[]{:S(2)}) collective-permute-start(f32[1,4,48,512]{3,2,1,0:T(8,128)} %get-tuple-element.287), channel_id=1, source_target_pairs={{0,8},{4,12},{8,0},{12,4},{16,24},{20,28},{24,16},{28,20},{1,9},{5... | collective-permute-start | bytes 1179656 | tf_op jit(solution)/shard_map/ppermute | solution.py:872
  238.3 20.3 %collective-permute-start.50 = (f32[4,4,128,128]{3,2,1,0:T(8,128)}, f32[4,4,128,128]{3,2,1,0:T(8,128)S(1)}, u32[]{:S(2)}, u32[]{:S(2)}) collective-permute-start(f32[4,4,128,128]{3,2,1,0:T(8,128)} %bitcast.62), channel_id=1, source_target_pairs={{0,4},{4,0},{8,12},{12,8},{16,20},{20,16},{24,28},{28,24},{1,5},{5... | collective-permute-start | bytes 3145736 | tf_op jit(solution)/shard_map/ppermute | solution.py:872
  319.1 15.7 %collective-permute-start.73 = (f32[4,128,512]{2,1,0:T(8,128)S(1)}, f32[4,128,512]{2,1,0:T(8,128)S(1)}, u32[]{:S(2)}, u32[]{:S(2)}) collective-permute-start(f32[4,128,512]{2,1,0:T(8,128)S(1)} %bitcast.214), channel_id=1, source_target_pairs={{0,4},{4,0},{8,12},{12,8},{16,20},{20,16},{24,28},{28,24},{1,5},{5... | collective-permute-start | bytes 3145736 | tf_op jit(solution)/shard_map/ppermute | solution.py:872
  319.1 15.6 %collective-permute-start.72 = (f32[4,128,512]{2,1,0:T(8,128)S(1)}, f32[4,128,512]{2,1,0:T(8,128)S(1)}, u32[]{:S(2)}, u32[]{:S(2)}) collective-permute-start(f32[4,128,512]{2,1,0:T(8,128)S(1)} %bitcast.212), channel_id=1, source_target_pairs={{0,4},{4,0},{8,12},{12,8},{16,20},{20,16},{24,28},{28,24},{1,5},{5... | collective-permute-start | bytes 3145736 | tf_op jit(solution)/shard_map/ppermute | solution.py:872
  319.6 15.0 %collective-permute-start.71 = (f32[2,96,512]{2,1,0:T(8,128)S(1)}, f32[2,96,512]{2,1,0:T(8,128)S(1)}, u32[]{:S(2)}, u32[]{:S(2)}) collective-permute-start(f32[2,96,512]{2,1,0:T(8,128)S(1)} %pad_maximum_fusion.12), channel_id=1, source_target_pairs={{0,16},{4,20},{8,24},{12,28},{16,0},{20,4},{24,8},{28,12},{1,17},{... | collective-permute-start | bytes 1179656 | tf_op jit(solution)/shard_map/ppermute | solution.py:872
  (117 other events, 943.7 us)

commit v5 on v4

--- a/solution.py
+++ b/solution.py
@@ -123,7 +123,7 @@
                 )
             return 0
 
-        lax.fori_loop(0, run // pair, forward, 0)
+        lax.fori_loop(0, run // pair, forward, 0, unroll=True)
 
     def mix(m, _):
         xr = x_scr[pl.ds(m, contexts, stride=SEQ_LEN), :].astype(BF)
@@ -136,7 +136,7 @@
         y_scr[pl.ds(MODES + m, contexts, stride=SEQ_LEN), :] = y[:, LANES:]
         return 0
 
-    lax.fori_loop(0, MODES, mix, 0, unroll=4)
+    lax.fori_loop(0, MODES, mix, 0, unroll=16)
 
     for r in range(owners):
         for number in range(2):
@@ -155,7 +155,7 @@
                     target[p * pair + k] = res[:, k * LANES : (k + 1) * LANES]
                 return 0
 
-            lax.fori_loop(0, half // pair, inverse, 0)
+            lax.fori_loop(0, half // pair, inverse, 0, unroll=True)
 
 
 def spectrum_call(queries, wt, tf, ti):
@@ -203,7 +203,7 @@
                     ]
                 return 0
 
-            lax.fori_loop(0, half // pair, forward, 0)
+            lax.fori_loop(0, half // pair, forward, 0, unroll=True)
 
     def mix(m, _):
         yr = y_scr[pl.ds(m, contexts, stride=SEQ_LEN), :].astype(BF)
@@ -215,7 +215,7 @@
         x_scr[pl.ds(MODES + m, contexts, stride=SEQ_LEN), :] = dx[:, LANES:]
         return 0
 
-    lax.fori_loop(0, MODES, mix, 0, unroll=4)
+    lax.fori_loop(0, MODES, mix, 0, unroll=16)
     bias_ref[...] = jnp.zeros_like(bias_ref)
 
     for r in range(owners):
@@ -238,7 +238,7 @@
             bias_ref[...] += total
             return 0
 
-        lax.fori_loop(0, run // pair, inverse, 0)
+        lax.fori_loop(0, run // pair, inverse, 0, unroll=True)
 
 
 def query_grad_call(first, second, wt, tit, tft, waits):
@@ -293,7 +293,7 @@
             dw_scr[pl.ds(c * total + m, HEAD_DIM, stride=MODES), :] = part
         return 0
 
-    lax.fori_loop(0, MODES, mix, 0, unroll=4)
+    lax.fori_loop(0, MODES, mix, 0, unroll=16)
     copies = []
     for j in range(pieces):
         for c in range(2):
@@ -687,7 +687,7 @@
             pltpu.SemaphoreType.DMA((len(packed), count * shared)),
         ],
         compiler_params=pltpu.CompilerParams(vmem_limit_bytes=56 * MIB),
-        cost_estimate=cost(26, 24e6),
+        cost_estimate=cost(5, 4e6),
         name="local_layer",
     )(
         starts[number * ctx_half : (number + 1) * ctx_half],

time: 374 us -> 367 us (0.981)
  Pallas kernels: 133 us -> 119 us
  waiting for transfers between devices: 87.5 us -> 91.3 us
    pallas_call x1, Pallas kernels: 14.8 us -> 8.65 us  [spectrum_call(): pl.pallas_call(spectrum_kernel, out_shape=[out] * (2 * owners) + [jax.Sha...]
    pallas_call x1, Pallas kernels: 12.6 us -> 6.61 us  [query_grad_call(): pl.pallas_call(body, in_specs=[whole] * (3 + 2 * owners) + [pl.BlockSpec(...]
  transfers between devices with their start and end apart: 77 -> 77, of which waited for: 24 -> 26; matrix products, arithmetic and copies ran while one was open for 8% -> 8% of each run, Pallas kernels for 27% -> 24%
where the time goes in v5:
time: 367 us; the launch traced here: 360 us
  Pallas kernels  119 us (32%)
  waiting for transfers between devices  91.3 us (25%)
  starting transfers between devices  87.5 us (24%)
  local copies, waits for them, and re-layouts  29.3 us (8%)
  other arithmetic  23.4 us (6%)
  between operations  10.1 us (3%)
    pallas_call x2, Pallas kernels, local_call(): pl.pallas_call(partial(local_kernel, chunk=CHUNK, hidden_width=hidden, he...  50.6 us
    ppermute x44, waiting for transfers between devices, swap(): return lax.ppermute(value, axis, [(i, i ^ 1 << bit) for i in range(size)])  49.1 us
    ppermute x33, starting transfers between devices, shift(): return lax.ppermute(v, 'head', [(i, (i + r) % nhead) for i in range(nhead)])  47 us
    ppermute x33, waiting for transfers between devices, shift(): return lax.ppermute(v, 'head', [(i, (i + r) % nhead) for i in range(nhead)])  42.2 us
    ppermute x44, starting transfers between devices, swap(): return lax.ppermute(value, axis, [(i, i ^ 1 << bit) for i in range(size)])  40.5 us
    pallas_call x1, Pallas kernels, adam_call(): pl.pallas_call(partial(adam_kernel, views=views, leads=leads, grads=len(g...  19.7 us
    unnamed x141, local copies, waits for them, and re-layouts  18.9 us
    pallas_call x2, Pallas kernels, outer_call(): pl.pallas_call(partial(outer_kernel, halves=[len(p) for p in products], o...  15.8 us
  transfers between devices with their start and end apart: 77, of which 26 were waited for; matrix products, arithmetic and copies ran while one was open for 8% of the time, Pallas kernels for 24%

profile of v5, /device:TPU:0, one launch (start us, length us, event | category | flops | bytes accessed | tf_op | source)
XLA Modules:
  0.0 360.3 jit_solution(12887342770359121551)
XLA Ops:
  1.7 5.1 %collective-permute-start.2 = (bf16[512,128]{1,0:T(8,128)(2,1)S(1)}, bf16[512,128]{1,0:T(8,128)(2,1)S(1)}, u32[]{:S(2)}, u32[]{:S(2)}) collective-permute-start(bf16[512,128]{1,0:T(8,128)(2,1)S(1)} %convert_element_type.111.refs_0_), channel_id=1, source_target_pairs={{0,3},{1,0},{2,1},{3,2},{4,7},{5,4},{6,5},{7,6},{8,11},{9,8},{10,9... | collective-permute-start | bytes 393224 | tf_op jit(solution)/shard_map/ppermute | solution.py:1048
  14.1 5.7 %copy.86 = f32[2,128,4096]{1,2,0:T(8,128)} copy(f32[2,128,4096]{2,1,0:T(8,128)} %bitcast.199) | data formatting | bytes 8388608 | tf_op jit(solution)/shard_map/reshape | solution.py:1068
  22.2 2.5 collective-permute-start.3
  28.0 6.7 %collective-permute-done.6 = bf16[144,512]{1,0:T(8,128)(2,1)S(1)} collective-permute-done((bf16[144,512]{1,0:T(8,128)(2,1)S(1)}, bf16[144,512]{1,0:T(8,128)(2,1)S(1)}, u32[]{:S(2)}, u32[]{:S(2)}) %collective-permute-start.6) | collective-permute-done | bytes 147488 | tf_op jit(solution)/shard_map/ppermute | solution.py:1048
  34.7 9.2 %collective-permute-done.5 = bf16[144,512]{1,0:T(8,128)(2,1)S(1)} collective-permute-done((bf16[144,512]{1,0:T(8,128)(2,1)S(1)}, bf16[144,512]{1,0:T(8,128)(2,1)S(1)}, u32[]{:S(2)}, u32[]{:S(2)}) %collective-permute-start.5) | collective-permute-done | bytes 147488 | tf_op jit(solution)/shard_map/ppermute | solution.py:1048
  48.9 9.9 %collective-permute-done.7 = bf16[1024,128]{1,0:T(8,128)(2,1)S(1)} collective-permute-done((bf16[1024,128]{1,0:T(8,128)(2,1)S(1)}, bf16[1024,128]{1,0:T(8,128)(2,1)S(1)}, u32[]{:S(2)}, u32[]{:S(2)}) %collective-permute-start.7) | collective-permute-done | bytes 262176 | tf_op jit(solution)/shard_map/ppermute | solution.py:1048
  64.6 8.7 %spectrum.1 = (bf16[4,128,128]{2,1,0:T(8,128)(2,1)S(1)}, bf16[4,128,128]{2,1,0:T(8,128)(2,1)S(1)}, bf16[4,128,128]{2,1,0:T(8,128)(2,1)S(1)}, bf16[4,128,128]{2,1...) custom-call(f32[8192,128]{1,0:T(8,128)S(1)} %bitcast.169, ...), custom_call_target="tpu_custom_call" | custom-call | flops 16499999744 | bytes 7000000 | tf_op jit(solution)/shard_map/spectrum/pallas_call | solution.py:166
  78.1 3.8 %collective-permute-start.13 = (bf16[512,128]{1,0:T(8,128)(2,1)S(1)}, bf16[512,128]{1,0:T(8,128)(2,1)S(1)}, u32[]{:S(2)}, u32[]{:S(2)}) collective-permute-start(bf16[512,128]{1,0:T(8,128)(2,1)S(1)} %bitcast.193), channel_id=1, source_target_pairs={{0,3},{1,0},{2,1},{3,2},{4,7},{5,4},{6,5},{7,6},{8,11},{9,8},{10,9... | collective-permute-start | bytes 393224 | tf_op jit(solution)/shard_map/ppermute | solution.py:1048
  82.0 3.1 collective-permute-start.14
  87.5 9.6 %collective-permute-done.14.refs_9_ = bf16[512,128]{1,0:T(8,128)(2,1)S(1)} collective-permute-done((bf16[512,128]{1,0:T(8,128)(2,1)S(1)}, bf16[512,128]{1,0:T(8,128)(2,1)S(1)}, u32[]{:S(2)}, u32[]{:S(2)}) %collective-permute-start.14) | collective-permute-done | bytes 131104 | tf_op jit(solution)/shard_map/ppermute | solution.py:1048
  99.4 25.3 %local_layer.2 = (bf16[512,128]{1,0:T(8,128)(2,1)}, bf16[512,128]{1,0:T(8,128)(2,1)}, bf16[512,128]{1,0:T(8,128)(2,1)}, bf16[512,128]{1,0:T(8,128)(2,1)}, bf16[4...) custom-call(s32[4,5]{1,0:T(4,128)} %get-tuple-element.405.refs_0_, ...), custom_call_target="tpu_custom_call" | custom-call | flops 5500000256 | bytes 4000000 | tf_op jit(solution)/shard_map/local_layer/pallas_call | solution.py:654
  127.8 3.0 collective-permute-start.20
  131.5 25.3 %local_layer.3 = (bf16[512,128]{1,0:T(8,128)(2,1)}, bf16[512,128]{1,0:T(8,128)(2,1)}, bf16[512,128]{1,0:T(8,128)(2,1)}, bf16[512,128]{1,0:T(8,128)(2,1)}, bf16[4...) custom-call(s32[4,5]{1,0:T(4,128)} %get-tuple-element.404.refs_0_, ...), custom_call_target="tpu_custom_call" | custom-call | flops 5500000256 | bytes 4000000 | tf_op jit(solution)/shard_map/local_layer/pallas_call | solution.py:654
  157.6 11.1 %layer_grads.1 = (bf16[4,4,64,512]{3,2,1,0:T(8,128)(2,1)}, f32[4,4,64,512]{3,2,1,0:T(8,128)}, f32[4,4,16,512]{3,2,1,0:T(8,128)}, f32[4,4,16,512]{3,2,1,0:T(8,128...) custom-call(s32[1]{0:T(128)} %bitcast.7.refs_2_.me_ref, ...), custom_call_target="tpu_custom_call" | custom-call | flops 330000000 | bytes 100000 | tf_op jit(solution)/shard_map/layer_grads/pallas_call | solution.py:760
  171.6 3.7 %collective-permute-done.28.refs_5_.refs_7_ = f32[4,4,16,512]{3,2,1,0:T(8,128)S(1)} collective-permute-done((f32[4,4,16,512]{3,2,1,0:T(8,128)}, f32[4,4,16,512]{3,2,1,0:T(8,128)S(1)}, u32[]{:S(2)}, u32[]{:S(2)}) %collective-permute-start.28) | collective-permute-done | bytes 524320 | tf_op jit(solution)/shard_map/ppermute | solution.py:872
  184.2 5.4 %split_add.6 = (bf16[2,4,64,512]{3,2,1,0:T(8,128)(2,1)}, f32[2,4,64,512]{3,2,1,0:T(8,128)S(1)}, f32[2,4,16,512]{3,2,1,0:T(8,128)}, f32[2,4,16,512]{3,2,1,0:T(8,1...) custom-call(f32[4,4,64,512]{3,2,1,0:T(8,128)S(1)} %copy-done, ...), custom_call_target="tpu_custom_call" | custom-call | flops 330000000 | bytes 100000 | tf_op jit(solution)/shard_map/split_add/pallas_call | solution.py:899
  193.8 6.6 %query_grads.1 = (bf16[8,128,128]{2,1,0:T(8,128)(2,1)S(1)}, bf16[8,128,128]{2,1,0:T(8,128)(2,1)}, bf16[8,128,128]{2,1,0:T(8,128)(2,1)S(1)}, bf16[8,128,128]{2,1,...) custom-call(f32[8192,128]{1,0:T(8,128)S(1)} %bitcast.170, bf16[128,256]{1,0:T(8,128)(2,1)S(1)} %copy-done.31, ...), custom_call_target="tpu_custom_call" | custom-call | flops 12099999744 | bytes 7000000 | tf_op jit(solution)/shard_map/query_grads/pallas_call | solution.py:254
  202.1 2.8 collective-permute-start.45
  205.9 3.1 collective-permute-done.31.refs_1_.refs_3_
  208.9 5.9 %collective-permute-done.33.refs_9_.refs_11_ = f32[2,4,48,512]{3,2,1,0:T(8,128)S(1)} collective-permute-done((f32[2,4,48,512]{3,2,1,0:T(8,128)}, f32[2,4,48,512]{3,2,1,0:T(8,128)S(1)}, u32[]{:S(2)}, u32[]{:S(2)}) %collective-permute-start.33) | collective-permute-done | bytes 786464 | tf_op jit(solution)/shard_map/ppermute | solution.py:872
  223.2 5.5 %mode_grads.1 = (f32[4,512,128]{2,1,0:T(8,128)}, f32[4,512,128]{2,1,0:T(8,128)S(1)}, f32[4,512,128]{2,1,0:T(8,128)S(1)}, f32[4,512,128]{2,1,0:T(8,128)S(1)}) custom-call(s32[1]{0:T(128)} %bitcast.7.refs_2_.me_ref, bf16[64,32,256]{2,1,0:T(8,128)(2,1)S(1)} %copy-done.40, bf16[64,64,128]{2,1,0:T(8,128)(2,1)S(1)} %copy-done.38, ...), custom_call_target="tpu_custom_call" | custom-call | flops 9900000256 | bytes 8000000 | tf_op jit(solution)/shard_map/mode_grads/pallas_call | solution.py:317
  232.8 4.7 %query_weight_grads.1 = (bf16[4,4,64,128]{3,2,1,0:T(8,128)(2,1)}, f32[4,4,64,128]{3,2,1,0:T(8,128)}) custom-call(s32[1]{0:T(128)} %bitcast.7.refs_2_.me_ref, bf16[1024,512]{1,0:T(8,128)(2,1)} %refs_0_.1, bf16[4,1024,128]{2,1,0:T(8,128)(2,1)} %pad_maximum_fusion.2.refs_1_), custom_call_target="tpu_custom_call" | custom-call | flops 330000000 | bytes 100000 | tf_op jit(solution)/shard_map/query_weight_grads/pallas_call | solution.py:760
  242.4 2.7 collective-permute-start.38
  248.3 2.8 collective-permute-done.49.refs_1_.refs_3_
  260.6 4.7 %collective-permute-done.56.refs_1_.refs_3_ = f32[2,4,128,128]{3,2,1,0:T(8,128)S(1)} collective-permute-done((f32[2,4,128,128]{3,2,1,0:T(8,128)S(1)}, f32[2,4,128,128]{3,2,1,0:T(8,128)S(1)}, u32[]{:S(2)}, u32[]{:S(2)}) %collective-permute-start.56) | collective-permute-done | bytes 524320 | tf_op jit(solution)/shard_map/ppermute | solution.py:872
  269.9 2.6 collective-permute-done.43
  278.8 2.6 collective-permute-start.55
  288.9 5.0 %collective-permute-done.60 = f32[2,128,512]{2,1,0:T(8,128)S(1)} collective-permute-done((f32[2,128,512]{2,1,0:T(8,128)S(1)}, f32[2,128,512]{2,1,0:T(8,128)S(1)}, u32[]{:S(2)}, u32[]{:S(2)}) %collective-permute-start.60) | collective-permute-done | bytes 524320 | tf_op jit(solution)/shard_map/ppermute | solution.py:872
  308.5 3.1 collective-permute-done.67
  315.6 7.9 %collective-permute-done.68 = f32[9,128]{1,0:T(8,128)S(1)} collective-permute-done((f32[9,128]{1,0:T(8,128)S(1)}, f32[9,128]{1,0:T(8,128)S(1)}, u32[]{:S(2)}, u32[]{:S(2)}) %collective-permute-start.68) | collective-permute-done | bytes 4640 | tf_op jit(solution)/shard_map/ppermute | solution.py:872
  327.4 2.9 collective-permute-start.74
  339.0 19.7 %adam.1 = (f32[512,128]{1,0:T(8,128)}, f32[512,128]{1,0:T(8,128)}, f32[512,128]{1,0:T(8,128)}, f32[128,512]{1,0:T(8,128)}, f32[128,512]{1,0:T(8,128)}, /*index=5...) custom-call(s32[1]{0:T(128)} %bitcast.7.refs_2_.me_ref, ...), custom_call_target="tpu_custom_call" | custom-call | flops 16499999744 | bytes 48000000 | tf_op jit(solution)/shard_map/adam/pallas_call | solution.py:854
  (371 shorter events, 129.3 us)
Async XLA Ops:
  1.7 18.8 %collective-permute-start.2 = (bf16[512,128]{1,0:T(8,128)(2,1)S(1)}, bf16[512,128]{1,0:T(8,128)(2,1)S(1)}, u32[]{:S(2)}, u32[]{:S(2)}) collective-permute-start(bf16[512,128]{1,0:T(8,128)(2,1)S(1)} %convert_element_type.111.refs_0_), channel_id=1, source_target_pairs={{0,3},{1,0},{2,1},{3,2},{4,7},{5,4},{6,5},{7,6},{8,11},{9,8},{10,9... | collective-permute-start | bytes 393224 | tf_op jit(solution)/shard_map/ppermute | solution.py:1048
  22.2 21.7 %collective-permute-start.3 = (bf16[1024,128]{1,0:T(8,128)(2,1)S(1)}, bf16[1024,128]{1,0:T(8,128)(2,1)S(1)}, u32[]{:S(2)}, u32[]{:S(2)}) collective-permute-start(bf16[1024,128]{1,0:T(8,128)(2,1)S(1)} %get-tuple-element.203), channel_id=1, source_target_pairs={{0,1},{1,2},{2,3},{3,0},{4,5},{5,6},{6,7},{7,4},{8,9},{9,10},{10,1... | collective-permute-start | bytes 786440 | tf_op jit(solution)/shard_map/ppermute | solution.py:1048
  26.4 17.5 %collective-permute-start.5 = (bf16[144,512]{1,0:T(8,128)(2,1)S(1)}, bf16[144,512]{1,0:T(8,128)(2,1)S(1)}, u32[]{:S(2)}, u32[]{:S(2)}) collective-permute-start(bf16[144,512]{1,0:T(8,128)(2,1)S(1)} %fusion.4), channel_id=1, source_target_pairs={{0,2},{1,3},{2,0},{3,1},{4,6},{5,7},{6,4},{7,5},{8,10},{9,11},{10,... | collective-permute-start | bytes 442376 | tf_op jit(solution)/shard_map/ppermute | solution.py:1048
  26.6 17.3 %collective-permute-start.4 = (bf16[144,512]{1,0:T(8,128)(2,1)S(1)}, bf16[144,512]{1,0:T(8,128)(2,1)S(1)}, u32[]{:S(2)}, u32[]{:S(2)}) collective-permute-start(bf16[144,512]{1,0:T(8,128)(2,1)S(1)} %fusion.4), channel_id=1, source_target_pairs={{0,1},{1,2},{2,3},{3,0},{4,5},{5,6},{6,7},{7,4},{8,9},{9,10},{10,1... | collective-permute-start | bytes 442376 | tf_op jit(solution)/shard_map/ppermute | solution.py:1048
  44.0 17.1 %collective-permute-start.9 = (bf16[2,144,512]{2,1,0:T(8,128)(2,1)S(1)}, bf16[2,144,512]{2,1,0:T(8,128)(2,1)S(1)}, u32[]{:S(2)}, u32[]{:S(2)}) collective-permute-start(bf16[2,144,512]{2,1,0:T(8,128)(2,1)S(1)} %get-tuple-element.382), channel_id=1, source_target_pairs={{0,8},{4,12},{8,0},{12,4},{16,24},{20,28},{24,16},{28,20},{1,9},{5... | collective-permute-start | bytes 884744 | tf_op jit(solution)/shard_map/ppermute | solution.py:872
  75.4 24.0 %collective-permute-start.17 = (bf16[4,2,144,512]{3,2,1,0:T(8,128)(2,1)S(1)}, bf16[4,2,144,512]{3,2,1,0:T(8,128)(2,1)}, u32[]{:S(2)}, u32[]{:S(2)}) collective-permute-start(bf16[4,2,144,512]{3,2,1,0:T(8,128)(2,1)S(1)} %bitcast.206), channel_id=1, source_target_pairs={{0,4},{4,0},{8,12},{12,8},{16,20},{20,16},{24,28},{28,24},{1,5},{5... | collective-permute-start | bytes 3538952 | tf_op jit(solution)/shard_map/ppermute | solution.py:872
  76.7 22.6 %collective-permute-start.16 = (bf16[4,2,144,512]{3,2,1,0:T(8,128)(2,1)}, bf16[4,2,144,512]{3,2,1,0:T(8,128)(2,1)}, u32[]{:S(2)}, u32[]{:S(2)}) collective-permute-start(bf16[4,2,144,512]{3,2,1,0:T(8,128)(2,1)} %bitcast.29.refs_11_), channel_id=1, source_target_pairs={{0,4},{4,0},{8,12},{12,8},{16,20},{20,16},{24,28},{28,24},{1,5},{5... | collective-permute-start | bytes 3538952 | tf_op jit(solution)/shard_map/ppermute | solution.py:872
  82.0 15.1 %collective-permute-start.14 = (bf16[512,128]{1,0:T(8,128)(2,1)S(1)}, bf16[512,128]{1,0:T(8,128)(2,1)S(1)}, u32[]{:S(2)}, u32[]{:S(2)}) collective-permute-start(bf16[512,128]{1,0:T(8,128)(2,1)S(1)} %bitcast.192), channel_id=1, source_target_pairs={{0,2},{1,3},{2,0},{3,1},{4,6},{5,7},{6,4},{7,5},{8,10},{9,11},{10,... | collective-permute-start | bytes 393224 | tf_op jit(solution)/shard_map/ppermute | solution.py:1048
  97.1 30.7 %collective-permute-start.21 = (bf16[512,128]{1,0:T(8,128)(2,1)S(1)}, bf16[512,128]{1,0:T(8,128)(2,1)S(1)}, u32[]{:S(2)}, u32[]{:S(2)}) collective-permute-start(bf16[512,128]{1,0:T(8,128)(2,1)S(1)} %bitcast.187), channel_id=1, source_target_pairs={{0,3},{1,0},{2,1},{3,2},{4,7},{5,4},{6,5},{7,6},{8,11},{9,8},{10,9... | collective-permute-start | bytes 393224 | tf_op jit(solution)/shard_map/ppermute | solution.py:1048
  97.2 33.6 %collective-permute-start.22 = (bf16[512,128]{1,0:T(8,128)(2,1)S(1)}, bf16[512,128]{1,0:T(8,128)(2,1)S(1)}, u32[]{:S(2)}, u32[]{:S(2)}) collective-permute-start(bf16[512,128]{1,0:T(8,128)(2,1)S(1)} %bitcast.186), channel_id=1, source_target_pairs={{0,2},{1,3},{2,0},{3,1},{4,6},{5,7},{6,4},{7,5},{8,10},{9,11},{10,... | collective-permute-start | bytes 393224 | tf_op jit(solution)/shard_map/ppermute | solution.py:1048
  97.2 33.6 %collective-permute-start.23 = (bf16[512,128]{1,0:T(8,128)(2,1)S(1)}, bf16[512,128]{1,0:T(8,128)(2,1)S(1)}, u32[]{:S(2)}, u32[]{:S(2)}) collective-permute-start(bf16[512,128]{1,0:T(8,128)(2,1)S(1)} %bitcast.185), channel_id=1, source_target_pairs={{0,1},{1,2},{2,3},{3,0},{4,5},{5,6},{6,7},{7,4},{8,9},{9,10},{10,1... | collective-permute-start | bytes 393224 | tf_op jit(solution)/shard_map/ppermute | solution.py:1048
  124.7 32.1 %collective-permute-start.18 = (bf16[512,128]{1,0:T(8,128)(2,1)}, bf16[512,128]{1,0:T(8,128)(2,1)S(1)}, u32[]{:S(2)}, u32[]{:S(2)}) collective-permute-start(bf16[512,128]{1,0:T(8,128)(2,1)} %get-tuple-element.240), channel_id=1, source_target_pairs={{0,1},{1,2},{2,3},{3,0},{4,5},{5,6},{6,7},{7,4},{8,9},{9,10},{10,1... | collective-permute-start | bytes 393224 | tf_op jit(solution)/shard_map/ppermute | solution.py:1048
  126.3 30.6 %collective-permute-start.19 = (bf16[512,128]{1,0:T(8,128)(2,1)}, bf16[512,128]{1,0:T(8,128)(2,1)S(1)}, u32[]{:S(2)}, u32[]{:S(2)}) collective-permute-start(bf16[512,128]{1,0:T(8,128)(2,1)} %get-tuple-element.241), channel_id=1, source_target_pairs={{0,2},{1,3},{2,0},{3,1},{4,6},{5,7},{6,4},{7,5},{8,10},{9,11},{10,... | collective-permute-start | bytes 393224 | tf_op jit(solution)/shard_map/ppermute | solution.py:1048
  127.8 29.1 %collective-permute-start.20 = (bf16[512,128]{1,0:T(8,128)(2,1)}, bf16[512,128]{1,0:T(8,128)(2,1)S(1)}, u32[]{:S(2)}, u32[]{:S(2)}) collective-permute-start(bf16[512,128]{1,0:T(8,128)(2,1)} %get-tuple-element.242), channel_id=1, source_target_pairs={{0,3},{1,0},{2,1},{3,2},{4,7},{5,4},{6,5},{7,6},{8,11},{9,8},{10,9... | collective-permute-start | bytes 393224 | tf_op jit(solution)/shard_map/ppermute | solution.py:1048
  170.4 21.4 %collective-permute-start.24 = (bf16[512,128]{1,0:T(8,128)(2,1)}, bf16[512,128]{1,0:T(8,128)(2,1)S(1)}, u32[]{:S(2)}, u32[]{:S(2)}) collective-permute-start(bf16[512,128]{1,0:T(8,128)(2,1)} %get-tuple-element.248), channel_id=1, source_target_pairs={{0,1},{1,2},{2,3},{3,0},{4,5},{5,6},{6,7},{7,4},{8,9},{9,10},{10,1... | collective-permute-start | bytes 393224 | tf_op jit(solution)/shard_map/ppermute | solution.py:1048
  176.2 17.1 %collective-permute-start.25 = (bf16[512,128]{1,0:T(8,128)(2,1)}, bf16[512,128]{1,0:T(8,128)(2,1)S(1)}, u32[]{:S(2)}, u32[]{:S(2)}) collective-permute-start(bf16[512,128]{1,0:T(8,128)(2,1)} %get-tuple-element.249), channel_id=1, source_target_pairs={{0,2},{1,3},{2,0},{3,1},{4,6},{5,7},{6,4},{7,5},{8,10},{9,11},{10,... | collective-permute-start | bytes 393224 | tf_op jit(solution)/shard_map/ppermute | solution.py:1048
  176.2 17.6 %collective-permute-start.26 = (bf16[512,128]{1,0:T(8,128)(2,1)}, bf16[512,128]{1,0:T(8,128)(2,1)S(1)}, u32[]{:S(2)}, u32[]{:S(2)}) collective-permute-start(bf16[512,128]{1,0:T(8,128)(2,1)} %get-tuple-element.250), channel_id=1, source_target_pairs={{0,3},{1,0},{2,1},{3,2},{4,7},{5,4},{6,5},{7,6},{8,11},{9,8},{10,9... | collective-permute-start | bytes 393224 | tf_op jit(solution)/shard_map/ppermute | solution.py:1048
  189.6 15.6 %collective-permute-start.32 = (f32[2,4,16,512]{3,2,1,0:T(8,128)}, f32[2,4,16,512]{3,2,1,0:T(8,128)S(1)}, u32[]{:S(2)}, u32[]{:S(2)}) collective-permute-start(f32[2,4,16,512]{3,2,1,0:T(8,128)} %get-tuple-element.279), channel_id=1, source_target_pairs={{0,8},{4,12},{8,0},{12,4},{16,24},{20,28},{24,16},{28,20},{1,9},{5... | collective-permute-start | bytes 786440 | tf_op jit(solution)/shard_map/ppermute | solution.py:872
  190.3 15.0 %collective-permute-start.34 = (f32[2,4,16,512]{3,2,1,0:T(8,128)}, f32[2,4,16,512]{3,2,1,0:T(8,128)S(1)}, u32[]{:S(2)}, u32[]{:S(2)}) collective-permute-start(f32[2,4,16,512]{3,2,1,0:T(8,128)} %get-tuple-element.281), channel_id=1, source_target_pairs={{0,16},{4,20},{8,24},{12,28},{16,0},{20,4},{24,8},{28,12},{1,17},{... | collective-permute-start | bytes 786440 | tf_op jit(solution)/shard_map/ppermute | solution.py:872
  191.8 17.2 %collective-permute-start.31 = (bf16[2,4,64,512]{3,2,1,0:T(8,128)(2,1)}, bf16[2,4,64,512]{3,2,1,0:T(8,128)(2,1)S(1)}, u32[]{:S(2)}, u32[]{:S(2)}) collective-permute-start(bf16[2,4,64,512]{3,2,1,0:T(8,128)(2,1)} %get-tuple-element.278), channel_id=1, source_target_pairs={{0,8},{4,12},{8,0},{12,4},{16,24},{20,28},{24,16},{28,20},{1,9},{5... | collective-permute-start | bytes 1572872 | tf_op jit(solution)/shard_map/ppermute | solution.py:872
  193.3 21.6 %collective-permute-start.33 = (f32[2,4,48,512]{3,2,1,0:T(8,128)}, f32[2,4,48,512]{3,2,1,0:T(8,128)S(1)}, u32[]{:S(2)}, u32[]{:S(2)}) collective-permute-start(f32[2,4,48,512]{3,2,1,0:T(8,128)} %get-tuple-element.280), channel_id=1, source_target_pairs={{0,16},{4,20},{8,24},{12,28},{16,0},{20,4},{24,8},{28,12},{1,17},{... | collective-permute-start | bytes 2359304 | tf_op jit(solution)/shard_map/ppermute | solution.py:872
  202.1 27.5 %collective-permute-start.45 = (bf16[1024,128]{1,0:T(8,128)(2,1)}, bf16[1024,128]{1,0:T(8,128)(2,1)}, u32[]{:S(2)}, u32[]{:S(2)}) collective-permute-start(bf16[1024,128]{1,0:T(8,128)(2,1)} %bitcast.59), channel_id=1, source_target_pairs={{0,3},{1,0},{2,1},{3,2},{4,7},{5,4},{6,5},{7,6},{8,11},{9,8},{10,9... | collective-permute-start | bytes 786440 | tf_op jit(solution)/shard_map/ppermute | solution.py:1048
  205.2 24.9 %collective-permute-start.46 = (bf16[1024,128]{1,0:T(8,128)(2,1)S(1)}, bf16[1024,128]{1,0:T(8,128)(2,1)S(1)}, u32[]{:S(2)}, u32[]{:S(2)}) collective-permute-start(bf16[1024,128]{1,0:T(8,128)(2,1)S(1)} %bitcast.182), channel_id=1, source_target_pairs={{0,2},{1,3},{2,0},{3,1},{4,6},{5,7},{6,4},{7,5},{8,10},{9,11},{10,... | collective-permute-start | bytes 786440 | tf_op jit(solution)/shard_map/ppermute | solution.py:1048
  205.3 25.4 %collective-permute-start.47 = (bf16[1024,128]{1,0:T(8,128)(2,1)S(1)}, bf16[1024,128]{1,0:T(8,128)(2,1)S(1)}, u32[]{:S(2)}, u32[]{:S(2)}) collective-permute-start(bf16[1024,128]{1,0:T(8,128)(2,1)S(1)} %bitcast.181), channel_id=1, source_target_pairs={{0,1},{1,2},{2,3},{3,0},{4,5},{5,6},{6,7},{7,4},{8,9},{9,10},{10,1... | collective-permute-start | bytes 786440 | tf_op jit(solution)/shard_map/ppermute | solution.py:1048
  220.1 17.4 %collective-permute-start.39 = (f32[1,4,16,512]{3,2,1,0:T(8,128)}, f32[1,4,16,512]{3,2,1,0:T(8,128)}, u32[]{:S(2)}, u32[]{:S(2)}) collective-permute-start(f32[1,4,16,512]{3,2,1,0:T(8,128)} %get-tuple-element.285), channel_id=1, source_target_pairs={{0,16},{4,20},{8,24},{12,28},{16,0},{20,4},{24,8},{28,12},{1,17},{... | collective-permute-start | bytes 393224 | tf_op jit(solution)/shard_map/ppermute | solution.py:872
  221.7 17.3 %collective-permute-start.41 = (f32[1,4,16,512]{3,2,1,0:T(8,128)}, f32[1,4,16,512]{3,2,1,0:T(8,128)}, u32[]{:S(2)}, u32[]{:S(2)}) collective-permute-start(f32[1,4,16,512]{3,2,1,0:T(8,128)} %get-tuple-element.289), channel_id=1, source_target_pairs={{0,8},{4,12},{8,0},{12,4},{16,24},{20,28},{24,16},{28,20},{1,9},{5... | collective-permute-start | bytes 393224 | tf_op jit(solution)/shard_map/ppermute | solution.py:872
  230.2 15.5 %collective-permute-start.40 = (f32[1,4,48,512]{3,2,1,0:T(8,128)}, f32[1,4,48,512]{3,2,1,0:T(8,128)}, u32[]{:S(2)}, u32[]{:S(2)}) collective-permute-start(f32[1,4,48,512]{3,2,1,0:T(8,128)} %get-tuple-element.287), channel_id=1, source_target_pairs={{0,8},{4,12},{8,0},{12,4},{16,24},{20,28},{24,16},{28,20},{1,9},{5... | collective-permute-start | bytes 1179656 | tf_op jit(solution)/shard_map/ppermute | solution.py:872
  230.7 20.3 %collective-permute-start.50 = (f32[4,4,128,128]{3,2,1,0:T(8,128)}, f32[4,4,128,128]{3,2,1,0:T(8,128)S(1)}, u32[]{:S(2)}, u32[]{:S(2)}) collective-permute-start(f32[4,4,128,128]{3,2,1,0:T(8,128)} %bitcast.62), channel_id=1, source_target_pairs={{0,4},{4,0},{8,12},{12,8},{16,20},{20,16},{24,28},{28,24},{1,5},{5... | collective-permute-start | bytes 3145736 | tf_op jit(solution)/shard_map/ppermute | solution.py:872
  242.4 14.8 %collective-permute-start.38 = (bf16[64,512]{1,0:T(8,128)(2,1)S(1)}, bf16[64,512]{1,0:T(8,128)(2,1)S(1)}, u32[]{:S(2)}, u32[]{:S(2)}) collective-permute-start(bf16[64,512]{1,0:T(8,128)(2,1)S(1)} %get-tuple-element.384), channel_id=1, source_target_pairs={{0,3},{1,0},{2,1},{3,2},{4,7},{5,4},{6,5},{7,6},{8,11},{9,8},{10,9... | collective-permute-start | bytes 196616 | tf_op jit(solution)/shard_map/ppermute | solution.py:1048
  311.6 15.7 %collective-permute-start.73 = (f32[4,128,512]{2,1,0:T(8,128)S(1)}, f32[4,128,512]{2,1,0:T(8,128)S(1)}, u32[]{:S(2)}, u32[]{:S(2)}) collective-permute-start(f32[4,128,512]{2,1,0:T(8,128)S(1)} %bitcast.214), channel_id=1, source_target_pairs={{0,4},{4,0},{8,12},{12,8},{16,20},{20,16},{24,28},{28,24},{1,5},{5... | collective-permute-start | bytes 3145736 | tf_op jit(solution)/shard_map/ppermute | solution.py:872
  311.7 15.6 %collective-permute-start.72 = (f32[4,128,512]{2,1,0:T(8,128)S(1)}, f32[4,128,512]{2,1,0:T(8,128)S(1)}, u32[]{:S(2)}, u32[]{:S(2)}) collective-permute-start(f32[4,128,512]{2,1,0:T(8,128)S(1)} %bitcast.212), channel_id=1, source_target_pairs={{0,4},{4,0},{8,12},{12,8},{16,20},{20,16},{24,28},{28,24},{1,5},{5... | collective-permute-start | bytes 3145736 | tf_op jit(solution)/shard_map/ppermute | solution.py:872
  312.2 15.0 %collective-permute-start.71 = (f32[2,96,512]{2,1,0:T(8,128)S(1)}, f32[2,96,512]{2,1,0:T(8,128)S(1)}, u32[]{:S(2)}, u32[]{:S(2)}) collective-permute-start(f32[2,96,512]{2,1,0:T(8,128)S(1)} %pad_maximum_fusion.12), channel_id=1, source_target_pairs={{0,16},{4,20},{8,24},{12,28},{16,0},{20,4},{24,8},{28,12},{1,17},{... | collective-permute-start | bytes 1179656 | tf_op jit(solution)/shard_map/ppermute | solution.py:872
  (117 other events, 920.4 us)
